TPU v7x, 32 devices: a whole 2x2x4 slice. The times are simulated.
32 devices in a mesh: feat: 8 (over z, x), ex: 4 (over y, core).
Axes of the slice: x: 2, y: 2, z: 4, core: 2. Of those that a mesh axis runs over, the one named last changes fastest.
Arguments:
- grads: bfloat16 [256, 1048576], P('ex', 'feat'), may hold values from -6 to 6
- first_factor: bfloat16 [1024, 1024, 64], P('feat'), may hold values from -0.1875 to 0.1875
- second_factor: bfloat16 [64, 1024, 128], P('feat'), may hold values from -0.1875 to 0.1875
- picks: int32 [8, 8], replicated, may hold values from 0 to 255
Outputs:
- sketch: float32 [256, 8192], P('ex', 'feat')
- coverage: float32 [8, 256], P(None, 'ex')
All inputs are finite; a program needn't handle non-finite values.
Results may differ from a plain program's by a relative error of at most 0.003.
Values may be sent and summed in bfloat16 or wider, within the bound.
No kernel may reach another device: no remote copies, remote signals or barrier semaphores. Data moves between devices by JAX's collectives and lax.ppermute only.
A program may use at most 128 MiB of HBM per device.

v0:
```python
import jax
import jax.numpy as jnp
from jax import lax
from jax.sharding import PartitionSpec as P

SKETCH = 8192


def per_device(grads, first_factor, second_factor, picks):
    ex_rows = grads.shape[0]
    local_blocks = first_factor.shape[0]
    blocks = grads.reshape(ex_rows, local_blocks, first_factor.shape[1])
    inner = jnp.einsum(
        "ebi,bik->kbe", blocks, first_factor, preferred_element_type=jnp.float32
    ).astype(jnp.bfloat16)
    piece = lax.all_to_all(inner, "feat", split_axis=0, concat_axis=1, tiled=True)
    mapped = jnp.einsum("kbe,kbj->ekj", piece, second_factor, preferred_element_type=jnp.float32)
    sketch = mapped.reshape(piece.shape[2], second_factor.shape[0] * second_factor.shape[2])
    base = lax.axis_index("ex") * ex_rows
    row_ids = base + jnp.arange(ex_rows, dtype=jnp.int32)
    rows_out = []
    running = None
    for r in range(picks.shape[0]):
        onehot = (picks[r][:, None] == row_ids[None, :]).astype(jnp.float32)
        fetch_part = jnp.dot(
            onehot, sketch, precision=lax.Precision.HIGHEST, preferred_element_type=jnp.float32
        )
        diff = sketch[:, None, :] - lax.psum(fetch_part, "ex")[None, :, :]
        part = jnp.sum(diff * diff, axis=2)
        nearest = jnp.min(lax.psum(part, "feat") / SKETCH, axis=1)
        running = nearest if running is None else jnp.minimum(running, nearest)
        rows_out.append(running)
    coverage = jnp.stack(rows_out, axis=0)
    return (sketch, coverage)


def solution(mesh):
    in_specs = (P("ex", "feat"), P("feat", None, None), P("feat", None, None), P())
    out_specs = (P("ex", "feat"), P(None, "ex"))
    return jax.shard_map(
        per_device, mesh=mesh, in_specs=in_specs, out_specs=out_specs, check_vma=False
    )
```

profile of v0, /device:TPU:0, one launch (start us, length us, event | category | flops | bytes accessed | tf_op | source)
XLA Modules:
  0.0 149.0 jit_solution(17843747449955727261)
XLA Ops:
  7.2 0.0 copy-start
  7.2 14.4 %convert_bitcast_fusion = bf16[64,128,64]{2,0,1:T(8,128)(2,1)} fusion(bf16[128,1024,64]{1,2,0:T(8,128)(2,1)} %param.5, bf16[8,128,8,1024]{3,2,1,0:T(8,128)(2,1)} %bitcast.85), kind=kOutput, calls=%fused_computation.11 | convolution fusion | flops 1074266112 | bytes 34603008 | tf_op jit(solution)/shard_map/ebi,bik->kbe/dot_general | solution.py:13
  21.6 0.0 copy-start.2
  21.6 4.1 %copy.28 = bf16[64,128,64]{1,2,0:T(8,128)(2,1)} copy(bf16[64,128,64]{2,0,1:T(8,128)(2,1)} %convert_bitcast_fusion) | data formatting | bytes 2097152 | tf_op jit(solution)/shard_map/convert_element_type | solution.py:15
  25.7 7.3 %all-to-all-start = ((bf16[64,128,64]{1,2,0:T(8,128)(2,1)}), bf16[64,128,64]{1,2,0:T(8,128)(2,1)S(1)}, u32[]{:S(2)}, u32[]{:S(2)}) async-start(bf16[64,128,64]{1,2,0:T(8,128)(2,1)} %copy.28), calls=%async_computation | async-start | bytes 2097152 | tf_op jit(solution)/shard_map/all_to_all | solution.py:16
  32.9 0.0 all-reduce.4.cloned.1.call-start
  33.0 0.0 copy-done.2
  33.0 25.7 %all-to-all-done = bf16[64,128,64]{1,2,0:T(8,128)(2,1)S(1)} async-done(((bf16[64,128,64]{1,2,0:T(8,128)(2,1)}), bf16[64,128,64]{1,2,0:T(8,128)(2,1)S(1)}, u32[]{:S(2)}, u32[]{:S(2)}) %all-to-all-start) | async-done | bytes 1048608 | tf_op jit(solution)/shard_map/all_to_all | solution.py:16
  58.7 1.7 %copy.49 = bf16[8,8,128,64]{2,0,3,1:T(8,128)(2,1)} copy(bf16[8,8,128,64]{2,3,1,0:T(8,128)(2,1)S(1)} %bitcast.82) | data formatting | bytes 2097152 | tf_op jit(solution)/shard_map/all_to_all | solution.py:16
  60.4 1.5 %all_to_all.16 = bf16[8,1024,64]{1,2,0:T(8,128)(2,1)S(1)} reshape(bf16[8,8,128,64]{2,1,3,0:T(8,128)(2,1)} %bitcast.83) | data formatting | bytes 2097152 | tf_op jit(solution)/shard_map/all_to_all | solution.py:16
  61.9 0.0 copy-done
  62.0 0.5 convolution_bitcast_fusion
  62.5 0.0 copy-start.1
  62.5 0.8 fusion.11
  63.3 0.8 fusion.13
  64.2 0.8 fusion.15
  65.0 0.8 fusion.17
  65.8 0.8 fusion.19
  66.6 0.8 fusion.5
  67.5 0.8 fusion.7
  68.3 0.8 fusion.9
  69.1 0.0 all-reduce.4.cloned.1.call-update
  69.2 31.8 %all-reduce.4.cloned.1.call-done = (f32[8,1024]{1,0:T(8,128)}, f32[8,1024]{1,0:T(8,128)}, f32[8,1024]{1,0:T(8,128)}, f32[8,1024]{1,0:T(8,128)}, f32[8,1024]{1,0:...) async-done(((f32[8,1024]{1,0:T(8,128)}, f32[8,1024]{1,0:T(8,128)}, f32[8,1024]{1,0:T(8,128)}, f32[8,1024]{1,0:T(8,128)}, f32[8,1024]{1,0:T(8,128)}, ...) | async-done | bytes 262160 | tf_op jit(solution)/shard_map/psum | solution.py:28
  101.0 2.8 %multiply_reduce_fusion = (f32[64,8]{1,0:T(8,128)S(1)}, f32[64,8]{1,0:T(8,128)S(1)}, f32[64,8]{1,0:T(8,128)S(1)}, f32[64,8]{1,0:T(8,128)S(1)}, f32[64,8]{1,0:T(8...) fusion(f32[8,1024]{1,0:T(8,128)} %get-tuple-element.18, f32[64,1024]{1,0:T(8,128)S(1)} %bitcast.80, ...), kind=kLoop, calls=%fused_computation.3 | loop fusion | flops 12578816 | bytes 540672 | tf_op jit(solution)/shard_map/reduce_sum | solution.py:29
  103.8 0.1 copy.31
  103.9 0.1 copy.32
  104.0 0.1 copy.33
  104.0 0.1 copy.34
  104.1 0.1 copy.35
  104.1 0.1 copy.36
  104.2 0.1 copy.37
  104.3 0.1 copy.38
  104.3 37.1 %all-reduce = (f32[64,8]{0,1:T(8,128)S(1)}, f32[64,8]{0,1:T(8,128)S(1)}, f32[64,8]{0,1:T(8,128)S(1)}, f32[64,8]{0,1:T(8,128)S(1)}, f32[64,8]{0,1:T(8,128)S(1)}, ...) all-reduce(f32[64,8]{0,1:T(8,128)S(1)} %copy.31, ...), channel_id=1, replica_groups=mesh['feat'=8,'ex'=4] {'feat'}, use_global_device_ids=true, to_apply=%region_2.0 | all-reduce | flops 4096 | bytes 32768 | tf_op jit(solution)/shard_map/psum | solution.py:30
  141.6 0.6 stack.5
  142.2 0.0 copy-done.1
  (8 shorter events, 0.1 us)
Async XLA Ops:
  7.2 54.8 %copy-start = (bf16[8,1024,128]{2,1,0:T(8,128)(2,1)S(1)}, bf16[8,1024,128]{2,1,0:T(8,128)(2,1)}, u32[]{:S(2)}) copy-start(bf16[8,1024,128]{2,1,0:T(8,128)(2,1)} %param.6) | copy-start | bytes 6291460
  21.6 11.4 %copy-start.2 = (s32[8,8]{1,0:T(8,128)S(1)}, s32[8,8]{1,0:T(8,128)}, u32[]{:S(2)}) copy-start(s32[8,8]{1,0:T(8,128)} %param.7) | copy-start | bytes 772
  25.7 33.0 %all-to-all-start = ((bf16[64,128,64]{1,2,0:T(8,128)(2,1)}), bf16[64,128,64]{1,2,0:T(8,128)(2,1)S(1)}, u32[]{:S(2)}, u32[]{:S(2)}) async-start(bf16[64,128,64]{1,2,0:T(8,128)(2,1)} %copy.28), calls=%async_computation | async-start | bytes 2097152 | tf_op jit(solution)/shard_map/all_to_all | solution.py:16
  32.9 68.1 %all-reduce.4.cloned.1.call-start = ((), (), s32[]{:S(2)}) async-start(), calls=%async_computation.1 | async-start | bytes 524288 | tf_op jit(solution)/shard_map/psum | solution.py:28
  62.5 79.7 %copy-start.1 = (f32[8,8,8,128]{3,2,0,1:T(8,128)}, f32[8,8,8,128]{3,2,0,1:T(8,128)S(1)}, u32[]{:S(2)}) copy-start(f32[8,8,8,128]{3,2,0,1:T(8,128)S(1)} %copy.50) | copy-start | bytes 786436
Sparse Core Ops, SparseCore 0:
  69.3 31.6 all-reduce.3
where the time goes:
time: 149 us
  waiting for transfers between devices  57.5 us (39%)
  blocking collectives  37.1 us (25%)
  matrix products  21.6 us (14%)
  between operations  14.1 us (9%)
  local copies, waits for them, and re-layouts  8.42 us (6%)
  starting transfers between devices  7.29 us (5%)
  other arithmetic  2.93 us (2%)
    psum x1, blocking collectives, per_device(): nearest = jnp.min(lax.psum(part, 'feat') / SKETCH, axis=1)  37.1 us
    psum x1, waiting for transfers between devices, per_device(): diff = sketch[:, None, :] - lax.psum(fetch_part, 'ex')[None, :, :]  31.8 us
    all_to_all x1, waiting for transfers between devices, per_device(): lax.all_to_all(inner, 'feat', split_axis=0, concat_axis=1, tiled=True)  25.7 us
    dot_general x1, matrix products, per_device(): jnp.einsum('ebi,bik->kbe', blocks, first_factor, preferred_element_type=j...  14.4 us
    all_to_all x1, starting transfers between devices, per_device(): lax.all_to_all(inner, 'feat', split_axis=0, concat_axis=1, tiled=True)  7.25 us
    dot_general x8, matrix products, per_device(): jnp.dot(onehot, sketch, precision=lax.Precision.HIGHEST, preferred_elemen...  6.64 us
    convert_element_type x1, local copies, waits for them, and re-layouts, per_device(): inner = jnp.einsum('ebi,bik->kbe', blocks, first_factor, preferred_elemen...  4.05 us
    all_to_all x2, local copies, waits for them, and re-layouts, per_device(): lax.all_to_all(inner, 'feat', split_axis=0, concat_axis=1, tiled=True)  3.23 us
  transfers between devices with their start and end apart: 2, of which 2 were waited for; matrix products, arithmetic and copies ran while one was open for 0% of the time, Pallas kernels for 0%

commit v1 on v0

v1 whole, which is shorter than its diff:
```python
import functools

import jax
import jax.numpy as jnp
from jax import lax
from jax.experimental import pallas as pl
from jax.experimental.pallas import tpu as pltpu
from jax.sharding import PartitionSpec as P

F32 = jnp.float32
BF16 = jnp.bfloat16
VMEM_LIMIT = 48 * 1024 * 1024
NT = (((1,), (1,)), ((), ()))
NN = (((1,), (0,)), ((), ()))


def params(**kw):
    return pltpu.CompilerParams(vmem_limit_bytes=VMEM_LIMIT, **kw)


def first_kernel(step_blocks, half, flush, g0, g1, w0, w1, out, acc):
    s = pl.program_id(0)
    groups, size = w0.shape[1], w0.shape[2]
    for t in range(step_blocks):
        cols = slice(t * size, (t + 1) * size)
        low = lax.dot_general(w0[t], g0[:, cols], NT, preferred_element_type=F32)
        high = lax.dot_general(w1[t], g1[:, cols], NT, preferred_element_type=F32)
        row = s * step_blocks + t
        acc[pl.ds(row, groups, stride=half), :] = jnp.concatenate([low, high], axis=1)

    steps = flush // step_blocks

    @pl.when(s % steps == steps - 1)
    def _():
        start = pl.multiple_of((s // steps) * flush, flush)
        for k in range(groups):
            out[k, pl.ds(start, flush), :] = acc[pl.ds(k * half + start, flush), :].astype(BF16)


def first_products(grads, factor, start, count):
    rows = grads.shape[0]
    _, groups, size = factor.shape
    half = count // 2
    step_blocks = min(4, half)
    flush = min(16, half)
    low, high = start // step_blocks, (start + half) // step_blocks
    g_spec = lambda first: pl.BlockSpec((rows, step_blocks * size), lambda s, first=first: (0, first + s))
    w_spec = lambda first: pl.BlockSpec((step_blocks, groups, size), lambda s, first=first: (first + s, 0, 0))
    return pl.pallas_call(
        functools.partial(first_kernel, step_blocks, half, flush),
        grid=(half // step_blocks,),
        in_specs=[g_spec(low), g_spec(high), w_spec(low), w_spec(high)],
        out_specs=pl.BlockSpec((groups, half, 2 * rows), lambda s: (0, 0, 0)),
        out_shape=jax.ShapeDtypeStruct((groups, half, 2 * rows), BF16),
        scratch_shapes=[pltpu.VMEM((groups * half, 2 * rows), F32)],
        compiler_params=params(dimension_semantics=("arbitrary",)),
        cost_estimate=pl.CostEstimate(
            flops=2 * count * rows * groups * size,
            bytes_accessed=2 * count * size * (rows + groups),
            transcendentals=0,
        ),
        name="first_products",
    )(grads, grads, factor, factor)


def turn_kernel(halves, second, *outs):
    groups, sources, _, width = second.shape
    for k in range(groups):
        start = 0
        for half, out in zip(halves, outs):
            for h in range(2):
                rows = second[k, :, start + h * half : start + (h + 1) * half, :]
                rows = rows.reshape(sources * half, width)
                out[k, h * width : (h + 1) * width, :] = rows.T
            start += 2 * half


def turned(second, sources, halves):
    groups, total, width = second.shape
    second = second.reshape(groups, sources, total // sources, width)
    return pl.pallas_call(
        functools.partial(turn_kernel, halves),
        out_shape=[jax.ShapeDtypeStruct((groups, 2 * width, sources * half), BF16) for half in halves],
        compiler_params=params(),
        name="turned_factor",
    )(second)


def second_kernel(chunks, *refs):
    base, picks, *rest = refs
    turned_refs, pieces, (sketch, fetched, held) = rest[:chunks], rest[chunks : 2 * chunks], rest[2 * chunks :]
    groups, both, _ = turned_refs[0].shape
    width, rows = both // 2, sketch.shape[0]
    slots = fetched.shape[1]
    if groups < slots:
        held[...] = jnp.zeros_like(held)
    for k in range(groups):
        total = None
        for a, x in zip(turned_refs, pieces):
            right = x[:, k].reshape(a.shape[2], 2 * rows)
            part = lax.dot_general(a[k], right, NN, preferred_element_type=F32)
            total = part if total is None else total + part
        mapped = (total[:width, :rows] + total[width:, rows:]).T
        sketch[:, k * width : (k + 1) * width] = mapped
        held[pl.ds(k, rows, stride=slots), :] = mapped
    rounds, each = picks.shape
    for r in range(rounds):
        for p in range(each):
            at = picks[r, p] - base[0]
            mine = (at >= 0) & (at < rows)
            start = pl.multiple_of(jnp.clip(at, 0, rows - 1) * slots, slots)
            fetched[r * each + p] = jnp.where(mine, held[pl.ds(start, slots), :], 0.0)


def second_products(base, picks, turned_factors, pieces, rows):
    chunks = len(pieces)
    groups, both, _ = turned_factors[0].shape
    width = both // 2
    slots = -(-groups // 8) * 8
    smem = pl.BlockSpec(memory_space=pltpu.SMEM)
    vmem = pl.BlockSpec(memory_space=pltpu.VMEM)
    return pl.pallas_call(
        functools.partial(second_kernel, chunks),
        in_specs=[smem, smem] + [vmem] * (2 * chunks),
        out_specs=[vmem, vmem],
        out_shape=[
            jax.ShapeDtypeStruct((rows, groups * width), F32),
            jax.ShapeDtypeStruct((picks.size, slots, width), F32),
        ],
        scratch_shapes=[pltpu.VMEM((rows * slots, width), F32)],
        compiler_params=params(),
        name="second_products",
    )(base, picks, *turned_factors, *pieces)


def distance_kernel(sketch, *refs):
    *fetched, out, total = refs
    rows, dims = sketch.shape
    count, _, width = total.shape
    center = fetched[0][...]
    for other in fetched[1:]:
        center = center + other[...]
    total[...] = center
    lane = lax.broadcasted_iota(jnp.int32, (rows, 128), 1)

    def one(p, sums):
        acc = None
        for t in range(dims // width):
            diff = sketch[:, t * width : (t + 1) * width] - total[p, t : t + 1, :]
            acc = diff * diff if acc is None else acc + diff * diff
        return jnp.where(lane == p, jnp.sum(acc, axis=1, keepdims=True), sums)

    sums = lax.fori_loop(0, count, one, jnp.zeros((rows, 128), F32))
    half = count // 2
    by_pick = sums.T
    out[...] = jnp.concatenate([by_pick[:half], by_pick[half:count]], axis=1)


def distances(sketch, fetched):
    vmem = pl.BlockSpec(memory_space=pltpu.VMEM)
    count = fetched[0].shape[0]
    return pl.pallas_call(
        distance_kernel,
        in_specs=[vmem] * (1 + len(fetched)),
        out_specs=vmem,
        out_shape=jax.ShapeDtypeStruct((count // 2, 2 * sketch.shape[0]), F32),
        scratch_shapes=[pltpu.VMEM(fetched[0].shape, F32)],
        compiler_params=params(),
        name="distances",
    )(sketch, *fetched)


def nearest_kernel(sketch_size, each, parts, out):
    total = parts[0]
    for i in range(1, parts.shape[0]):
        total = total + parts[i]
    total = total / sketch_size
    half, rows = out.shape[0] // 2, out.shape[1]
    near = [jnp.min(total[r * each : (r + 1) * each, :], axis=0, keepdims=True) for r in range(half)]
    running = None
    for r in range(2 * half):
        row = near[r % half][:, (r // half) * rows : (r // half + 1) * rows]
        running = row if running is None else jnp.minimum(running, row)
        out[r : r + 1, :] = running


def nearest(parts, sketch_size, rounds):
    vmem = pl.BlockSpec(memory_space=pltpu.VMEM)
    each = 2 * parts.shape[1] // rounds
    return pl.pallas_call(
        functools.partial(nearest_kernel, sketch_size, each),
        in_specs=[vmem],
        out_specs=vmem,
        out_shape=jax.ShapeDtypeStruct((rounds, parts.shape[2] // 2), F32),
        compiler_params=params(),
        name="nearest",
    )(parts)


def per_device(chunks, feat, ex, grads, first_factor, second_factor, picks):
    rows = grads.shape[0]
    local_blocks = first_factor.shape[0]
    groups, _, width = second_factor.shape
    factor = jnp.swapaxes(first_factor, 1, 2)
    pieces, start = [], 0
    for count in chunks:
        inner = first_products(grads, factor, start, count)
        piece = lax.all_to_all(inner, "feat", split_axis=0, concat_axis=0, tiled=True)
        pieces.append(piece.reshape(feat, groups, count // 2, 2 * rows))
        start += count
    turned_factors = turned(second_factor, feat, [count // 2 for count in chunks])
    base = (lax.axis_index("ex") * rows).astype(jnp.int32).reshape(1)
    sketch, fetched = second_products(base, picks, turned_factors, pieces, rows)
    step = 1
    parts = [fetched]
    while step < ex:
        parts = parts + [lax.ppermute(x, "ex", [(i, i ^ step) for i in range(ex)]) for x in parts]
        step *= 2
    part = distances(sketch, parts)
    spread = jnp.broadcast_to(part[None], (feat,) + part.shape)
    gathered = lax.all_to_all(spread, "feat", split_axis=0, concat_axis=0, tiled=True)
    coverage = nearest(gathered, feat * groups * width, picks.shape[0])
    return (sketch, coverage)


def solution(mesh):
    feat, ex = mesh.shape["feat"], mesh.shape["ex"]
    in_specs = (P("ex", "feat"), P("feat", None, None), P("feat", None, None), P())
    out_specs = (P("ex", "feat"), P(None, "ex"))

    def run(grads, first_factor, second_factor, picks):
        blocks = first_factor.shape[0] // feat
        chunks = [blocks]
        return jax.shard_map(
            functools.partial(per_device, chunks, feat, ex),
            mesh=mesh,
            in_specs=in_specs,
            out_specs=out_specs,
            check_vma=False,
        )(grads, first_factor, second_factor, picks)

    return run
```

time: 149 us -> 89.5 us (0.60)
  Pallas kernels: 0 us -> 29.8 us
  blocking collectives: 37.1 us -> 10.7 us
  waiting for transfers between devices: 57.5 us -> 34.9 us
  matrix products: 21.6 us -> 0 us
  between operations: 14.1 us -> 0.67 us
  local copies, waits for them, and re-layouts: 8.42 us -> 2.61 us
  starting transfers between devices: 7.29 us -> 10.3 us
  other arithmetic: 2.93 us -> 0 us
    psum x1 -> x0, blocking collectives: 37.1 us -> none  [per_device(): nearest = jnp.min(lax.psum(part, 'feat') / SKETCH, axis=1)]
    psum x1 -> x0, waiting for transfers between devices: 31.8 us -> none  [per_device(): diff = sketch[:, None, :] - lax.psum(fetch_part, 'ex')[None, :, :]]
    pallas_call x0 -> x5, Pallas kernels: none -> 29.8 us  [the longest x1 19.2 us: first_products(): pl.pallas_call(functools.partial(first_kernel, step_blocks, half, flush),...]
    dot_general x10 -> x0, matrix products: 21.6 us -> none  [the longest x1 14.4 us: per_device(): jnp.einsum('ebi,bik->kbe', blocks, first_factor, preferred_element_type=j...]
    ppermute x0 -> x3, waiting for transfers between devices: none -> 11.3 us  [per_device(): lax.ppermute(x, 'ex', [(i, i ^ step) for i in range(ex)])]
    all_to_all x0 -> x1, blocking collectives: none -> 10.7 us  [per_device(): lax.all_to_all(spread, 'feat', split_axis=0, concat_axis=0, tiled=True)]
    convert_element_type x1 -> x0, local copies, waits for them, and re-layouts: 4.05 us -> none  [per_device(): inner = jnp.einsum('ebi,bik->kbe', blocks, first_factor, preferred_elemen...]
    all_to_all x2 -> x0, local copies, waits for them, and re-layouts: 3.23 us -> none  [per_device(): lax.all_to_all(inner, 'feat', split_axis=0, concat_axis=1, tiled=True)]
  transfers between devices with their start and end apart: 2 -> 4, of which waited for: 2 -> 3; matrix products, arithmetic and copies ran while one was open for 0% -> 0% of each run, Pallas kernels for 0% -> 1%
where the time goes in v1:
time: 89.5 us; the launch traced here: 89 us
  waiting for transfers between devices  34.9 us (39%)
  Pallas kernels  29.8 us (33%)
  blocking collectives  10.7 us (12%)
  starting transfers between devices  10.3 us (12%)
  local copies, waits for them, and re-layouts  2.61 us (3%)
    all_to_all x1, waiting for transfers between devices, per_device(): lax.all_to_all(inner, 'feat', split_axis=0, concat_axis=0, tiled=True)  23.6 us
    pallas_call x1, Pallas kernels, first_products(): pl.pallas_call(functools.partial(first_kernel, step_blocks, half, flush),...  19.2 us
    ppermute x3, waiting for transfers between devices, per_device(): lax.ppermute(x, 'ex', [(i, i ^ step) for i in range(ex)])  11.3 us
    all_to_all x1, blocking collectives, per_device(): lax.all_to_all(spread, 'feat', split_axis=0, concat_axis=0, tiled=True)  10.7 us
    all_to_all x1, starting transfers between devices, per_device(): lax.all_to_all(inner, 'feat', split_axis=0, concat_axis=0, tiled=True)  7.25 us
    pallas_call x1, Pallas kernels, distances(): pl.pallas_call(distance_kernel, in_specs=[vmem] * (1 + len(fetched)), out...  7.08 us
    ppermute x3, starting transfers between devices, per_device(): lax.ppermute(x, 'ex', [(i, i ^ step) for i in range(ex)])  3.05 us
    unnamed x6, local copies, waits for them, and re-layouts  2.54 us
  transfers between devices with their start and end apart: 4, of which 3 were waited for; matrix products, arithmetic and copies ran while one was open for 0% of the time, Pallas kernels for 1%

profile of v1, /device:TPU:0, one launch (start us, length us, event | category | flops | bytes accessed | tf_op | source)
XLA Modules:
  0.0 89.0 jit_solution(1943022312486564215)
XLA Ops:
  0.6 0.0 copy-start.2
  0.6 19.2 %first_products.1 = bf16[64,64,128]{2,1,0:T(8,128)(2,1)} custom-call(bf16[64,131072]{1,0:T(8,128)(2,1)} %g1.1, bf16[64,131072]{1,0:T(8,128)(2,1)} %g1.1, bf16[128,64,1024]{2,1,0:T(8,128)(2,1)} %bitcast.6, bf16[128,64,1024]{2,1,0:T(8,128)(2,1)} %bitcast.7), custom_call_target="tpu_custom_call" | custom-call | flops 1073741824 | bytes 33554432 | tf_op jit(solution)/shard_map/first_products/pallas_call | solution.py:49
  19.9 7.3 %all-to-all-start = ((bf16[64,64,128]{2,1,0:T(8,128)(2,1)}), bf16[64,64,128]{2,1,0:T(8,128)(2,1)S(1)}, u32[]{:S(2)}, u32[]{:S(2)}) async-start(bf16[64,64,128]{2,1,0:T(8,128)(2,1)} %first_products.1), calls=%async_computation | async-start | bytes 2097152 | tf_op jit(solution)/shard_map/all_to_all | solution.py:208
  27.1 0.0 copy-start
  27.1 1.6 %copy-done = bf16[8,1024,128]{2,1,0:T(8,128)(2,1)S(1)} copy-done((bf16[8,1024,128]{2,1,0:T(8,128)(2,1)S(1)}, bf16[8,1024,128]{2,1,0:T(8,128)(2,1)}, u32[]{:S(2)}) %copy-start) | copy-done | bytes 2097176
  28.7 0.6 turned_factor.1.refs_2_
  29.3 23.6 %all-to-all-done = bf16[64,64,128]{2,1,0:T(8,128)(2,1)S(1)} async-done(((bf16[64,64,128]{2,1,0:T(8,128)(2,1)}), bf16[64,64,128]{2,1,0:T(8,128)(2,1)S(1)}, u32[]{:S(2)}, u32[]{:S(2)}) %all-to-all-start) | async-done | bytes 1048608 | tf_op jit(solution)/shard_map/all_to_all | solution.py:208
  52.9 0.0 copy-done.2
  52.9 2.3 %second_products.1 = (f32[64,1024]{1,0:T(8,128)}, f32[64,8,128]{2,1,0:T(8,128)S(1)}) custom-call(s32[1]{0:T(128)} %bitcast.refs_0_, s32[8,8]{1,0:T(8,128)S(1)} %copy-done.2, bf16[8,256,512]{2,1,0:T(8,128)(2,1)S(1)} %turned_factor.1.refs_2_, bf16[8,8,64,128]{3,2,1,0:T(8,128)(2,1)S(1)} %bitcast.4), custom_call_target="tpu_custom_call" | custom-call | tf_op jit(solution)/shard_map/second_products/pallas_call | solution.py:122
  55.1 0.0 collective-permute-start
  55.1 1.5 %collective-permute-start.1 = (f32[64,8,128]{2,1,0:T(8,128)S(1)}, f32[64,8,128]{2,1,0:T(8,128)S(1)}, u32[]{:S(2)}, u32[]{:S(2)}) collective-permute-start(f32[64,8,128]{2,1,0:T(8,128)S(1)} %get-tuple-element.5.refs_0_), channel_id=1, source_target_pairs={{0,2},{1,3},{2,0},{3,1},{4,6},{5,7},{6,4},{7,5},{8,10},{9,11},{10,... | collective-permute-start | bytes 786440 | tf_op jit(solution)/shard_map/ppermute | solution.py:217
  56.7 0.0 collective-permute-done.refs_1_
  56.7 1.5 %collective-permute-start.2 = (f32[64,8,128]{2,1,0:T(8,128)S(1)}, f32[64,8,128]{2,1,0:T(8,128)S(1)}, u32[]{:S(2)}, u32[]{:S(2)}) collective-permute-start(f32[64,8,128]{2,1,0:T(8,128)S(1)} %collective-permute-done.refs_1_), channel_id=1, source_target_pairs={{0,2},{1,3},{2,0},{3,1},{4,6},{5,7},{6,4},{7,5},{8,10},{9,11},{10,... | collective-permute-start | bytes 786440 | tf_op jit(solution)/shard_map/ppermute | solution.py:217
  58.2 6.0 %collective-permute-done.1.refs_2_ = f32[64,8,128]{2,1,0:T(8,128)S(1)} collective-permute-done((f32[64,8,128]{2,1,0:T(8,128)S(1)}, f32[64,8,128]{2,1,0:T(8,128)S(1)}, u32[]{:S(2)}, u32[]{:S(2)}) %collective-permute-start.1) | collective-permute-done | bytes 262176 | tf_op jit(solution)/shard_map/ppermute | solution.py:217
  64.3 5.2 %collective-permute-done.2.refs_3_ = f32[64,8,128]{2,1,0:T(8,128)S(1)} collective-permute-done((f32[64,8,128]{2,1,0:T(8,128)S(1)}, f32[64,8,128]{2,1,0:T(8,128)S(1)}, u32[]{:S(2)}, u32[]{:S(2)}) %collective-permute-start.2) | collective-permute-done | bytes 262176 | tf_op jit(solution)/shard_map/ppermute | solution.py:217
  69.5 0.0 copy-start.1
  69.5 0.9 %copy-done.1 = f32[64,1024]{1,0:T(8,128)S(1)} copy-done((f32[64,1024]{1,0:T(8,128)S(1)}, f32[64,1024]{1,0:T(8,128)}, u32[]{:S(2)}) %copy-start.1) | copy-done | bytes 262168
  70.4 7.1 %distances.1 = f32[32,128]{1,0:T(8,128)S(1)} custom-call(f32[64,1024]{1,0:T(8,128)S(1)} %copy-done.1, f32[64,8,128]{2,1,0:T(8,128)S(1)} %get-tuple-element.5.refs_0_, f32[64,8,128]{2,1,0:T(8,128)S(1)} %collective-permute-done.refs_1_, f32[64,8,128]{2,1,0:T(8,128)S(1)} %collective-permute-done.1.refs_2_, f32[64,8,128]{2,1,0:T(8,128)S(1)} %collective-permute-done.2.refs_3_), custom_call_target="tpu_custom_call" | custom-call | tf_op jit(solution)/shard_map/distances/pallas_call | solution.py:162
  77.5 0.1 broadcast_in_dim.2
  77.6 10.7 %all_to_all.10.parts = f32[8,32,128]{2,1,0:T(8,128)S(1)} all-to-all(f32[8,32,128]{2,1,0:T(8,128)S(1)} %broadcast_in_dim.2), channel_id=1, replica_groups=mesh['feat'=8,'ex'=4] {'feat'}, dimensions={0} | all-to-all | bytes 262144 | tf_op jit(solution)/shard_map/all_to_all | solution.py:221
  88.3 0.7 nearest.1
Async XLA Ops:
  0.6 52.3 %copy-start.2 = (s32[8,8]{1,0:T(8,128)S(1)}, s32[8,8]{1,0:T(8,128)}, u32[]{:S(2)}) copy-start(s32[8,8]{1,0:T(8,128)} %refs_1_.1) | copy-start | bytes 772
  19.9 33.0 %all-to-all-start = ((bf16[64,64,128]{2,1,0:T(8,128)(2,1)}), bf16[64,64,128]{2,1,0:T(8,128)(2,1)S(1)}, u32[]{:S(2)}, u32[]{:S(2)}) async-start(bf16[64,64,128]{2,1,0:T(8,128)(2,1)} %first_products.1), calls=%async_computation | async-start | bytes 2097152 | tf_op jit(solution)/shard_map/all_to_all | solution.py:208
  27.1 1.6 %copy-start = (bf16[8,1024,128]{2,1,0:T(8,128)(2,1)S(1)}, bf16[8,1024,128]{2,1,0:T(8,128)(2,1)}, u32[]{:S(2)}) copy-start(bf16[8,1024,128]{2,1,0:T(8,128)(2,1)} %param.6) | copy-start | bytes 6291460
  55.1 1.5 %collective-permute-start = (f32[64,8,128]{2,1,0:T(8,128)S(1)}, f32[64,8,128]{2,1,0:T(8,128)S(1)}, u32[]{:S(2)}, u32[]{:S(2)}) collective-permute-start(f32[64,8,128]{2,1,0:T(8,128)S(1)} %get-tuple-element.5.refs_0_), channel_id=1, source_target_pairs={{0,1},{1,0},{2,3},{3,2},{4,5},{5,4},{6,7},{7,6},{8,9},{9,8},{10,11... | collective-permute-start | bytes 786440 | tf_op jit(solution)/shard_map/ppermute | solution.py:217
  55.1 9.1 %collective-permute-start.1 = (f32[64,8,128]{2,1,0:T(8,128)S(1)}, f32[64,8,128]{2,1,0:T(8,128)S(1)}, u32[]{:S(2)}, u32[]{:S(2)}) collective-permute-start(f32[64,8,128]{2,1,0:T(8,128)S(1)} %get-tuple-element.5.refs_0_), channel_id=1, source_target_pairs={{0,2},{1,3},{2,0},{3,1},{4,6},{5,7},{6,4},{7,5},{8,10},{9,11},{10,... | collective-permute-start | bytes 786440 | tf_op jit(solution)/shard_map/ppermute | solution.py:217
  56.7 12.8 %collective-permute-start.2 = (f32[64,8,128]{2,1,0:T(8,128)S(1)}, f32[64,8,128]{2,1,0:T(8,128)S(1)}, u32[]{:S(2)}, u32[]{:S(2)}) collective-permute-start(f32[64,8,128]{2,1,0:T(8,128)S(1)} %collective-permute-done.refs_1_), channel_id=1, source_target_pairs={{0,2},{1,3},{2,0},{3,1},{4,6},{5,7},{6,4},{7,5},{8,10},{9,11},{10,... | collective-permute-start | bytes 786440 | tf_op jit(solution)/shard_map/ppermute | solution.py:217
  69.5 1.0 %copy-start.1 = (f32[64,1024]{1,0:T(8,128)S(1)}, f32[64,1024]{1,0:T(8,128)}, u32[]{:S(2)}) copy-start(f32[64,1024]{1,0:T(8,128)} %get-tuple-element.2.sketch) | copy-start | bytes 786436

commit v2 on v0

v2 whole, which is shorter than its diff:
```python
import functools

import jax
import jax.numpy as jnp
from jax import lax
from jax.experimental import pallas as pl
from jax.experimental.pallas import tpu as pltpu
from jax.sharding import PartitionSpec as P

F32 = jnp.float32
BF16 = jnp.bfloat16
MIB = 1024 * 1024
NT = (((1,), (1,)), ((), ()))
NN = (((1,), (0,)), ((), ()))


def params(mib=8):
    return pltpu.CompilerParams(vmem_limit_bytes=mib * MIB)


def first_kernel(feat, start, half, step, flush, *refs):
    grads, factor, *outs, g_buf, w_buf, acc, sems = refs
    _, groups, size = factor.shape
    kept = groups // feat
    steps = half // step
    split = len(outs) > 1
    me = lax.axis_index("feat") if split else 0

    def copies(i):
        for h in range(2):
            block = start + h * half + i * step
            yield pltpu.make_async_copy(
                grads.at[:, pl.ds(block * size, step * size)], g_buf.at[h, i], sems.at[h, i, 0]
            )
            yield pltpu.make_async_copy(factor.at[pl.ds(block, step)], w_buf.at[h, i], sems.at[h, i, 1])

    for i in range(steps):
        for copy in copies(i):
            copy.start()
    for i in range(steps):
        for copy in copies(i):
            copy.wait()
        for t in range(step):
            cols = slice(t * size, (t + 1) * size)
            low = lax.dot_general(w_buf[0, i, t], g_buf[0, i, :, cols], NT, preferred_element_type=F32)
            high = lax.dot_general(w_buf[1, i, t], g_buf[1, i, :, cols], NT, preferred_element_type=F32)
            acc[pl.ds(i * step + t, groups, stride=half), :] = jnp.concatenate([low, high], axis=1)
        if (i + 1) * step % flush == 0:
            done = (i + 1) * step - flush
            for d in range(feat):
                first = (me ^ d) * (kept * half)
                for q in range(kept):
                    at = pl.multiple_of(first + q * half + done, 8)
                    rows = acc[pl.ds(at, flush), :].astype(BF16)
                    if split:
                        outs[d][q, done : done + flush, :] = rows
                    else:
                        outs[0][d * kept + q, done : done + flush, :] = rows


def first_products(grads, factor, feat, start, count, split):
    rows = grads.shape[0]
    _, groups, size = factor.shape
    kept = groups // feat
    half = count // 2
    step, flush = min(4, half), min(16, half)
    steps = half // step
    lanes = 2 * rows
    if split:
        out_shape = [jax.ShapeDtypeStruct((kept, half, lanes), BF16)] * feat
    else:
        out_shape = [jax.ShapeDtypeStruct((groups, half, lanes), BF16)]
    vmem = pl.BlockSpec(memory_space=pltpu.VMEM)
    hbm = pl.BlockSpec(memory_space=pl.ANY)
    return pl.pallas_call(
        functools.partial(first_kernel, feat, start, half, step, flush),
        in_specs=[hbm, hbm],
        out_specs=[vmem] * len(out_shape),
        out_shape=out_shape,
        scratch_shapes=[
            pltpu.VMEM((2, steps, rows, step * size), BF16),
            pltpu.VMEM((2, steps, step, groups, size), BF16),
            pltpu.VMEM((groups * half, lanes), F32),
            pltpu.SemaphoreType.DMA((2, steps, 2)),
        ],
        compiler_params=params(48),
        cost_estimate=pl.CostEstimate(
            flops=2 * count * rows * groups * size,
            bytes_accessed=2 * count * size * (rows + groups),
            transcendentals=0,
        ),
        name="first_products",
    )(grads, factor)


def turn_kernel(plan, local, second, *outs):
    me = lax.axis_index("feat")
    for (relative, sources, start, half), out in zip(plan, outs):
        for k in range(second.shape[0]):
            for h in range(2):
                rows = []
                for d in sources:
                    source = me ^ d if relative else d
                    at = source * local + start + h * half
                    rows.append(second[k, pl.ds(pl.multiple_of(at, 8) if relative else at, half), :])
                width = second.shape[2]
                out[k, h * width : (h + 1) * width, :] = jnp.concatenate(rows, axis=0).T


def turned(second, local, plan):
    groups, _, width = second.shape
    vmem = pl.BlockSpec(memory_space=pltpu.VMEM)
    return pl.pallas_call(
        functools.partial(turn_kernel, plan, local),
        in_specs=[vmem],
        out_specs=[vmem] * len(plan),
        out_shape=[
            jax.ShapeDtypeStruct((groups, 2 * width, len(sources) * half), BF16) for _, sources, _, half in plan
        ],
        compiler_params=params(),
        name="turned_factor",
    )(second)


def products(k, factors, pieces, rows):
    total = None
    for a, own in zip(factors, pieces):
        if len(own) == 1:
            groups = a.shape[0]
            own = [own[0].at[pl.ds(s * groups, groups)] for s in range(own[0].shape[0] // groups)]
        right = jnp.concatenate([x[k] for x in own], axis=0)
        part = lax.dot_general(a[k], right, NN, preferred_element_type=F32)
        total = part if total is None else total + part
    width = total.shape[0] // 2
    return (total[:width, :rows] + total[width:, rows:]).T


def split_refs(counts, refs):
    refs = list(refs)
    factors = [refs.pop(0) for _ in counts]
    pieces = [[refs.pop(0) for _ in range(n)] for n in counts]
    return factors, pieces, refs


def early_kernel(counts, *refs):
    factors, pieces, (out,) = split_refs(counts, refs)
    groups, both, _ = factors[0].shape
    width = both // 2
    for k in range(groups):
        out[:, k * width : (k + 1) * width] = products(k, factors, pieces, out.shape[0])


def early_products(factors, pieces, rows):
    groups, both, _ = factors[0].shape
    vmem = pl.BlockSpec(memory_space=pltpu.VMEM)
    counts = [len(own) for own in pieces]
    return pl.pallas_call(
        functools.partial(early_kernel, counts),
        in_specs=[vmem] * (len(counts) + sum(counts)),
        out_specs=vmem,
        out_shape=jax.ShapeDtypeStruct((rows, groups * both // 2), F32),
        compiler_params=params(),
        name="early_products",
    )(*factors, *[x for own in pieces for x in own])


def late_kernel(counts, picks, early, *refs):
    factors, pieces, (sketch, mine, other, held) = split_refs(counts, refs)
    groups, both, _ = factors[0].shape
    width, rows = both // 2, sketch.shape[0]
    slots = mine.shape[1]
    if groups < slots:
        held[...] = jnp.zeros_like(held)
    for k in range(groups):
        cols = slice(k * width, (k + 1) * width)
        mapped = early[:, cols] + products(k, factors, pieces, rows)
        sketch[:, cols] = mapped
        held[pl.ds(k, rows, stride=slots), :] = mapped
    rounds, each = picks.shape
    place = lax.axis_index("ex")
    base, core = place * rows, place % 2
    half = rounds // 2
    for r in range(half):
        for p in range(each):
            for out, side in ((mine, core), (other, 1 - core)):
                at = picks[side * half + r, p] - base
                held_here = (at >= 0) & (at < rows)
                start = pl.multiple_of(jnp.clip(at, 0, rows - 1) * slots, slots)
                out[r * each + p] = jnp.where(held_here, held[pl.ds(start, slots), :], 0.0)


def late_products(picks, early, factors, pieces):
    rows = early.shape[0]
    groups, both, _ = factors[0].shape
    width = both // 2
    slots = -(-groups // 8) * 8
    smem = pl.BlockSpec(memory_space=pltpu.SMEM)
    vmem = pl.BlockSpec(memory_space=pltpu.VMEM)
    counts = [len(own) for own in pieces]
    fetched = jax.ShapeDtypeStruct((picks.size // 2, slots, width), F32)
    return pl.pallas_call(
        functools.partial(late_kernel, counts),
        in_specs=[smem] + [vmem] * (1 + len(counts) + sum(counts)),
        out_specs=[vmem] * 3,
        out_shape=[jax.ShapeDtypeStruct(early.shape, F32), fetched, fetched],
        scratch_shapes=[pltpu.VMEM((rows * slots, width), F32)],
        compiler_params=params(),
        name="late_products",
    )(picks, early, *factors, *[x for own in pieces for x in own])


def distance_kernel(unroll, sketch, first, second, *refs):
    *before, out, center = refs
    rows, dims = sketch.shape
    count, _, width = center.shape
    center[...] = first[...] + second[...]
    lane = lax.broadcasted_iota(jnp.int32, (8, 128), 1)

    def some(i, sums):
        sums = list(sums)
        for g in range(rows // 8):
            block = [sketch[g * 8 : (g + 1) * 8, t * width : (t + 1) * width] for t in range(dims // width)]
            for u in range(unroll):
                p = i * unroll + u
                acc = None
                for t, own in enumerate(block):
                    diff = own - center[p, t : t + 1, :]
                    acc = diff * diff if acc is None else acc + diff * diff
                sums[g] = jnp.where(lane == p, jnp.sum(acc, axis=1, keepdims=True), sums[g])
        return tuple(sums)

    zeros = tuple(jnp.zeros((8, 128), F32) for _ in range(rows // 8))
    sums = lax.fori_loop(0, count // unroll, some, zeros)
    by_pick = jnp.concatenate(sums, axis=0).T[:count]
    if before:
        by_pick = jnp.concatenate([before[0][...], by_pick], axis=1)
    out[...] = by_pick


def distances(sketch, first, second, before=()):
    vmem = pl.BlockSpec(memory_space=pltpu.VMEM)
    count, rows = first.shape[0], sketch.shape[0]
    return pl.pallas_call(
        functools.partial(distance_kernel, 4),
        in_specs=[vmem] * (3 + len(before)),
        out_specs=vmem,
        out_shape=jax.ShapeDtypeStruct((count, rows * (1 + len(before))), F32),
        scratch_shapes=[pltpu.VMEM(first.shape, F32)],
        compiler_params=params(),
        name="distances",
    )(sketch, first, second, *before)


def nearest_kernel(sketch_size, each, parts, out):
    total = parts[0]
    for i in range(1, parts.shape[0]):
        total = total + parts[i]
    total = total / sketch_size
    half, rows = out.shape[0] // 2, out.shape[1]
    core = lax.axis_index("ex") % 2
    near = [jnp.min(total[r * each : (r + 1) * each, :], axis=0, keepdims=True) for r in range(half)]
    running = None
    for r in range(2 * half):
        own, other = near[r % half][:, :rows], near[r % half][:, rows:]
        row = jnp.where(core == r // half, own, other)
        running = row if running is None else jnp.minimum(running, row)
        out[r : r + 1, :] = running


def nearest(parts, sketch_size, rounds):
    vmem = pl.BlockSpec(memory_space=pltpu.VMEM)
    each = 2 * parts.shape[1] // rounds
    return pl.pallas_call(
        functools.partial(nearest_kernel, sketch_size, each),
        in_specs=[vmem],
        out_specs=vmem,
        out_shape=jax.ShapeDtypeStruct((rounds, parts.shape[2] // 2), F32),
        compiler_params=params(),
        name="nearest",
    )(parts)


def swap(x, axis, size, step):
    return lax.ppermute(x, axis, [(i, i ^ step) for i in range(size)])


def per_device(feat, ex, grads, first_factor, second_factor, picks):
    rows = grads.shape[0]
    local = first_factor.shape[0]
    groups, _, width = second_factor.shape
    near = feat // 2
    factor = jnp.swapaxes(first_factor, 1, 2)
    first_count = local // 2 if local % 64 == 0 else 0
    plan, pieces = [], []
    if first_count:
        (inner,) = first_products(grads, factor, feat, 0, first_count, False)
        inner = lax.all_to_all(inner, "feat", split_axis=0, concat_axis=0, tiled=True)
        pieces.append([inner])
        plan.append((False, tuple(range(feat)), 0, first_count // 2))
    split = first_products(grads, factor, feat, first_count, local - first_count, True)
    far = [swap(x, "feat", feat, d) for d, x in enumerate(split) if d >= near]
    close = [x if d == 0 else swap(x, "feat", feat, d) for d, x in enumerate(split[:near])]
    pieces += [close, far]
    half = (local - first_count) // 2
    plan += [(True, tuple(range(near)), first_count, half), (True, tuple(range(near, feat)), first_count, half)]

    factors = turned(second_factor, local, plan)
    early = early_products(factors[:-1], pieces[:-1], rows)
    sketch, mine, other = late_products(picks, early, factors[-1:], pieces[-1:])

    chip = mine + swap(other, "ex", ex, 1)
    across = [chip]
    step = 2
    while step < ex:
        across = across + [swap(x, "ex", ex, step) for x in across]
        step *= 2
    across = [across[0], sum(across[1:])]
    part = distances(sketch, *across)
    part = distances(sketch, *[swap(x, "ex", ex, 1) for x in across], before=(part,))
    spread = jnp.broadcast_to(part[None], (feat,) + part.shape)
    gathered = lax.all_to_all(spread, "feat", split_axis=0, concat_axis=0, tiled=True)
    coverage = nearest(gathered, feat * groups * width, picks.shape[0])
    return (sketch, coverage)


def solution(mesh):
    feat, ex = mesh.shape["feat"], mesh.shape["ex"]
    in_specs = (P("ex", "feat"), P("feat", None, None), P("feat", None, None), P())
    out_specs = (P("ex", "feat"), P(None, "ex"))
    return jax.shard_map(
        functools.partial(per_device, feat, ex),
        mesh=mesh,
        in_specs=in_specs,
        out_specs=out_specs,
        check_vma=False,
    )
```

time: 149 us -> 65.4 us (0.44)
  waiting for transfers between devices: 57.5 us -> 10.8 us
  blocking collectives: 37.1 us -> 11 us
  matrix products: 21.6 us -> 0 us
  Pallas kernels: 0 us -> 21.4 us
  between operations: 14.1 us -> 0.72 us
  starting transfers between devices: 7.29 us -> 20.3 us
  local copies, waits for them, and re-layouts: 8.42 us -> 0.98 us
  other arithmetic: 2.93 us -> 0.02 us
    psum x1 -> x0, blocking collectives: 37.1 us -> none  [per_device(): nearest = jnp.min(lax.psum(part, 'feat') / SKETCH, axis=1)]
    psum x1 -> x0, waiting for transfers between devices: 31.8 us -> none  [per_device(): diff = sketch[:, None, :] - lax.psum(fetch_part, 'ex')[None, :, :]]
    all_to_all x1, waiting for transfers between devices: 25.7 us -> 0.01 us  [per_device(): lax.all_to_all(inner, 'feat', split_axis=0, concat_axis=0, tiled=True)]
    dot_general x10 -> x0, matrix products: 21.6 us -> none  [the longest x1 14.4 us: per_device(): jnp.einsum('ebi,bik->kbe', blocks, first_factor, preferred_element_type=j...]
    pallas_call x0 -> x8, Pallas kernels: none -> 21.4 us  [the longest x2 14.2 us: first_products(): pl.pallas_call(functools.partial(first_kernel, feat, start, half, step, f...]
    ppermute x0 -> x11, starting transfers between devices: none -> 13 us  [swap(): return lax.ppermute(x, axis, [(i, i ^ step) for i in range(size)])]
    all_to_all x0 -> x1, blocking collectives: none -> 11 us  [per_device(): lax.all_to_all(spread, 'feat', split_axis=0, concat_axis=0, tiled=True)]
    ppermute x0 -> x11, waiting for transfers between devices: none -> 10.8 us  [swap(): return lax.ppermute(x, axis, [(i, i ^ step) for i in range(size)])]
  transfers between devices with their start and end apart: 2 -> 12, of which waited for: 2 -> 4; matrix products, arithmetic and copies ran while one was open for 0% -> 0% of each run, Pallas kernels for 0% -> 15%
where the time goes in v2:
time: 65.4 us; the launch traced here: 65.2 us
  Pallas kernels  21.4 us (33%)
  starting transfers between devices  20.3 us (31%)
  blocking collectives  11 us (17%)
  waiting for transfers between devices  10.8 us (17%)
  local copies, waits for them, and re-layouts  0.98 us (1%)
  between operations  0.72 us (1%)
    pallas_call x2, Pallas kernels, first_products(): pl.pallas_call(functools.partial(first_kernel, feat, start, half, step, f...  14.2 us
    ppermute x11, starting transfers between devices, swap(): return lax.ppermute(x, axis, [(i, i ^ step) for i in range(size)])  13 us
    all_to_all x1, blocking collectives, per_device(): lax.all_to_all(spread, 'feat', split_axis=0, concat_axis=0, tiled=True)  11 us
    ppermute x11, waiting for transfers between devices, swap(): return lax.ppermute(x, axis, [(i, i ^ step) for i in range(size)])  10.8 us
    all_to_all x1, starting transfers between devices, per_device(): lax.all_to_all(inner, 'feat', split_axis=0, concat_axis=0, tiled=True)  7.27 us
    pallas_call x2, Pallas kernels, distances(): pl.pallas_call(functools.partial(distance_kernel, 4), in_specs=[vmem] * (...  3.11 us
    pallas_call x1, Pallas kernels, late_products(): pl.pallas_call(functools.partial(late_kernel, counts), in_specs=[smem] +...  2.06 us
  transfers between devices with their start and end apart: 12, of which 4 were waited for; matrix products, arithmetic and copies ran while one was open for 0% of the time, Pallas kernels for 15%

profile of v2, /device:TPU:0, one launch (start us, length us, event | category | flops | bytes accessed | tf_op | source)
XLA Modules:
  0.0 65.2 jit_solution(9169774815223410547)
XLA Ops:
  0.6 7.4 %first_products.2 = bf16[64,32,128]{2,1,0:T(8,128)(2,1)} custom-call(bf16[64,131072]{1,0:T(8,128)(2,1)} %refs_0_.3, bf16[128,64,1024]{2,1,0:T(8,128)(2,1)} %bitcast.1), custom_call_target="tpu_custom_call" | custom-call | flops 536870912 | bytes 16777216 | tf_op jit(solution)/shard_map/first_products/pallas_call | solution.py:75
  8.0 7.3 %all-to-all-start = ((bf16[64,32,128]{2,1,0:T(8,128)(2,1)}), bf16[64,32,128]{2,1,0:T(8,128)(2,1)S(1)}, u32[]{:S(2)}, u32[]{:S(2)}) async-start(bf16[64,32,128]{2,1,0:T(8,128)(2,1)} %first_products.2), calls=%async_computation | async-start | bytes 1048576 | tf_op jit(solution)/shard_map/all_to_all | solution.py:297
  15.3 0.0 copy-start
  15.3 0.0 copy-start.2
  15.3 6.7 %first_products.3 = (bf16[8,32,128]{2,1,0:T(8,128)(2,1)S(1)}, bf16[8,32,128]{2,1,0:T(8,128)(2,1)S(1)}, bf16[8,32,128]{2,1,0:T(8,128)(2,1)S(1)}, bf16[8,32,128]{2...) custom-call(bf16[64,131072]{1,0:T(8,128)(2,1)} %refs_0_.3, ...), custom_call_target="tpu_custom_call" | custom-call | flops 536870912 | bytes 16777216 | tf_op jit(solution)/shard_map/first_products/pallas_call | solution.py:75
  22.1 2.1 %collective-permute-start = (bf16[8,32,128]{2,1,0:T(8,128)(2,1)S(1)}, bf16[8,32,128]{2,1,0:T(8,128)(2,1)S(1)}, u32[]{:S(2)}, u32[]{:S(2)}) collective-permute-start(bf16[8,32,128]{2,1,0:T(8,128)(2,1)S(1)} %get-tuple-element.19), channel_id=1, source_target_pairs={{0,4},{4,0},{8,12},{12,8},{16,20},{20,16},{24,28},{28,24},{1,5},{5... | collective-permute-start | bytes 196616 | tf_op jit(solution)/shard_map/ppermute | solution.py:284
  24.2 1.5 %collective-permute-start.1 = (bf16[8,32,128]{2,1,0:T(8,128)(2,1)S(1)}, bf16[8,32,128]{2,1,0:T(8,128)(2,1)S(1)}, u32[]{:S(2)}, u32[]{:S(2)}) collective-permute-start(bf16[8,32,128]{2,1,0:T(8,128)(2,1)S(1)} %get-tuple-element.20), channel_id=1, source_target_pairs={{0,8},{4,12},{8,0},{12,4},{16,24},{20,28},{24,16},{28,20},{1,9},{5... | collective-permute-start | bytes 196616 | tf_op jit(solution)/shard_map/ppermute | solution.py:284
  25.6 0.1 collective-permute-start.2
  25.7 2.8 %collective-permute-start.3 = (bf16[8,32,128]{2,1,0:T(8,128)(2,1)S(1)}, bf16[8,32,128]{2,1,0:T(8,128)(2,1)S(1)}, u32[]{:S(2)}, u32[]{:S(2)}) collective-permute-start(bf16[8,32,128]{2,1,0:T(8,128)(2,1)S(1)} %get-tuple-element.23), channel_id=1, source_target_pairs={{0,16},{4,20},{8,24},{12,28},{16,0},{20,4},{24,8},{28,12},{1,17},{... | collective-permute-start | bytes 196616 | tf_op jit(solution)/shard_map/ppermute | solution.py:284
  28.5 1.5 %collective-permute-start.4 = (bf16[8,32,128]{2,1,0:T(8,128)(2,1)S(1)}, bf16[8,32,128]{2,1,0:T(8,128)(2,1)S(1)}, u32[]{:S(2)}, u32[]{:S(2)}) collective-permute-start(bf16[8,32,128]{2,1,0:T(8,128)(2,1)S(1)} %get-tuple-element.24), channel_id=1, source_target_pairs={{0,20},{4,16},{8,28},{12,24},{16,4},{20,0},{24,12},{28,8},{1,21},{... | collective-permute-start | bytes 196616 | tf_op jit(solution)/shard_map/ppermute | solution.py:284
  30.0 0.0 collective-permute-done.refs_4_
  30.0 3.3 %collective-permute-start.5 = (bf16[8,32,128]{2,1,0:T(8,128)(2,1)S(1)}, bf16[8,32,128]{2,1,0:T(8,128)(2,1)S(1)}, u32[]{:S(2)}, u32[]{:S(2)}) collective-permute-start(bf16[8,32,128]{2,1,0:T(8,128)(2,1)S(1)} %get-tuple-element.25), channel_id=1, source_target_pairs={{0,24},{4,28},{8,16},{12,20},{16,8},{20,12},{24,0},{28,4},{1,25},{... | collective-permute-start | bytes 196616 | tf_op jit(solution)/shard_map/ppermute | solution.py:284
  33.3 0.0 collective-permute-done.1.refs_5_
  33.3 0.3 collective-permute-start.6
  33.5 0.0 copy-done
  33.5 0.6 turned_factor.1
  34.1 0.0 collective-permute-done.2.refs_6_
  34.2 0.0 all-to-all-done.refs_2_
  34.2 0.8 %early_products.1.early = f32[64,1024]{1,0:T(8,128)S(1)} custom-call(bf16[8,256,256]{2,1,0:T(8,128)(2,1)S(1)} %get-tuple-element.16.refs_0_, bf16[8,256,128]{2,1,0:T(8,128)(2,1)S(1)} %get-tuple-element.17.refs_1_, bf16[64,32,128]{2,1,0:T(8,128)(2,1)S(1)} %all-to-all-done.refs_2_, bf16[8,32,128]{2,1,0:T(8,128)(2,1)S(1)} %get-tuple-element.18.refs_3_, ...), custom_call_target="tpu_custom_call" | custom-call | tf_op jit(solution)/shard_map/early_products/pallas_call | solution.py:157
  34.9 0.0 collective-permute-done.3.refs_1_
  34.9 4.4 %collective-permute-done.4.refs_2_ = bf16[8,32,128]{2,1,0:T(8,128)(2,1)S(1)} collective-permute-done((bf16[8,32,128]{2,1,0:T(8,128)(2,1)S(1)}, bf16[8,32,128]{2,1,0:T(8,128)(2,1)S(1)}, u32[]{:S(2)}, u32[]{:S(2)}) %collective-permute-start.4) | collective-permute-done | bytes 65568 | tf_op jit(solution)/shard_map/ppermute | solution.py:284
  39.4 0.0 collective-permute-done.5.refs_3_
  39.4 1.0 %collective-permute-done.6.refs_4_ = bf16[8,32,128]{2,1,0:T(8,128)(2,1)S(1)} collective-permute-done((bf16[8,32,128]{2,1,0:T(8,128)(2,1)S(1)}, bf16[8,32,128]{2,1,0:T(8,128)(2,1)S(1)}, u32[]{:S(2)}, u32[]{:S(2)}) %collective-permute-start.6) | collective-permute-done | bytes 65568 | tf_op jit(solution)/shard_map/ppermute | solution.py:284
  40.3 0.0 copy-done.2
  40.3 2.1 %late_products.1 = (f32[64,1024]{1,0:T(8,128)}, f32[32,8,128]{2,1,0:T(8,128)S(1)}, f32[32,8,128]{2,1,0:T(8,128)S(1)}) custom-call(s32[8,8]{1,0:T(8,128)S(1)} %copy-done.2, f32[64,1024]{1,0:T(8,128)S(1)} %early_products.1.early, bf16[8,256,128]{2,1,0:T(8,128)(2,1)S(1)} %get-tuple-element.22.refs_0_, bf16[8,32,128]{2,1,0:T(8,128)(2,1)S(1)} %collective-permute-done.3.refs_1_, ...), custom_call_target="tpu_custom_call" | custom-call | tf_op jit(solution)/shard_map/late_products/pallas_call | solution.py:201
  42.4 0.0 collective-permute-start.7
  42.4 1.3 %collective-permute-done.7 = f32[32,8,128]{2,1,0:T(8,128)S(1)} collective-permute-done((f32[32,8,128]{2,1,0:T(8,128)S(1)}, f32[32,8,128]{2,1,0:T(8,128)S(1)}, u32[]{:S(2)}, u32[]{:S(2)}) %collective-permute-start.7) | collective-permute-done | bytes 131104 | tf_op jit(solution)/shard_map/ppermute | solution.py:284
  43.8 1.6 %collective-permute-start.9 = (f32[32,8,128]{2,1,0:T(8,128)S(1)}, f32[32,8,128]{2,1,0:T(8,128)S(1)}, u32[]{:S(2)}, u32[]{:S(2)}) collective-permute-start(f32[32,8,128]{2,1,0:T(8,128)S(1)} %add.3.first), channel_id=1, source_target_pairs={{0,2},{1,3},{2,0},{3,1},{4,6},{5,7},{6,4},{7,5},{8,10},{9,11},{10,... | collective-permute-start | bytes 393224 | tf_op jit(solution)/shard_map/ppermute | solution.py:284
  45.4 0.0 collective-permute-start.8
  45.4 4.0 %collective-permute-done.9.second = f32[32,8,128]{2,1,0:T(8,128)S(1)} collective-permute-done((f32[32,8,128]{2,1,0:T(8,128)S(1)}, f32[32,8,128]{2,1,0:T(8,128)S(1)}, u32[]{:S(2)}, u32[]{:S(2)}) %collective-permute-start.9) | collective-permute-done | bytes 131104 | tf_op jit(solution)/shard_map/ppermute | solution.py:284
  49.4 0.0 collective-permute-start.10
  49.4 0.0 copy-start.1
  49.4 0.9 %copy-done.1 = f32[64,1024]{1,0:T(8,128)S(1)} copy-done((f32[64,1024]{1,0:T(8,128)S(1)}, f32[64,1024]{1,0:T(8,128)}, u32[]{:S(2)}) %copy-start.1) | copy-done | bytes 262168
  50.3 1.5 %distances.2.refs_0_ = f32[32,64]{1,0:T(8,128)S(1)} custom-call(f32[64,1024]{1,0:T(8,128)S(1)} %copy-done.1, f32[32,8,128]{2,1,0:T(8,128)S(1)} %add.3.first, f32[32,8,128]{2,1,0:T(8,128)S(1)} %collective-permute-done.9.second), custom_call_target="tpu_custom_call" | custom-call | tf_op jit(solution)/shard_map/distances/pallas_call | solution.py:243
  51.9 0.0 collective-permute-done.8.first
  51.9 0.0 collective-permute-done.10.second
  51.9 1.6 %distances.3 = f32[32,128]{1,0:T(8,128)S(1)} custom-call(f32[64,1024]{1,0:T(8,128)S(1)} %copy-done.1, f32[32,8,128]{2,1,0:T(8,128)S(1)} %collective-permute-done.8.first, f32[32,8,128]{2,1,0:T(8,128)S(1)} %collective-permute-done.10.second, f32[32,64]{1,0:T(8,128)S(1)} %distances.2.refs_0_), custom_call_target="tpu_custom_call" | custom-call | tf_op jit(solution)/shard_map/distances/pallas_call | solution.py:243
  53.5 11.0 %all_to_all.10.parts = f32[8,32,128]{2,1,0:T(8,128)S(1)} all-to-all(f32[8,32,128]{2,1,0:T(8,128)S(1)} %broadcast_in_dim.2), channel_id=1, replica_groups=mesh['feat'=8,'ex'=4] {'feat'}, dimensions={0} | all-to-all | bytes 262144 | tf_op jit(solution)/shard_map/all_to_all | solution.py:321
  64.5 0.7 %nearest.1 = f32[8,64]{1,0:T(8,128)} custom-call(f32[8,32,128]{2,1,0:T(8,128)S(1)} %all_to_all.10.parts), custom_call_target="tpu_custom_call" | custom-call | tf_op jit(solution)/shard_map/nearest/pallas_call | solution.py:273
  (2 shorter events, 0.0 us)
Async XLA Ops:
  8.0 26.1 %all-to-all-start = ((bf16[64,32,128]{2,1,0:T(8,128)(2,1)}), bf16[64,32,128]{2,1,0:T(8,128)(2,1)S(1)}, u32[]{:S(2)}, u32[]{:S(2)}) async-start(bf16[64,32,128]{2,1,0:T(8,128)(2,1)} %first_products.2), calls=%async_computation | async-start | bytes 1048576 | tf_op jit(solution)/shard_map/all_to_all | solution.py:297
  15.3 18.2 %copy-start = (bf16[8,1024,128]{2,1,0:T(8,128)(2,1)S(1)}, bf16[8,1024,128]{2,1,0:T(8,128)(2,1)}, u32[]{:S(2)}) copy-start(bf16[8,1024,128]{2,1,0:T(8,128)(2,1)} %second.1) | copy-start | bytes 6291460
  15.3 25.0 %copy-start.2 = (s32[8,8]{1,0:T(8,128)S(1)}, s32[8,8]{1,0:T(8,128)}, u32[]{:S(2)}) copy-start(s32[8,8]{1,0:T(8,128)} %picks.1) | copy-start | bytes 772
  22.1 7.9 %collective-permute-start = (bf16[8,32,128]{2,1,0:T(8,128)(2,1)S(1)}, bf16[8,32,128]{2,1,0:T(8,128)(2,1)S(1)}, u32[]{:S(2)}, u32[]{:S(2)}) collective-permute-start(bf16[8,32,128]{2,1,0:T(8,128)(2,1)S(1)} %get-tuple-element.19), channel_id=1, source_target_pairs={{0,4},{4,0},{8,12},{12,8},{16,20},{20,16},{24,28},{28,24},{1,5},{5... | collective-permute-start | bytes 196616 | tf_op jit(solution)/shard_map/ppermute | solution.py:284
  24.2 9.1 %collective-permute-start.1 = (bf16[8,32,128]{2,1,0:T(8,128)(2,1)S(1)}, bf16[8,32,128]{2,1,0:T(8,128)(2,1)S(1)}, u32[]{:S(2)}, u32[]{:S(2)}) collective-permute-start(bf16[8,32,128]{2,1,0:T(8,128)(2,1)S(1)} %get-tuple-element.20), channel_id=1, source_target_pairs={{0,8},{4,12},{8,0},{12,4},{16,24},{20,28},{24,16},{28,20},{1,9},{5... | collective-permute-start | bytes 196616 | tf_op jit(solution)/shard_map/ppermute | solution.py:284
  25.6 8.5 %collective-permute-start.2 = (bf16[8,32,128]{2,1,0:T(8,128)(2,1)S(1)}, bf16[8,32,128]{2,1,0:T(8,128)(2,1)S(1)}, u32[]{:S(2)}, u32[]{:S(2)}) collective-permute-start(bf16[8,32,128]{2,1,0:T(8,128)(2,1)S(1)} %get-tuple-element.21), channel_id=1, source_target_pairs={{0,12},{4,8},{8,4},{12,0},{16,28},{20,24},{24,20},{28,16},{1,13},{... | collective-permute-start | bytes 196616 | tf_op jit(solution)/shard_map/ppermute | solution.py:284
  25.7 9.2 %collective-permute-start.3 = (bf16[8,32,128]{2,1,0:T(8,128)(2,1)S(1)}, bf16[8,32,128]{2,1,0:T(8,128)(2,1)S(1)}, u32[]{:S(2)}, u32[]{:S(2)}) collective-permute-start(bf16[8,32,128]{2,1,0:T(8,128)(2,1)S(1)} %get-tuple-element.23), channel_id=1, source_target_pairs={{0,16},{4,20},{8,24},{12,28},{16,0},{20,4},{24,8},{28,12},{1,17},{... | collective-permute-start | bytes 196616 | tf_op jit(solution)/shard_map/ppermute | solution.py:284
  28.5 10.8 %collective-permute-start.4 = (bf16[8,32,128]{2,1,0:T(8,128)(2,1)S(1)}, bf16[8,32,128]{2,1,0:T(8,128)(2,1)S(1)}, u32[]{:S(2)}, u32[]{:S(2)}) collective-permute-start(bf16[8,32,128]{2,1,0:T(8,128)(2,1)S(1)} %get-tuple-element.24), channel_id=1, source_target_pairs={{0,20},{4,16},{8,28},{12,24},{16,4},{20,0},{24,12},{28,8},{1,21},{... | collective-permute-start | bytes 196616 | tf_op jit(solution)/shard_map/ppermute | solution.py:284
  30.0 9.4 %collective-permute-start.5 = (bf16[8,32,128]{2,1,0:T(8,128)(2,1)S(1)}, bf16[8,32,128]{2,1,0:T(8,128)(2,1)S(1)}, u32[]{:S(2)}, u32[]{:S(2)}) collective-permute-start(bf16[8,32,128]{2,1,0:T(8,128)(2,1)S(1)} %get-tuple-element.25), channel_id=1, source_target_pairs={{0,24},{4,28},{8,16},{12,20},{16,8},{20,12},{24,0},{28,4},{1,25},{... | collective-permute-start | bytes 196616 | tf_op jit(solution)/shard_map/ppermute | solution.py:284
  33.3 7.1 %collective-permute-start.6 = (bf16[8,32,128]{2,1,0:T(8,128)(2,1)S(1)}, bf16[8,32,128]{2,1,0:T(8,128)(2,1)S(1)}, u32[]{:S(2)}, u32[]{:S(2)}) collective-permute-start(bf16[8,32,128]{2,1,0:T(8,128)(2,1)S(1)} %get-tuple-element.26), channel_id=1, source_target_pairs={{0,28},{4,24},{8,20},{12,16},{16,12},{20,8},{24,4},{28,0},{1,29},{... | collective-permute-start | bytes 196616 | tf_op jit(solution)/shard_map/ppermute | solution.py:284
  42.4 1.3 %collective-permute-start.7 = (f32[32,8,128]{2,1,0:T(8,128)S(1)}, f32[32,8,128]{2,1,0:T(8,128)S(1)}, u32[]{:S(2)}, u32[]{:S(2)}) collective-permute-start(f32[32,8,128]{2,1,0:T(8,128)S(1)} %get-tuple-element.29), channel_id=1, source_target_pairs={{0,1},{1,0},{2,3},{3,2},{4,5},{5,4},{6,7},{7,6},{8,9},{9,8},{10,11... | collective-permute-start | bytes 393224 | tf_op jit(solution)/shard_map/ppermute | solution.py:284
  43.8 5.6 %collective-permute-start.9 = (f32[32,8,128]{2,1,0:T(8,128)S(1)}, f32[32,8,128]{2,1,0:T(8,128)S(1)}, u32[]{:S(2)}, u32[]{:S(2)}) collective-permute-start(f32[32,8,128]{2,1,0:T(8,128)S(1)} %add.3.first), channel_id=1, source_target_pairs={{0,2},{1,3},{2,0},{3,1},{4,6},{5,7},{6,4},{7,5},{8,10},{9,11},{10,... | collective-permute-start | bytes 393224 | tf_op jit(solution)/shard_map/ppermute | solution.py:284
  45.4 6.5 %collective-permute-start.8 = (f32[32,8,128]{2,1,0:T(8,128)S(1)}, f32[32,8,128]{2,1,0:T(8,128)S(1)}, u32[]{:S(2)}, u32[]{:S(2)}) collective-permute-start(f32[32,8,128]{2,1,0:T(8,128)S(1)} %add.3.first), channel_id=1, source_target_pairs={{0,1},{1,0},{2,3},{3,2},{4,5},{5,4},{6,7},{7,6},{8,9},{9,8},{10,11... | collective-permute-start | bytes 393224 | tf_op jit(solution)/shard_map/ppermute | solution.py:284
  49.4 2.5 %collective-permute-start.10 = (f32[32,8,128]{2,1,0:T(8,128)S(1)}, f32[32,8,128]{2,1,0:T(8,128)S(1)}, u32[]{:S(2)}, u32[]{:S(2)}) collective-permute-start(f32[32,8,128]{2,1,0:T(8,128)S(1)} %collective-permute-done.9.second), channel_id=1, source_target_pairs={{0,1},{1,0},{2,3},{3,2},{4,5},{5,4},{6,7},{7,6},{8,9},{9,8},{10,11... | collective-permute-start | bytes 393224 | tf_op jit(solution)/shard_map/ppermute | solution.py:284
  49.4 1.0 %copy-start.1 = (f32[64,1024]{1,0:T(8,128)S(1)}, f32[64,1024]{1,0:T(8,128)}, u32[]{:S(2)}) copy-start(f32[64,1024]{1,0:T(8,128)} %get-tuple-element.14.sketch) | copy-start | bytes 786436

commit v3 on v2

--- a/solution.py
+++ b/solution.py
@@ -58,7 +58,7 @@
                         outs[0][d * kept + q, done : done + flush, :] = rows
 
 
-def first_products(grads, factor, feat, start, count, split):
+def first_products(grads, factor, feat, split, start, count):
     rows = grads.shape[0]
     _, groups, size = factor.shape
     kept = groups // feat
@@ -95,15 +95,17 @@
 
 def turn_kernel(plan, local, second, *outs):
     me = lax.axis_index("feat")
-    for (relative, sources, start, half), out in zip(plan, outs):
+    width = second.shape[2]
+    for spans, out in zip(plan, outs):
         for k in range(second.shape[0]):
             for h in range(2):
                 rows = []
-                for d in sources:
-                    source = me ^ d if relative else d
-                    at = source * local + start + h * half
-                    rows.append(second[k, pl.ds(pl.multiple_of(at, 8) if relative else at, half), :])
-                width = second.shape[2]
+                for relative, source, start, half in spans:
+                    if relative:
+                        at = pl.multiple_of((me ^ source) * local + start + h * half, 8)
+                    else:
+                        at = source * local + start + h * half
+                    rows.append(second[k, pl.ds(at, half), :])
                 out[k, h * width : (h + 1) * width, :] = jnp.concatenate(rows, axis=0).T
 
 
@@ -115,7 +117,7 @@
         in_specs=[vmem],
         out_specs=[vmem] * len(plan),
         out_shape=[
-            jax.ShapeDtypeStruct((groups, 2 * width, len(sources) * half), BF16) for _, sources, _, half in plan
+            jax.ShapeDtypeStruct((groups, 2 * width, sum(span[-1] for span in spans)), BF16) for spans in plan
         ],
         compiler_params=params(),
         name="turned_factor",
@@ -125,10 +127,8 @@
 def products(k, factors, pieces, rows):
     total = None
     for a, own in zip(factors, pieces):
-        if len(own) == 1:
-            groups = a.shape[0]
-            own = [own[0].at[pl.ds(s * groups, groups)] for s in range(own[0].shape[0] // groups)]
-        right = jnp.concatenate([x[k] for x in own], axis=0)
+        groups = a.shape[0]
+        right = jnp.concatenate([x[at + k] for x in own for at in range(0, x.shape[0], groups)], axis=0)
         part = lax.dot_general(a[k], right, NN, preferred_element_type=F32)
         total = part if total is None else total + part
     width = total.shape[0] // 2
@@ -210,7 +210,14 @@
 
 
 def distance_kernel(unroll, sketch, first, second, *refs):
-    *before, out, center = refs
+    if len(refs) == 4:
+        kept, out, center, sem = refs
+        before = None
+        copy = pltpu.make_async_copy(sketch, kept, sem)
+        copy.start()
+    else:
+        before, out, center = refs
+        copy = None
     rows, dims = sketch.shape
     count, _, width = center.shape
     center[...] = first[...] + second[...]
@@ -232,29 +239,43 @@
     zeros = tuple(jnp.zeros((8, 128), F32) for _ in range(rows // 8))
     sums = lax.fori_loop(0, count // unroll, some, zeros)
     by_pick = jnp.concatenate(sums, axis=0).T[:count]
-    if before:
-        by_pick = jnp.concatenate([before[0][...], by_pick], axis=1)
-    out[...] = by_pick
-
-
-def distances(sketch, first, second, before=()):
-    vmem = pl.BlockSpec(memory_space=pltpu.VMEM)
+    if before is not None:
+        by_pick = jnp.concatenate([before[...], by_pick], axis=1)
+    out[...] = by_pick.astype(out.dtype)
+    if copy is not None:
+        copy.wait()
+
+
+def distances(sketch, first, second, before=None):
+    vmem = pl.BlockSpec(memory_space=pltpu.VMEM)
+    hbm = pl.BlockSpec(memory_space=pl.ANY)
     count, rows = first.shape[0], sketch.shape[0]
+    center = pltpu.VMEM(first.shape, F32)
+    if before is None:
+        return pl.pallas_call(
+            functools.partial(distance_kernel, 4),
+            in_specs=[vmem] * 3,
+            out_specs=[hbm, vmem],
+            out_shape=[jax.ShapeDtypeStruct(sketch.shape, F32), jax.ShapeDtypeStruct((count, rows), F32)],
+            scratch_shapes=[center, pltpu.SemaphoreType.DMA],
+            compiler_params=params(),
+            name="distances",
+        )(sketch, first, second)
     return pl.pallas_call(
         functools.partial(distance_kernel, 4),
-        in_specs=[vmem] * (3 + len(before)),
+        in_specs=[vmem] * 4,
         out_specs=vmem,
-        out_shape=jax.ShapeDtypeStruct((count, rows * (1 + len(before))), F32),
-        scratch_shapes=[pltpu.VMEM(first.shape, F32)],
+        out_shape=jax.ShapeDtypeStruct((count, 2 * rows), BF16),
+        scratch_shapes=[center],
         compiler_params=params(),
         name="distances",
-    )(sketch, first, second, *before)
+    )(sketch, first, second, before)
 
 
 def nearest_kernel(sketch_size, each, parts, out):
-    total = parts[0]
+    total = parts[0].astype(F32)
     for i in range(1, parts.shape[0]):
-        total = total + parts[i]
+        total = total + parts[i].astype(F32)
     total = total / sketch_size
     half, rows = out.shape[0] // 2, out.shape[1]
     core = lax.axis_index("ex") % 2
@@ -290,19 +311,18 @@
     groups, _, width = second_factor.shape
     near = feat // 2
     factor = jnp.swapaxes(first_factor, 1, 2)
-    first_count = local // 2 if local % 64 == 0 else 0
-    plan, pieces = [], []
-    if first_count:
-        (inner,) = first_products(grads, factor, feat, 0, first_count, False)
-        inner = lax.all_to_all(inner, "feat", split_axis=0, concat_axis=0, tiled=True)
-        pieces.append([inner])
-        plan.append((False, tuple(range(feat)), 0, first_count // 2))
-    split = first_products(grads, factor, feat, first_count, local - first_count, True)
-    far = [swap(x, "feat", feat, d) for d, x in enumerate(split) if d >= near]
+    count = local // 2 if local % 64 == 0 else local
+    start, half = local - count, count // 2
+    pieces, plan = [], []
+    if start:
+        (inner,) = first_products(grads, factor, feat, False, 0, start)
+        pieces.append([lax.all_to_all(inner, "feat", split_axis=0, concat_axis=0, tiled=True)])
+        plan.append([(False, d, 0, start // 2) for d in range(feat)])
+    split = first_products(grads, factor, feat, True, start, count)
+    far = [swap(x, "feat", feat, near + i) for i, x in enumerate(split[near:])]
     close = [x if d == 0 else swap(x, "feat", feat, d) for d, x in enumerate(split[:near])]
     pieces += [close, far]
-    half = (local - first_count) // 2
-    plan += [(True, tuple(range(near)), first_count, half), (True, tuple(range(near, feat)), first_count, half)]
+    plan += [[(True, d, start, half) for d in places] for places in (range(near), range(near, feat))]
 
     factors = turned(second_factor, local, plan)
     early = early_products(factors[:-1], pieces[:-1], rows)
@@ -315,12 +335,12 @@
         across = across + [swap(x, "ex", ex, step) for x in across]
         step *= 2
     across = [across[0], sum(across[1:])]
-    part = distances(sketch, *across)
-    part = distances(sketch, *[swap(x, "ex", ex, 1) for x in across], before=(part,))
+    kept, part = distances(sketch, *across)
+    part = distances(sketch, *[swap(x, "ex", ex, 1) for x in across], before=part)
     spread = jnp.broadcast_to(part[None], (feat,) + part.shape)
     gathered = lax.all_to_all(spread, "feat", split_axis=0, concat_axis=0, tiled=True)
     coverage = nearest(gathered, feat * groups * width, picks.shape[0])
-    return (sketch, coverage)
+    return (kept, coverage)
 
 
 def solution(mesh):

time: 65.4 us -> 63.1 us (0.965)
  local copies, waits for them, and re-layouts: 0.98 us -> 0.03 us
  blocking collectives: 11 us -> 10.2 us
  Pallas kernels: 21.4 us -> 20.7 us
    unnamed x6 -> x4, local copies, waits for them, and re-layouts: 0.96 us -> 0.01 us
    all_to_all x1, blocking collectives: 11 us -> 10.2 us  [per_device(): lax.all_to_all(spread, 'feat', split_axis=0, concat_axis=0, tiled=True)]
    pallas_call x1, Pallas kernels: 2.06 us -> 1.36 us  [late_products(): pl.pallas_call(functools.partial(late_kernel, counts), in_specs=[smem] +...]
where the time goes in v3:
time: 63.1 us; the launch traced here: 62.9 us
  Pallas kernels  20.7 us (33%)
  starting transfers between devices  20.4 us (32%)
  waiting for transfers between devices  10.8 us (17%)
  blocking collectives  10.2 us (16%)
  between operations  0.75 us (1%)
    pallas_call x2, Pallas kernels, first_products(): pl.pallas_call(functools.partial(first_kernel, feat, start, half, step, f...  14.2 us
    ppermute x11, starting transfers between devices, swap(): return lax.ppermute(x, axis, [(i, i ^ step) for i in range(size)])  13.1 us
    ppermute x11, waiting for transfers between devices, swap(): return lax.ppermute(x, axis, [(i, i ^ step) for i in range(size)])  10.8 us
    all_to_all x1, blocking collectives, per_device(): lax.all_to_all(spread, 'feat', split_axis=0, concat_axis=0, tiled=True)  10.2 us
    all_to_all x1, starting transfers between devices, per_device(): lax.all_to_all(inner, 'feat', split_axis=0, concat_axis=0, tiled=True)  7.27 us
    pallas_call x1, Pallas kernels, distances(): pl.pallas_call(functools.partial(distance_kernel, 4), in_specs=[vmem] * 4...  1.59 us
    pallas_call x1, Pallas kernels, distances(): pl.pallas_call(functools.partial(distance_kernel, 4), in_specs=[vmem] * 3...  1.54 us
    pallas_call x1, Pallas kernels, late_products(): pl.pallas_call(functools.partial(late_kernel, counts), in_specs=[smem] +...  1.36 us
  transfers between devices with their start and end apart: 12, of which 4 were waited for; matrix products, arithmetic and copies ran while one was open for 0% of the time, Pallas kernels for 15%

profile of v3, /device:TPU:0, one launch (start us, length us, event | category | flops | bytes accessed | tf_op | source)
XLA Modules:
  0.0 62.9 jit_solution(5511968555851700410)
XLA Ops:
  0.6 7.4 %first_products.2 = bf16[64,32,128]{2,1,0:T(8,128)(2,1)} custom-call(bf16[64,131072]{1,0:T(8,128)(2,1)} %refs_0_.3, bf16[128,64,1024]{2,1,0:T(8,128)(2,1)} %bitcast.1), custom_call_target="tpu_custom_call" | custom-call | flops 536870912 | bytes 16777216 | tf_op jit(solution)/shard_map/first_products/pallas_call | solution.py:75
  8.0 7.3 %all-to-all-start = ((bf16[64,32,128]{2,1,0:T(8,128)(2,1)}), bf16[64,32,128]{2,1,0:T(8,128)(2,1)S(1)}, u32[]{:S(2)}, u32[]{:S(2)}) async-start(bf16[64,32,128]{2,1,0:T(8,128)(2,1)} %first_products.2), calls=%async_computation | async-start | bytes 1048576 | tf_op jit(solution)/shard_map/all_to_all | solution.py:319
  15.3 0.0 copy-start
  15.3 0.0 copy-start.1
  15.3 6.7 %first_products.3 = (bf16[8,32,128]{2,1,0:T(8,128)(2,1)S(1)}, bf16[8,32,128]{2,1,0:T(8,128)(2,1)S(1)}, bf16[8,32,128]{2,1,0:T(8,128)(2,1)S(1)}, bf16[8,32,128]{2...) custom-call(bf16[64,131072]{1,0:T(8,128)(2,1)} %refs_0_.3, ...), custom_call_target="tpu_custom_call" | custom-call | flops 536870912 | bytes 16777216 | tf_op jit(solution)/shard_map/first_products/pallas_call | solution.py:75
  22.1 2.1 %collective-permute-start = (bf16[8,32,128]{2,1,0:T(8,128)(2,1)S(1)}, bf16[8,32,128]{2,1,0:T(8,128)(2,1)S(1)}, u32[]{:S(2)}, u32[]{:S(2)}) collective-permute-start(bf16[8,32,128]{2,1,0:T(8,128)(2,1)S(1)} %get-tuple-element.21), channel_id=1, source_target_pairs={{0,4},{4,0},{8,12},{12,8},{16,20},{20,16},{24,28},{28,24},{1,5},{5... | collective-permute-start | bytes 196616 | tf_op jit(solution)/shard_map/ppermute | solution.py:305
  24.2 1.5 %collective-permute-start.1 = (bf16[8,32,128]{2,1,0:T(8,128)(2,1)S(1)}, bf16[8,32,128]{2,1,0:T(8,128)(2,1)S(1)}, u32[]{:S(2)}, u32[]{:S(2)}) collective-permute-start(bf16[8,32,128]{2,1,0:T(8,128)(2,1)S(1)} %get-tuple-element.22), channel_id=1, source_target_pairs={{0,8},{4,12},{8,0},{12,4},{16,24},{20,28},{24,16},{28,20},{1,9},{5... | collective-permute-start | bytes 196616 | tf_op jit(solution)/shard_map/ppermute | solution.py:305
  25.6 0.1 collective-permute-start.2
  25.7 2.8 %collective-permute-start.3 = (bf16[8,32,128]{2,1,0:T(8,128)(2,1)S(1)}, bf16[8,32,128]{2,1,0:T(8,128)(2,1)S(1)}, u32[]{:S(2)}, u32[]{:S(2)}) collective-permute-start(bf16[8,32,128]{2,1,0:T(8,128)(2,1)S(1)} %get-tuple-element.25), channel_id=1, source_target_pairs={{0,16},{4,20},{8,24},{12,28},{16,0},{20,4},{24,8},{28,12},{1,17},{... | collective-permute-start | bytes 196616 | tf_op jit(solution)/shard_map/ppermute | solution.py:305
  28.5 1.5 %collective-permute-start.4 = (bf16[8,32,128]{2,1,0:T(8,128)(2,1)S(1)}, bf16[8,32,128]{2,1,0:T(8,128)(2,1)S(1)}, u32[]{:S(2)}, u32[]{:S(2)}) collective-permute-start(bf16[8,32,128]{2,1,0:T(8,128)(2,1)S(1)} %get-tuple-element.26), channel_id=1, source_target_pairs={{0,20},{4,16},{8,28},{12,24},{16,4},{20,0},{24,12},{28,8},{1,21},{... | collective-permute-start | bytes 196616 | tf_op jit(solution)/shard_map/ppermute | solution.py:305
  30.0 0.0 collective-permute-done.refs_4_
  30.0 3.3 %collective-permute-start.5 = (bf16[8,32,128]{2,1,0:T(8,128)(2,1)S(1)}, bf16[8,32,128]{2,1,0:T(8,128)(2,1)S(1)}, u32[]{:S(2)}, u32[]{:S(2)}) collective-permute-start(bf16[8,32,128]{2,1,0:T(8,128)(2,1)S(1)} %get-tuple-element.27), channel_id=1, source_target_pairs={{0,24},{4,28},{8,16},{12,20},{16,8},{20,12},{24,0},{28,4},{1,25},{... | collective-permute-start | bytes 196616 | tf_op jit(solution)/shard_map/ppermute | solution.py:305
  33.3 0.0 collective-permute-done.1.refs_5_
  33.3 0.3 collective-permute-start.6
  33.5 0.0 copy-done
  33.5 0.6 turned_factor.1
  34.1 0.0 collective-permute-done.2.refs_6_
  34.2 0.0 all-to-all-done.refs_2_
  34.2 0.8 %early_products.1.early = f32[64,1024]{1,0:T(8,128)S(1)} custom-call(bf16[8,256,256]{2,1,0:T(8,128)(2,1)S(1)} %get-tuple-element.18.refs_0_, bf16[8,256,128]{2,1,0:T(8,128)(2,1)S(1)} %get-tuple-element.19.refs_1_, bf16[64,32,128]{2,1,0:T(8,128)(2,1)S(1)} %all-to-all-done.refs_2_, bf16[8,32,128]{2,1,0:T(8,128)(2,1)S(1)} %get-tuple-element.20.refs_3_, ...), custom_call_target="tpu_custom_call" | custom-call | tf_op jit(solution)/shard_map/early_products/pallas_call | solution.py:157
  34.9 0.0 collective-permute-done.3.refs_1_
  34.9 4.4 %collective-permute-done.4.refs_2_ = bf16[8,32,128]{2,1,0:T(8,128)(2,1)S(1)} collective-permute-done((bf16[8,32,128]{2,1,0:T(8,128)(2,1)S(1)}, bf16[8,32,128]{2,1,0:T(8,128)(2,1)S(1)}, u32[]{:S(2)}, u32[]{:S(2)}) %collective-permute-start.4) | collective-permute-done | bytes 65568 | tf_op jit(solution)/shard_map/ppermute | solution.py:305
  39.4 0.0 collective-permute-done.5.refs_3_
  39.4 1.0 %collective-permute-done.6.refs_4_ = bf16[8,32,128]{2,1,0:T(8,128)(2,1)S(1)} collective-permute-done((bf16[8,32,128]{2,1,0:T(8,128)(2,1)S(1)}, bf16[8,32,128]{2,1,0:T(8,128)(2,1)S(1)}, u32[]{:S(2)}, u32[]{:S(2)}) %collective-permute-start.6) | collective-permute-done | bytes 65568 | tf_op jit(solution)/shard_map/ppermute | solution.py:305
  40.3 0.0 copy-done.1
  40.3 1.4 %late_products.1 = (f32[64,1024]{1,0:T(8,128)S(1)}, f32[32,8,128]{2,1,0:T(8,128)S(1)}, f32[32,8,128]{2,1,0:T(8,128)S(1)}) custom-call(s32[8,8]{1,0:T(8,128)S(1)} %copy-done.1, f32[64,1024]{1,0:T(8,128)S(1)} %early_products.1.early, bf16[8,256,128]{2,1,0:T(8,128)(2,1)S(1)} %get-tuple-element.24.refs_0_, ...), custom_call_target="tpu_custom_call" | custom-call | tf_op jit(solution)/shard_map/late_products/pallas_call | solution.py:201
  41.7 0.1 collective-permute-start.7
  41.8 1.3 %collective-permute-done.7 = f32[32,8,128]{2,1,0:T(8,128)S(1)} collective-permute-done((f32[32,8,128]{2,1,0:T(8,128)S(1)}, f32[32,8,128]{2,1,0:T(8,128)S(1)}, u32[]{:S(2)}, u32[]{:S(2)}) %collective-permute-start.7) | collective-permute-done | bytes 131104 | tf_op jit(solution)/shard_map/ppermute | solution.py:305
  43.2 1.6 %collective-permute-start.8 = (f32[32,8,128]{2,1,0:T(8,128)S(1)}, f32[32,8,128]{2,1,0:T(8,128)S(1)}, u32[]{:S(2)}, u32[]{:S(2)}) collective-permute-start(f32[32,8,128]{2,1,0:T(8,128)S(1)} %add.3.first), channel_id=1, source_target_pairs={{0,2},{1,3},{2,0},{3,1},{4,6},{5,7},{6,4},{7,5},{8,10},{9,11},{10,... | collective-permute-start | bytes 393224 | tf_op jit(solution)/shard_map/ppermute | solution.py:305
  44.7 0.0 collective-permute-start.9
  44.7 4.0 %collective-permute-done.8.second = f32[32,8,128]{2,1,0:T(8,128)S(1)} collective-permute-done((f32[32,8,128]{2,1,0:T(8,128)S(1)}, f32[32,8,128]{2,1,0:T(8,128)S(1)}, u32[]{:S(2)}, u32[]{:S(2)}) %collective-permute-start.8) | collective-permute-done | bytes 131104 | tf_op jit(solution)/shard_map/ppermute | solution.py:305
  48.8 0.0 collective-permute-start.10
  48.8 1.5 %distances.2 = (f32[64,1024]{1,0:T(8,128)}, f32[32,64]{1,0:T(8,128)S(1)}) custom-call(f32[64,1024]{1,0:T(8,128)S(1)} %get-tuple-element.29.sketch, f32[32,8,128]{2,1,0:T(8,128)S(1)} %add.3.first, f32[32,8,128]{2,1,0:T(8,128)S(1)} %collective-permute-done.8.second), custom_call_target="tpu_custom_call" | custom-call | tf_op jit(solution)/shard_map/distances/pallas_call | solution.py:255
  50.3 0.0 collective-permute-done.9.first
  50.3 0.0 collective-permute-done.10.second
  50.3 1.6 %distances.3 = bf16[32,128]{1,0:T(8,128)(2,1)S(1)} custom-call(f32[64,1024]{1,0:T(8,128)S(1)} %get-tuple-element.29.sketch, f32[32,8,128]{2,1,0:T(8,128)S(1)} %collective-permute-done.9.first, f32[32,8,128]{2,1,0:T(8,128)S(1)} %collective-permute-done.10.second, f32[32,64]{1,0:T(8,128)S(1)} %get-tuple-element.33.refs_0_), custom_call_target="tpu_custom_call" | custom-call | tf_op jit(solution)/shard_map/distances/pallas_call | solution.py:264
  52.0 10.2 %all_to_all.10.parts = bf16[8,32,128]{2,1,0:T(8,128)(2,1)S(1)} all-to-all(bf16[8,32,128]{2,1,0:T(8,128)(2,1)S(1)} %broadcast_in_dim.2), channel_id=1, replica_groups=mesh['feat'=8,'ex'=4] {'feat'}, dimensions={0} | all-to-all | bytes 131072 | tf_op jit(solution)/shard_map/all_to_all | solution.py:341
  62.2 0.7 %nearest.1 = f32[8,64]{1,0:T(8,128)} custom-call(bf16[8,32,128]{2,1,0:T(8,128)(2,1)S(1)} %all_to_all.10.parts), custom_call_target="tpu_custom_call" | custom-call | tf_op jit(solution)/shard_map/nearest/pallas_call | solution.py:294
  (2 shorter events, 0.0 us)
Async XLA Ops:
  8.0 26.1 %all-to-all-start = ((bf16[64,32,128]{2,1,0:T(8,128)(2,1)}), bf16[64,32,128]{2,1,0:T(8,128)(2,1)S(1)}, u32[]{:S(2)}, u32[]{:S(2)}) async-start(bf16[64,32,128]{2,1,0:T(8,128)(2,1)} %first_products.2), calls=%async_computation | async-start | bytes 1048576 | tf_op jit(solution)/shard_map/all_to_all | solution.py:319
  15.3 18.2 %copy-start = (bf16[8,1024,128]{2,1,0:T(8,128)(2,1)S(1)}, bf16[8,1024,128]{2,1,0:T(8,128)(2,1)}, u32[]{:S(2)}) copy-start(bf16[8,1024,128]{2,1,0:T(8,128)(2,1)} %second.1) | copy-start | bytes 6291460
  15.3 25.0 %copy-start.1 = (s32[8,8]{1,0:T(8,128)S(1)}, s32[8,8]{1,0:T(8,128)}, u32[]{:S(2)}) copy-start(s32[8,8]{1,0:T(8,128)} %picks.1) | copy-start | bytes 772
  22.1 7.9 %collective-permute-start = (bf16[8,32,128]{2,1,0:T(8,128)(2,1)S(1)}, bf16[8,32,128]{2,1,0:T(8,128)(2,1)S(1)}, u32[]{:S(2)}, u32[]{:S(2)}) collective-permute-start(bf16[8,32,128]{2,1,0:T(8,128)(2,1)S(1)} %get-tuple-element.21), channel_id=1, source_target_pairs={{0,4},{4,0},{8,12},{12,8},{16,20},{20,16},{24,28},{28,24},{1,5},{5... | collective-permute-start | bytes 196616 | tf_op jit(solution)/shard_map/ppermute | solution.py:305
  24.2 9.1 %collective-permute-start.1 = (bf16[8,32,128]{2,1,0:T(8,128)(2,1)S(1)}, bf16[8,32,128]{2,1,0:T(8,128)(2,1)S(1)}, u32[]{:S(2)}, u32[]{:S(2)}) collective-permute-start(bf16[8,32,128]{2,1,0:T(8,128)(2,1)S(1)} %get-tuple-element.22), channel_id=1, source_target_pairs={{0,8},{4,12},{8,0},{12,4},{16,24},{20,28},{24,16},{28,20},{1,9},{5... | collective-permute-start | bytes 196616 | tf_op jit(solution)/shard_map/ppermute | solution.py:305
  25.6 8.5 %collective-permute-start.2 = (bf16[8,32,128]{2,1,0:T(8,128)(2,1)S(1)}, bf16[8,32,128]{2,1,0:T(8,128)(2,1)S(1)}, u32[]{:S(2)}, u32[]{:S(2)}) collective-permute-start(bf16[8,32,128]{2,1,0:T(8,128)(2,1)S(1)} %get-tuple-element.23), channel_id=1, source_target_pairs={{0,12},{4,8},{8,4},{12,0},{16,28},{20,24},{24,20},{28,16},{1,13},{... | collective-permute-start | bytes 196616 | tf_op jit(solution)/shard_map/ppermute | solution.py:305
  25.7 9.2 %collective-permute-start.3 = (bf16[8,32,128]{2,1,0:T(8,128)(2,1)S(1)}, bf16[8,32,128]{2,1,0:T(8,128)(2,1)S(1)}, u32[]{:S(2)}, u32[]{:S(2)}) collective-permute-start(bf16[8,32,128]{2,1,0:T(8,128)(2,1)S(1)} %get-tuple-element.25), channel_id=1, source_target_pairs={{0,16},{4,20},{8,24},{12,28},{16,0},{20,4},{24,8},{28,12},{1,17},{... | collective-permute-start | bytes 196616 | tf_op jit(solution)/shard_map/ppermute | solution.py:305
  28.5 10.8 %collective-permute-start.4 = (bf16[8,32,128]{2,1,0:T(8,128)(2,1)S(1)}, bf16[8,32,128]{2,1,0:T(8,128)(2,1)S(1)}, u32[]{:S(2)}, u32[]{:S(2)}) collective-permute-start(bf16[8,32,128]{2,1,0:T(8,128)(2,1)S(1)} %get-tuple-element.26), channel_id=1, source_target_pairs={{0,20},{4,16},{8,28},{12,24},{16,4},{20,0},{24,12},{28,8},{1,21},{... | collective-permute-start | bytes 196616 | tf_op jit(solution)/shard_map/ppermute | solution.py:305
  30.0 9.4 %collective-permute-start.5 = (bf16[8,32,128]{2,1,0:T(8,128)(2,1)S(1)}, bf16[8,32,128]{2,1,0:T(8,128)(2,1)S(1)}, u32[]{:S(2)}, u32[]{:S(2)}) collective-permute-start(bf16[8,32,128]{2,1,0:T(8,128)(2,1)S(1)} %get-tuple-element.27), channel_id=1, source_target_pairs={{0,24},{4,28},{8,16},{12,20},{16,8},{20,12},{24,0},{28,4},{1,25},{... | collective-permute-start | bytes 196616 | tf_op jit(solution)/shard_map/ppermute | solution.py:305
  33.3 7.1 %collective-permute-start.6 = (bf16[8,32,128]{2,1,0:T(8,128)(2,1)S(1)}, bf16[8,32,128]{2,1,0:T(8,128)(2,1)S(1)}, u32[]{:S(2)}, u32[]{:S(2)}) collective-permute-start(bf16[8,32,128]{2,1,0:T(8,128)(2,1)S(1)} %get-tuple-element.28), channel_id=1, source_target_pairs={{0,28},{4,24},{8,20},{12,16},{16,12},{20,8},{24,4},{28,0},{1,29},{... | collective-permute-start | bytes 196616 | tf_op jit(solution)/shard_map/ppermute | solution.py:305
  41.7 1.4 %collective-permute-start.7 = (f32[32,8,128]{2,1,0:T(8,128)S(1)}, f32[32,8,128]{2,1,0:T(8,128)S(1)}, u32[]{:S(2)}, u32[]{:S(2)}) collective-permute-start(f32[32,8,128]{2,1,0:T(8,128)S(1)} %get-tuple-element.31), channel_id=1, source_target_pairs={{0,1},{1,0},{2,3},{3,2},{4,5},{5,4},{6,7},{7,6},{8,9},{9,8},{10,11... | collective-permute-start | bytes 393224 | tf_op jit(solution)/shard_map/ppermute | solution.py:305
  43.2 5.6 %collective-permute-start.8 = (f32[32,8,128]{2,1,0:T(8,128)S(1)}, f32[32,8,128]{2,1,0:T(8,128)S(1)}, u32[]{:S(2)}, u32[]{:S(2)}) collective-permute-start(f32[32,8,128]{2,1,0:T(8,128)S(1)} %add.3.first), channel_id=1, source_target_pairs={{0,2},{1,3},{2,0},{3,1},{4,6},{5,7},{6,4},{7,5},{8,10},{9,11},{10,... | collective-permute-start | bytes 393224 | tf_op jit(solution)/shard_map/ppermute | solution.py:305
  44.7 5.6 %collective-permute-start.9 = (f32[32,8,128]{2,1,0:T(8,128)S(1)}, f32[32,8,128]{2,1,0:T(8,128)S(1)}, u32[]{:S(2)}, u32[]{:S(2)}) collective-permute-start(f32[32,8,128]{2,1,0:T(8,128)S(1)} %add.3.first), channel_id=1, source_target_pairs={{0,1},{1,0},{2,3},{3,2},{4,5},{5,4},{6,7},{7,6},{8,9},{9,8},{10,11... | collective-permute-start | bytes 393224 | tf_op jit(solution)/shard_map/ppermute | solution.py:305
  48.8 1.6 %collective-permute-start.10 = (f32[32,8,128]{2,1,0:T(8,128)S(1)}, f32[32,8,128]{2,1,0:T(8,128)S(1)}, u32[]{:S(2)}, u32[]{:S(2)}) collective-permute-start(f32[32,8,128]{2,1,0:T(8,128)S(1)} %collective-permute-done.8.second), channel_id=1, source_target_pairs={{0,1},{1,0},{2,3},{3,2},{4,5},{5,4},{6,7},{7,6},{8,9},{9,8},{10,11... | collective-permute-start | bytes 393224 | tf_op jit(solution)/shard_map/ppermute | solution.py:305

commit v4 on v3

--- a/solution.py
+++ b/solution.py
@@ -10,6 +10,7 @@
 F32 = jnp.float32
 BF16 = jnp.bfloat16
 MIB = 1024 * 1024
+UNROLL = 4
 NT = (((1,), (1,)), ((), ()))
 NN = (((1,), (0,)), ((), ()))
 
@@ -209,67 +210,109 @@
     )(picks, early, *factors, *[x for own in pieces for x in own])
 
 
-def distance_kernel(unroll, sketch, first, second, *refs):
-    if len(refs) == 4:
-        kept, out, center, sem = refs
-        before = None
-        copy = pltpu.make_async_copy(sketch, kept, sem)
-        copy.start()
-    else:
-        before, out, center = refs
-        copy = None
+def listed(picks, chosen, side, own, rows):
+    rounds, each = picks.shape
+    count = rounds * each // 2
+    pair = lax.axis_index("ex") // 2
+
+    def one(i, n):
+        at = side * count + i
+        here = picks[at // each, at % each] // (2 * rows) == pair
+        chosen[n] = i
+        return n + (here if own else jnp.logical_not(here)).astype(jnp.int32)
+
+    n = lax.fori_loop(0, count, one, 0)
+    last = chosen[jnp.maximum(n - 1, 0)]
+    for extra in range(UNROLL - 1):
+        chosen[n + extra] = last
+    return (n + UNROLL - 1) // UNROLL
+
+
+def add_distances(sums, sketch, center, chosen, groups, first_lane):
     rows, dims = sketch.shape
-    count, _, width = center.shape
-    center[...] = first[...] + second[...]
+    width = center.shape[2]
     lane = lax.broadcasted_iota(jnp.int32, (8, 128), 1)
 
     def some(i, sums):
         sums = list(sums)
+        places = [chosen[i * UNROLL + u] for u in range(UNROLL)]
         for g in range(rows // 8):
             block = [sketch[g * 8 : (g + 1) * 8, t * width : (t + 1) * width] for t in range(dims // width)]
-            for u in range(unroll):
-                p = i * unroll + u
+            for p in places:
                 acc = None
                 for t, own in enumerate(block):
                     diff = own - center[p, t : t + 1, :]
                     acc = diff * diff if acc is None else acc + diff * diff
-                sums[g] = jnp.where(lane == p, jnp.sum(acc, axis=1, keepdims=True), sums[g])
+                sums[g] = jnp.where(lane == p + first_lane, jnp.sum(acc, axis=1, keepdims=True), sums[g])
         return tuple(sums)
 
-    zeros = tuple(jnp.zeros((8, 128), F32) for _ in range(rows // 8))
-    sums = lax.fori_loop(0, count // unroll, some, zeros)
-    by_pick = jnp.concatenate(sums, axis=0).T[:count]
-    if before is not None:
-        by_pick = jnp.concatenate([before[...], by_pick], axis=1)
-    out[...] = by_pick.astype(out.dtype)
-    if copy is not None:
-        copy.wait()
-
-
-def distances(sketch, first, second, before=None):
-    vmem = pl.BlockSpec(memory_space=pltpu.VMEM)
-    hbm = pl.BlockSpec(memory_space=pl.ANY)
-    count, rows = first.shape[0], sketch.shape[0]
-    center = pltpu.VMEM(first.shape, F32)
-    if before is None:
-        return pl.pallas_call(
-            functools.partial(distance_kernel, 4),
-            in_specs=[vmem] * 3,
-            out_specs=[hbm, vmem],
-            out_shape=[jax.ShapeDtypeStruct(sketch.shape, F32), jax.ShapeDtypeStruct((count, rows), F32)],
-            scratch_shapes=[center, pltpu.SemaphoreType.DMA],
-            compiler_params=params(),
-            name="distances",
-        )(sketch, first, second)
-    return pl.pallas_call(
-        functools.partial(distance_kernel, 4),
-        in_specs=[vmem] * 4,
+    return lax.fori_loop(0, groups, some, tuple(sums))
+
+
+def spread_sums(sums, rows):
+    return [sums[g * 8 : (g + 1) * 8, :] for g in range(rows // 8)]
+
+
+def held_kernel(picks, sketch, mine, other, kept, out, chosen, sem):
+    copy = pltpu.make_async_copy(sketch, kept, sem)
+    copy.start()
+    rows = sketch.shape[0]
+    core = lax.axis_index("ex") % 2
+    sums = [jnp.zeros((8, 128), F32) for _ in range(rows // 8)]
+    for side, center in enumerate((mine, other)):
+        groups = listed(picks, chosen, core if side == 0 else 1 - core, True, rows)
+        sums = add_distances(sums, sketch, center, chosen, groups, side * center.shape[0])
+    for g, own in enumerate(sums):
+        out[g * 8 : (g + 1) * 8, :] = own
+    copy.wait()
+
+
+def far_kernel(side, picks, sketch, center, before, out, chosen):
+    rows, count = sketch.shape[0], center.shape[0]
+    core = lax.axis_index("ex") % 2
+    groups = listed(picks, chosen, core if side == 0 else 1 - core, False, rows)
+    sums = add_distances(spread_sums(before, rows), sketch, center, chosen, groups, side * count)
+    if side == 0:
+        for g, own in enumerate(sums):
+            out[g * 8 : (g + 1) * 8, :] = own
+    else:
+        by_pick = jnp.concatenate(sums, axis=0).T
+        by_pick = jnp.concatenate([by_pick[:count], by_pick[count : 2 * count]], axis=1)
+        out[...] = by_pick.astype(out.dtype)
+
+
+def held_distances(picks, sketch, mine, other):
+    vmem = pl.BlockSpec(memory_space=pltpu.VMEM)
+    return pl.pallas_call(
+        held_kernel,
+        in_specs=[pl.BlockSpec(memory_space=pltpu.SMEM)] + [vmem] * 3,
+        out_specs=[pl.BlockSpec(memory_space=pl.ANY), vmem],
+        out_shape=[
+            jax.ShapeDtypeStruct(sketch.shape, F32),
+            jax.ShapeDtypeStruct((sketch.shape[0], 128), F32),
+        ],
+        scratch_shapes=[pltpu.SMEM((mine.shape[0] + UNROLL,), jnp.int32), pltpu.SemaphoreType.DMA],
+        compiler_params=params(),
+        name="held_distances",
+    )(picks, sketch, mine, other)
+
+
+def far_distances(side, picks, sketch, center, before):
+    vmem = pl.BlockSpec(memory_space=pltpu.VMEM)
+    count, rows = center.shape[0], sketch.shape[0]
+    if side == 0:
+        out = jax.ShapeDtypeStruct((rows, 128), F32)
+    else:
+        out = jax.ShapeDtypeStruct((count, 2 * rows), BF16)
+    return pl.pallas_call(
+        functools.partial(far_kernel, side),
+        in_specs=[pl.BlockSpec(memory_space=pltpu.SMEM)] + [vmem] * 3,
         out_specs=vmem,
-        out_shape=jax.ShapeDtypeStruct((count, 2 * rows), BF16),
-        scratch_shapes=[center],
-        compiler_params=params(),
-        name="distances",
-    )(sketch, first, second, before)
+        out_shape=out,
+        scratch_shapes=[pltpu.SMEM((count + UNROLL,), jnp.int32)],
+        compiler_params=params(),
+        name="far_distances",
+    )(picks, sketch, center, before)
 
 
 def nearest_kernel(sketch_size, each, parts, out):
@@ -328,15 +371,15 @@
     early = early_products(factors[:-1], pieces[:-1], rows)
     sketch, mine, other = late_products(picks, early, factors[-1:], pieces[-1:])
 
-    chip = mine + swap(other, "ex", ex, 1)
-    across = [chip]
-    step = 2
+    held = mine + swap(other, "ex", ex, 1)
+    across, step = [held], 2
     while step < ex:
         across = across + [swap(x, "ex", ex, step) for x in across]
         step *= 2
-    across = [across[0], sum(across[1:])]
-    kept, part = distances(sketch, *across)
-    part = distances(sketch, *[swap(x, "ex", ex, 1) for x in across], before=part)
+    away = sum(across[2:], across[1])
+    kept, part = held_distances(picks, sketch, held, swap(held, "ex", ex, 1))
+    part = far_distances(0, picks, sketch, away, part)
+    part = far_distances(1, picks, sketch, swap(away, "ex", ex, 1), part)
     spread = jnp.broadcast_to(part[None], (feat,) + part.shape)
     gathered = lax.all_to_all(spread, "feat", split_axis=0, concat_axis=0, tiled=True)
     coverage = nearest(gathered, feat * groups * width, picks.shape[0])

time: 63.1 us -> 67.9 us (1.076)
  Pallas kernels: 20.7 us -> 25.6 us
    pallas_call x2 -> x3, Pallas kernels: 3.14 us -> 7.98 us  [the longest x2 4.33 us: far_distances(): pl.pallas_call(functools.partial(far_kernel, side), in_specs=[pl.BlockSpe...]
  transfers between devices with their start and end apart: 12 -> 12, of which waited for: 4 -> 4; matrix products, arithmetic and copies ran while one was open for 0% -> 0% of each run, Pallas kernels for 15% -> 21%
where the time goes in v4:
time: 67.9 us; the launch traced here: 67.8 us
  Pallas kernels  25.6 us (38%)
  starting transfers between devices  20.4 us (30%)
  waiting for transfers between devices  10.8 us (16%)
  blocking collectives  10.2 us (15%)
  between operations  0.75 us (1%)
    pallas_call x2, Pallas kernels, first_products(): pl.pallas_call(functools.partial(first_kernel, feat, start, half, step, f...  14.2 us
    ppermute x11, starting transfers between devices, swap(): return lax.ppermute(x, axis, [(i, i ^ step) for i in range(size)])  13.1 us
    ppermute x11, waiting for transfers between devices, swap(): return lax.ppermute(x, axis, [(i, i ^ step) for i in range(size)])  10.8 us
    all_to_all x1, blocking collectives, per_device(): lax.all_to_all(spread, 'feat', split_axis=0, concat_axis=0, tiled=True)  10.2 us
    all_to_all x1, starting transfers between devices, per_device(): lax.all_to_all(inner, 'feat', split_axis=0, concat_axis=0, tiled=True)  7.27 us
    pallas_call x2, Pallas kernels, far_distances(): pl.pallas_call(functools.partial(far_kernel, side), in_specs=[pl.BlockSpe...  4.33 us
    pallas_call x1, Pallas kernels, held_distances(): pl.pallas_call(held_kernel, in_specs=[pl.BlockSpec(memory_space=pltpu.SME...  3.65 us
    pallas_call x1, Pallas kernels, late_products(): pl.pallas_call(functools.partial(late_kernel, counts), in_specs=[smem] +...  1.37 us
  transfers between devices with their start and end apart: 12, of which 4 were waited for; matrix products, arithmetic and copies ran while one was open for 0% of the time, Pallas kernels for 21%

profile of v4, /device:TPU:0, one launch (start us, length us, event | category | flops | bytes accessed | tf_op | source)
XLA Modules:
  0.0 67.8 jit_solution(1034448615699595194)
XLA Ops:
  0.6 7.4 %first_products.2 = bf16[64,32,128]{2,1,0:T(8,128)(2,1)} custom-call(bf16[64,131072]{1,0:T(8,128)(2,1)} %refs_0_.3, bf16[128,64,1024]{2,1,0:T(8,128)(2,1)} %bitcast.1), custom_call_target="tpu_custom_call" | custom-call | flops 536870912 | bytes 16777216 | tf_op jit(solution)/shard_map/first_products/pallas_call | solution.py:76
  8.0 7.3 %all-to-all-start = ((bf16[64,32,128]{2,1,0:T(8,128)(2,1)}), bf16[64,32,128]{2,1,0:T(8,128)(2,1)S(1)}, u32[]{:S(2)}, u32[]{:S(2)}) async-start(bf16[64,32,128]{2,1,0:T(8,128)(2,1)} %first_products.2), calls=%async_computation | async-start | bytes 1048576 | tf_op jit(solution)/shard_map/all_to_all | solution.py:362
  15.3 0.0 copy-start
  15.3 0.0 copy-start.1
  15.3 6.7 %first_products.3 = (bf16[8,32,128]{2,1,0:T(8,128)(2,1)S(1)}, bf16[8,32,128]{2,1,0:T(8,128)(2,1)S(1)}, bf16[8,32,128]{2,1,0:T(8,128)(2,1)S(1)}, bf16[8,32,128]{2...) custom-call(bf16[64,131072]{1,0:T(8,128)(2,1)} %refs_0_.3, ...), custom_call_target="tpu_custom_call" | custom-call | flops 536870912 | bytes 16777216 | tf_op jit(solution)/shard_map/first_products/pallas_call | solution.py:76
  22.1 2.1 %collective-permute-start = (bf16[8,32,128]{2,1,0:T(8,128)(2,1)S(1)}, bf16[8,32,128]{2,1,0:T(8,128)(2,1)S(1)}, u32[]{:S(2)}, u32[]{:S(2)}) collective-permute-start(bf16[8,32,128]{2,1,0:T(8,128)(2,1)S(1)} %get-tuple-element.21), channel_id=1, source_target_pairs={{0,4},{4,0},{8,12},{12,8},{16,20},{20,16},{24,28},{28,24},{1,5},{5... | collective-permute-start | bytes 196616 | tf_op jit(solution)/shard_map/ppermute | solution.py:348
  24.2 1.5 %collective-permute-start.1 = (bf16[8,32,128]{2,1,0:T(8,128)(2,1)S(1)}, bf16[8,32,128]{2,1,0:T(8,128)(2,1)S(1)}, u32[]{:S(2)}, u32[]{:S(2)}) collective-permute-start(bf16[8,32,128]{2,1,0:T(8,128)(2,1)S(1)} %get-tuple-element.22), channel_id=1, source_target_pairs={{0,8},{4,12},{8,0},{12,4},{16,24},{20,28},{24,16},{28,20},{1,9},{5... | collective-permute-start | bytes 196616 | tf_op jit(solution)/shard_map/ppermute | solution.py:348
  25.6 0.1 collective-permute-start.2
  25.7 2.8 %collective-permute-start.3 = (bf16[8,32,128]{2,1,0:T(8,128)(2,1)S(1)}, bf16[8,32,128]{2,1,0:T(8,128)(2,1)S(1)}, u32[]{:S(2)}, u32[]{:S(2)}) collective-permute-start(bf16[8,32,128]{2,1,0:T(8,128)(2,1)S(1)} %get-tuple-element.25), channel_id=1, source_target_pairs={{0,16},{4,20},{8,24},{12,28},{16,0},{20,4},{24,8},{28,12},{1,17},{... | collective-permute-start | bytes 196616 | tf_op jit(solution)/shard_map/ppermute | solution.py:348
  28.5 1.5 %collective-permute-start.4 = (bf16[8,32,128]{2,1,0:T(8,128)(2,1)S(1)}, bf16[8,32,128]{2,1,0:T(8,128)(2,1)S(1)}, u32[]{:S(2)}, u32[]{:S(2)}) collective-permute-start(bf16[8,32,128]{2,1,0:T(8,128)(2,1)S(1)} %get-tuple-element.26), channel_id=1, source_target_pairs={{0,20},{4,16},{8,28},{12,24},{16,4},{20,0},{24,12},{28,8},{1,21},{... | collective-permute-start | bytes 196616 | tf_op jit(solution)/shard_map/ppermute | solution.py:348
  30.0 0.0 collective-permute-done.refs_4_
  30.0 3.3 %collective-permute-start.5 = (bf16[8,32,128]{2,1,0:T(8,128)(2,1)S(1)}, bf16[8,32,128]{2,1,0:T(8,128)(2,1)S(1)}, u32[]{:S(2)}, u32[]{:S(2)}) collective-permute-start(bf16[8,32,128]{2,1,0:T(8,128)(2,1)S(1)} %get-tuple-element.27), channel_id=1, source_target_pairs={{0,24},{4,28},{8,16},{12,20},{16,8},{20,12},{24,0},{28,4},{1,25},{... | collective-permute-start | bytes 196616 | tf_op jit(solution)/shard_map/ppermute | solution.py:348
  33.3 0.0 collective-permute-done.1.refs_5_
  33.3 0.3 collective-permute-start.6
  33.5 0.0 copy-done
  33.5 0.6 turned_factor.1
  34.1 0.0 collective-permute-done.2.refs_6_
  34.2 0.0 all-to-all-done.refs_2_
  34.2 0.8 %early_products.1.early = f32[64,1024]{1,0:T(8,128)S(1)} custom-call(bf16[8,256,256]{2,1,0:T(8,128)(2,1)S(1)} %get-tuple-element.18.refs_0_, bf16[8,256,128]{2,1,0:T(8,128)(2,1)S(1)} %get-tuple-element.19.refs_1_, bf16[64,32,128]{2,1,0:T(8,128)(2,1)S(1)} %all-to-all-done.refs_2_, bf16[8,32,128]{2,1,0:T(8,128)(2,1)S(1)} %get-tuple-element.20.refs_3_, ...), custom_call_target="tpu_custom_call" | custom-call | tf_op jit(solution)/shard_map/early_products/pallas_call | solution.py:158
  34.9 0.0 collective-permute-done.3.refs_1_
  35.0 4.4 %collective-permute-done.4.refs_2_ = bf16[8,32,128]{2,1,0:T(8,128)(2,1)S(1)} collective-permute-done((bf16[8,32,128]{2,1,0:T(8,128)(2,1)S(1)}, bf16[8,32,128]{2,1,0:T(8,128)(2,1)S(1)}, u32[]{:S(2)}, u32[]{:S(2)}) %collective-permute-start.4) | collective-permute-done | bytes 65568 | tf_op jit(solution)/shard_map/ppermute | solution.py:348
  39.4 0.0 collective-permute-done.5.refs_3_
  39.4 1.0 %collective-permute-done.6.refs_4_ = bf16[8,32,128]{2,1,0:T(8,128)(2,1)S(1)} collective-permute-done((bf16[8,32,128]{2,1,0:T(8,128)(2,1)S(1)}, bf16[8,32,128]{2,1,0:T(8,128)(2,1)S(1)}, u32[]{:S(2)}, u32[]{:S(2)}) %collective-permute-start.6) | collective-permute-done | bytes 65568 | tf_op jit(solution)/shard_map/ppermute | solution.py:348
  40.3 0.0 copy-done.1
  40.3 1.4 %late_products.1 = (f32[64,1024]{1,0:T(8,128)S(1)}, f32[32,8,128]{2,1,0:T(8,128)S(1)}, f32[32,8,128]{2,1,0:T(8,128)S(1)}) custom-call(s32[8,8]{1,0:T(8,128)S(1)} %copy-done.1, f32[64,1024]{1,0:T(8,128)S(1)} %early_products.1.early, bf16[8,256,128]{2,1,0:T(8,128)(2,1)S(1)} %get-tuple-element.24.refs_0_, ...), custom_call_target="tpu_custom_call" | custom-call | tf_op jit(solution)/shard_map/late_products/pallas_call | solution.py:202
  41.7 0.1 collective-permute-start.7
  41.8 1.3 %collective-permute-done.7 = f32[32,8,128]{2,1,0:T(8,128)S(1)} collective-permute-done((f32[32,8,128]{2,1,0:T(8,128)S(1)}, f32[32,8,128]{2,1,0:T(8,128)S(1)}, u32[]{:S(2)}, u32[]{:S(2)}) %collective-permute-start.7) | collective-permute-done | bytes 131104 | tf_op jit(solution)/shard_map/ppermute | solution.py:348
  43.2 1.6 %collective-permute-start.9 = (f32[32,8,128]{2,1,0:T(8,128)S(1)}, f32[32,8,128]{2,1,0:T(8,128)S(1)}, u32[]{:S(2)}, u32[]{:S(2)}) collective-permute-start(f32[32,8,128]{2,1,0:T(8,128)S(1)} %add.3.mine), channel_id=1, source_target_pairs={{0,2},{1,3},{2,0},{3,1},{4,6},{5,7},{6,4},{7,5},{8,10},{9,11},{10,... | collective-permute-start | bytes 393224 | tf_op jit(solution)/shard_map/ppermute | solution.py:348
  44.7 0.0 collective-permute-start.8
  44.8 4.0 %collective-permute-done.9.center = f32[32,8,128]{2,1,0:T(8,128)S(1)} collective-permute-done((f32[32,8,128]{2,1,0:T(8,128)S(1)}, f32[32,8,128]{2,1,0:T(8,128)S(1)}, u32[]{:S(2)}, u32[]{:S(2)}) %collective-permute-start.9) | collective-permute-done | bytes 131104 | tf_op jit(solution)/shard_map/ppermute | solution.py:348
  48.8 0.0 collective-permute-start.10
  48.8 0.0 collective-permute-done.8.other
  48.8 3.6 %held_distances.1 = (f32[64,1024]{1,0:T(8,128)}, f32[64,128]{1,0:T(8,128)S(1)}) custom-call(s32[8,8]{1,0:T(8,128)S(1)} %copy-done.1, f32[64,1024]{1,0:T(8,128)S(1)} %get-tuple-element.29.sketch, f32[32,8,128]{2,1,0:T(8,128)S(1)} %add.3.mine, f32[32,8,128]{2,1,0:T(8,128)S(1)} %collective-permute-done.8.other), custom_call_target="tpu_custom_call" | custom-call | tf_op jit(solution)/shard_map/held_distances/pallas_call | solution.py:286
  52.4 2.2 %far_distances.2.before = f32[64,128]{1,0:T(8,128)S(1)} custom-call(s32[8,8]{1,0:T(8,128)S(1)} %copy-done.1, f32[64,1024]{1,0:T(8,128)S(1)} %get-tuple-element.29.sketch, f32[32,8,128]{2,1,0:T(8,128)S(1)} %collective-permute-done.9.center, f32[64,128]{1,0:T(8,128)S(1)} %get-tuple-element.33.before), custom_call_target="tpu_custom_call" | custom-call | tf_op jit(solution)/shard_map/far_distances/pallas_call | solution.py:307
  54.7 0.0 collective-permute-done.10.center
  54.7 2.1 %far_distances.3 = bf16[32,128]{1,0:T(8,128)(2,1)S(1)} custom-call(s32[8,8]{1,0:T(8,128)S(1)} %copy-done.1, f32[64,1024]{1,0:T(8,128)S(1)} %get-tuple-element.29.sketch, f32[32,8,128]{2,1,0:T(8,128)S(1)} %collective-permute-done.10.center, f32[64,128]{1,0:T(8,128)S(1)} %far_distances.2.before), custom_call_target="tpu_custom_call" | custom-call | tf_op jit(solution)/shard_map/far_distances/pallas_call | solution.py:307
  56.8 0.1 broadcast_in_dim.2
  56.9 10.2 %all_to_all.10.parts = bf16[8,32,128]{2,1,0:T(8,128)(2,1)S(1)} all-to-all(bf16[8,32,128]{2,1,0:T(8,128)(2,1)S(1)} %broadcast_in_dim.2), channel_id=1, replica_groups=mesh['feat'=8,'ex'=4] {'feat'}, dimensions={0} | all-to-all | bytes 131072 | tf_op jit(solution)/shard_map/all_to_all | solution.py:384
  67.1 0.7 %nearest.1 = f32[8,64]{1,0:T(8,128)} custom-call(bf16[8,32,128]{2,1,0:T(8,128)(2,1)S(1)} %all_to_all.10.parts), custom_call_target="tpu_custom_call" | custom-call | tf_op jit(solution)/shard_map/nearest/pallas_call | solution.py:337
  (1 shorter events, 0.0 us)
Async XLA Ops:
  8.0 26.1 %all-to-all-start = ((bf16[64,32,128]{2,1,0:T(8,128)(2,1)}), bf16[64,32,128]{2,1,0:T(8,128)(2,1)S(1)}, u32[]{:S(2)}, u32[]{:S(2)}) async-start(bf16[64,32,128]{2,1,0:T(8,128)(2,1)} %first_products.2), calls=%async_computation | async-start | bytes 1048576 | tf_op jit(solution)/shard_map/all_to_all | solution.py:362
  15.3 18.2 %copy-start = (bf16[8,1024,128]{2,1,0:T(8,128)(2,1)S(1)}, bf16[8,1024,128]{2,1,0:T(8,128)(2,1)}, u32[]{:S(2)}) copy-start(bf16[8,1024,128]{2,1,0:T(8,128)(2,1)} %second.1) | copy-start | bytes 6291460
  15.3 25.0 %copy-start.1 = (s32[8,8]{1,0:T(8,128)S(1)}, s32[8,8]{1,0:T(8,128)}, u32[]{:S(2)}) copy-start(s32[8,8]{1,0:T(8,128)} %picks.7) | copy-start | bytes 772
  22.1 7.9 %collective-permute-start = (bf16[8,32,128]{2,1,0:T(8,128)(2,1)S(1)}, bf16[8,32,128]{2,1,0:T(8,128)(2,1)S(1)}, u32[]{:S(2)}, u32[]{:S(2)}) collective-permute-start(bf16[8,32,128]{2,1,0:T(8,128)(2,1)S(1)} %get-tuple-element.21), channel_id=1, source_target_pairs={{0,4},{4,0},{8,12},{12,8},{16,20},{20,16},{24,28},{28,24},{1,5},{5... | collective-permute-start | bytes 196616 | tf_op jit(solution)/shard_map/ppermute | solution.py:348
  24.2 9.1 %collective-permute-start.1 = (bf16[8,32,128]{2,1,0:T(8,128)(2,1)S(1)}, bf16[8,32,128]{2,1,0:T(8,128)(2,1)S(1)}, u32[]{:S(2)}, u32[]{:S(2)}) collective-permute-start(bf16[8,32,128]{2,1,0:T(8,128)(2,1)S(1)} %get-tuple-element.22), channel_id=1, source_target_pairs={{0,8},{4,12},{8,0},{12,4},{16,24},{20,28},{24,16},{28,20},{1,9},{5... | collective-permute-start | bytes 196616 | tf_op jit(solution)/shard_map/ppermute | solution.py:348
  25.6 8.5 %collective-permute-start.2 = (bf16[8,32,128]{2,1,0:T(8,128)(2,1)S(1)}, bf16[8,32,128]{2,1,0:T(8,128)(2,1)S(1)}, u32[]{:S(2)}, u32[]{:S(2)}) collective-permute-start(bf16[8,32,128]{2,1,0:T(8,128)(2,1)S(1)} %get-tuple-element.23), channel_id=1, source_target_pairs={{0,12},{4,8},{8,4},{12,0},{16,28},{20,24},{24,20},{28,16},{1,13},{... | collective-permute-start | bytes 196616 | tf_op jit(solution)/shard_map/ppermute | solution.py:348
  25.7 9.3 %collective-permute-start.3 = (bf16[8,32,128]{2,1,0:T(8,128)(2,1)S(1)}, bf16[8,32,128]{2,1,0:T(8,128)(2,1)S(1)}, u32[]{:S(2)}, u32[]{:S(2)}) collective-permute-start(bf16[8,32,128]{2,1,0:T(8,128)(2,1)S(1)} %get-tuple-element.25), channel_id=1, source_target_pairs={{0,16},{4,20},{8,24},{12,28},{16,0},{20,4},{24,8},{28,12},{1,17},{... | collective-permute-start | bytes 196616 | tf_op jit(solution)/shard_map/ppermute | solution.py:348
  28.5 10.8 %collective-permute-start.4 = (bf16[8,32,128]{2,1,0:T(8,128)(2,1)S(1)}, bf16[8,32,128]{2,1,0:T(8,128)(2,1)S(1)}, u32[]{:S(2)}, u32[]{:S(2)}) collective-permute-start(bf16[8,32,128]{2,1,0:T(8,128)(2,1)S(1)} %get-tuple-element.26), channel_id=1, source_target_pairs={{0,20},{4,16},{8,28},{12,24},{16,4},{20,0},{24,12},{28,8},{1,21},{... | collective-permute-start | bytes 196616 | tf_op jit(solution)/shard_map/ppermute | solution.py:348
  30.0 9.4 %collective-permute-start.5 = (bf16[8,32,128]{2,1,0:T(8,128)(2,1)S(1)}, bf16[8,32,128]{2,1,0:T(8,128)(2,1)S(1)}, u32[]{:S(2)}, u32[]{:S(2)}) collective-permute-start(bf16[8,32,128]{2,1,0:T(8,128)(2,1)S(1)} %get-tuple-element.27), channel_id=1, source_target_pairs={{0,24},{4,28},{8,16},{12,20},{16,8},{20,12},{24,0},{28,4},{1,25},{... | collective-permute-start | bytes 196616 | tf_op jit(solution)/shard_map/ppermute | solution.py:348
  33.3 7.1 %collective-permute-start.6 = (bf16[8,32,128]{2,1,0:T(8,128)(2,1)S(1)}, bf16[8,32,128]{2,1,0:T(8,128)(2,1)S(1)}, u32[]{:S(2)}, u32[]{:S(2)}) collective-permute-start(bf16[8,32,128]{2,1,0:T(8,128)(2,1)S(1)} %get-tuple-element.28), channel_id=1, source_target_pairs={{0,28},{4,24},{8,20},{12,16},{16,12},{20,8},{24,4},{28,0},{1,29},{... | collective-permute-start | bytes 196616 | tf_op jit(solution)/shard_map/ppermute | solution.py:348
  41.7 1.4 %collective-permute-start.7 = (f32[32,8,128]{2,1,0:T(8,128)S(1)}, f32[32,8,128]{2,1,0:T(8,128)S(1)}, u32[]{:S(2)}, u32[]{:S(2)}) collective-permute-start(f32[32,8,128]{2,1,0:T(8,128)S(1)} %get-tuple-element.31), channel_id=1, source_target_pairs={{0,1},{1,0},{2,3},{3,2},{4,5},{5,4},{6,7},{7,6},{8,9},{9,8},{10,11... | collective-permute-start | bytes 393224 | tf_op jit(solution)/shard_map/ppermute | solution.py:348
  43.2 5.6 %collective-permute-start.9 = (f32[32,8,128]{2,1,0:T(8,128)S(1)}, f32[32,8,128]{2,1,0:T(8,128)S(1)}, u32[]{:S(2)}, u32[]{:S(2)}) collective-permute-start(f32[32,8,128]{2,1,0:T(8,128)S(1)} %add.3.mine), channel_id=1, source_target_pairs={{0,2},{1,3},{2,0},{3,1},{4,6},{5,7},{6,4},{7,5},{8,10},{9,11},{10,... | collective-permute-start | bytes 393224 | tf_op jit(solution)/shard_map/ppermute | solution.py:348
  44.7 4.0 %collective-permute-start.8 = (f32[32,8,128]{2,1,0:T(8,128)S(1)}, f32[32,8,128]{2,1,0:T(8,128)S(1)}, u32[]{:S(2)}, u32[]{:S(2)}) collective-permute-start(f32[32,8,128]{2,1,0:T(8,128)S(1)} %add.3.mine), channel_id=1, source_target_pairs={{0,1},{1,0},{2,3},{3,2},{4,5},{5,4},{6,7},{7,6},{8,9},{9,8},{10,11... | collective-permute-start | bytes 393224 | tf_op jit(solution)/shard_map/ppermute | solution.py:348
  48.8 5.9 %collective-permute-start.10 = (f32[32,8,128]{2,1,0:T(8,128)S(1)}, f32[32,8,128]{2,1,0:T(8,128)S(1)}, u32[]{:S(2)}, u32[]{:S(2)}) collective-permute-start(f32[32,8,128]{2,1,0:T(8,128)S(1)} %collective-permute-done.9.center), channel_id=1, source_target_pairs={{0,1},{1,0},{2,3},{3,2},{4,5},{5,4},{6,7},{7,6},{8,9},{9,8},{10,11... | collective-permute-start | bytes 393224 | tf_op jit(solution)/shard_map/ppermute | solution.py:348

commit v5 on v3

--- a/solution.py
+++ b/solution.py
@@ -222,22 +222,16 @@
     count, _, width = center.shape
     center[...] = first[...] + second[...]
     lane = lax.broadcasted_iota(jnp.int32, (8, 128), 1)
-
-    def some(i, sums):
-        sums = list(sums)
+    sums = [jnp.zeros((8, 128), F32)] * (rows // 8)
+    for p in range(0, count, unroll):
         for g in range(rows // 8):
             block = [sketch[g * 8 : (g + 1) * 8, t * width : (t + 1) * width] for t in range(dims // width)]
             for u in range(unroll):
-                p = i * unroll + u
                 acc = None
                 for t, own in enumerate(block):
-                    diff = own - center[p, t : t + 1, :]
+                    diff = own - center[p + u, t : t + 1, :]
                     acc = diff * diff if acc is None else acc + diff * diff
-                sums[g] = jnp.where(lane == p, jnp.sum(acc, axis=1, keepdims=True), sums[g])
-        return tuple(sums)
-
-    zeros = tuple(jnp.zeros((8, 128), F32) for _ in range(rows // 8))
-    sums = lax.fori_loop(0, count // unroll, some, zeros)
+                sums[g] = jnp.where(lane == p + u, jnp.sum(acc, axis=1, keepdims=True), sums[g])
     by_pick = jnp.concatenate(sums, axis=0).T[:count]
     if before is not None:
         by_pick = jnp.concatenate([before[...], by_pick], axis=1)

time: 63.1 us -> 62.4 us (0.989)
  Pallas kernels: 20.7 us -> 19.7 us
  transfers between devices with their start and end apart: 12 -> 12, of which waited for: 4 -> 5; matrix products, arithmetic and copies ran while one was open for 0% -> 0% of each run, Pallas kernels for 15% -> 15%
where the time goes in v5:
time: 62.4 us; the launch traced here: 62.1 us
  starting transfers between devices  20.4 us (33%)
  Pallas kernels  19.7 us (32%)
  waiting for transfers between devices  11.1 us (18%)
  blocking collectives  10.2 us (16%)
  between operations  0.74 us (1%)
    pallas_call x2, Pallas kernels, first_products(): pl.pallas_call(functools.partial(first_kernel, feat, start, half, step, f...  14.2 us
    ppermute x11, starting transfers between devices, swap(): return lax.ppermute(x, axis, [(i, i ^ step) for i in range(size)])  13.1 us
    ppermute x11, waiting for transfers between devices, swap(): return lax.ppermute(x, axis, [(i, i ^ step) for i in range(size)])  11.1 us
    all_to_all x1, blocking collectives, per_device(): lax.all_to_all(spread, 'feat', split_axis=0, concat_axis=0, tiled=True)  10.2 us
    all_to_all x1, starting transfers between devices, per_device(): lax.all_to_all(inner, 'feat', split_axis=0, concat_axis=0, tiled=True)  7.27 us
    pallas_call x1, Pallas kernels, late_products(): pl.pallas_call(functools.partial(late_kernel, counts), in_specs=[smem] +...  1.36 us
  transfers between devices with their start and end apart: 12, of which 5 were waited for; matrix products, arithmetic and copies ran while one was open for 0% of the time, Pallas kernels for 15%

profile of v5, /device:TPU:0, one launch (start us, length us, event | category | flops | bytes accessed | tf_op | source)
XLA Modules:
  0.0 62.1 jit_solution(10531145995736919524)
XLA Ops:
  0.6 7.4 %first_products.2 = bf16[64,32,128]{2,1,0:T(8,128)(2,1)} custom-call(bf16[64,131072]{1,0:T(8,128)(2,1)} %refs_0_.3, bf16[128,64,1024]{2,1,0:T(8,128)(2,1)} %bitcast.1), custom_call_target="tpu_custom_call" | custom-call | flops 536870912 | bytes 16777216 | tf_op jit(solution)/shard_map/first_products/pallas_call | solution.py:75
  8.0 7.3 %all-to-all-start = ((bf16[64,32,128]{2,1,0:T(8,128)(2,1)}), bf16[64,32,128]{2,1,0:T(8,128)(2,1)S(1)}, u32[]{:S(2)}, u32[]{:S(2)}) async-start(bf16[64,32,128]{2,1,0:T(8,128)(2,1)} %first_products.2), calls=%async_computation | async-start | bytes 1048576 | tf_op jit(solution)/shard_map/all_to_all | solution.py:313
  15.3 0.0 copy-start
  15.3 0.0 copy-start.1
  15.3 6.7 %first_products.3 = (bf16[8,32,128]{2,1,0:T(8,128)(2,1)S(1)}, bf16[8,32,128]{2,1,0:T(8,128)(2,1)S(1)}, bf16[8,32,128]{2,1,0:T(8,128)(2,1)S(1)}, bf16[8,32,128]{2...) custom-call(bf16[64,131072]{1,0:T(8,128)(2,1)} %refs_0_.3, ...), custom_call_target="tpu_custom_call" | custom-call | flops 536870912 | bytes 16777216 | tf_op jit(solution)/shard_map/first_products/pallas_call | solution.py:75
  22.1 2.1 %collective-permute-start = (bf16[8,32,128]{2,1,0:T(8,128)(2,1)S(1)}, bf16[8,32,128]{2,1,0:T(8,128)(2,1)S(1)}, u32[]{:S(2)}, u32[]{:S(2)}) collective-permute-start(bf16[8,32,128]{2,1,0:T(8,128)(2,1)S(1)} %get-tuple-element.21), channel_id=1, source_target_pairs={{0,4},{4,0},{8,12},{12,8},{16,20},{20,16},{24,28},{28,24},{1,5},{5... | collective-permute-start | bytes 196616 | tf_op jit(solution)/shard_map/ppermute | solution.py:299
  24.2 1.5 %collective-permute-start.1 = (bf16[8,32,128]{2,1,0:T(8,128)(2,1)S(1)}, bf16[8,32,128]{2,1,0:T(8,128)(2,1)S(1)}, u32[]{:S(2)}, u32[]{:S(2)}) collective-permute-start(bf16[8,32,128]{2,1,0:T(8,128)(2,1)S(1)} %get-tuple-element.22), channel_id=1, source_target_pairs={{0,8},{4,12},{8,0},{12,4},{16,24},{20,28},{24,16},{28,20},{1,9},{5... | collective-permute-start | bytes 196616 | tf_op jit(solution)/shard_map/ppermute | solution.py:299
  25.6 0.1 collective-permute-start.2
  25.7 2.8 %collective-permute-start.3 = (bf16[8,32,128]{2,1,0:T(8,128)(2,1)S(1)}, bf16[8,32,128]{2,1,0:T(8,128)(2,1)S(1)}, u32[]{:S(2)}, u32[]{:S(2)}) collective-permute-start(bf16[8,32,128]{2,1,0:T(8,128)(2,1)S(1)} %get-tuple-element.25), channel_id=1, source_target_pairs={{0,16},{4,20},{8,24},{12,28},{16,0},{20,4},{24,8},{28,12},{1,17},{... | collective-permute-start | bytes 196616 | tf_op jit(solution)/shard_map/ppermute | solution.py:299
  28.5 1.5 %collective-permute-start.4 = (bf16[8,32,128]{2,1,0:T(8,128)(2,1)S(1)}, bf16[8,32,128]{2,1,0:T(8,128)(2,1)S(1)}, u32[]{:S(2)}, u32[]{:S(2)}) collective-permute-start(bf16[8,32,128]{2,1,0:T(8,128)(2,1)S(1)} %get-tuple-element.26), channel_id=1, source_target_pairs={{0,20},{4,16},{8,28},{12,24},{16,4},{20,0},{24,12},{28,8},{1,21},{... | collective-permute-start | bytes 196616 | tf_op jit(solution)/shard_map/ppermute | solution.py:299
  30.0 0.0 collective-permute-done.refs_4_
  30.0 3.3 %collective-permute-start.5 = (bf16[8,32,128]{2,1,0:T(8,128)(2,1)S(1)}, bf16[8,32,128]{2,1,0:T(8,128)(2,1)S(1)}, u32[]{:S(2)}, u32[]{:S(2)}) collective-permute-start(bf16[8,32,128]{2,1,0:T(8,128)(2,1)S(1)} %get-tuple-element.27), channel_id=1, source_target_pairs={{0,24},{4,28},{8,16},{12,20},{16,8},{20,12},{24,0},{28,4},{1,25},{... | collective-permute-start | bytes 196616 | tf_op jit(solution)/shard_map/ppermute | solution.py:299
  33.3 0.0 collective-permute-done.1.refs_5_
  33.3 0.3 collective-permute-start.6
  33.5 0.0 copy-done
  33.5 0.6 turned_factor.1
  34.1 0.0 collective-permute-done.2.refs_6_
  34.2 0.0 all-to-all-done.refs_2_
  34.2 0.8 %early_products.1.early = f32[64,1024]{1,0:T(8,128)S(1)} custom-call(bf16[8,256,256]{2,1,0:T(8,128)(2,1)S(1)} %get-tuple-element.18.refs_0_, bf16[8,256,128]{2,1,0:T(8,128)(2,1)S(1)} %get-tuple-element.19.refs_1_, bf16[64,32,128]{2,1,0:T(8,128)(2,1)S(1)} %all-to-all-done.refs_2_, bf16[8,32,128]{2,1,0:T(8,128)(2,1)S(1)} %get-tuple-element.20.refs_3_, ...), custom_call_target="tpu_custom_call" | custom-call | tf_op jit(solution)/shard_map/early_products/pallas_call | solution.py:157
  34.9 0.0 collective-permute-done.3.refs_1_
  34.9 4.4 %collective-permute-done.4.refs_2_ = bf16[8,32,128]{2,1,0:T(8,128)(2,1)S(1)} collective-permute-done((bf16[8,32,128]{2,1,0:T(8,128)(2,1)S(1)}, bf16[8,32,128]{2,1,0:T(8,128)(2,1)S(1)}, u32[]{:S(2)}, u32[]{:S(2)}) %collective-permute-start.4) | collective-permute-done | bytes 65568 | tf_op jit(solution)/shard_map/ppermute | solution.py:299
  39.4 0.0 collective-permute-done.5.refs_3_
  39.4 1.0 %collective-permute-done.6.refs_4_ = bf16[8,32,128]{2,1,0:T(8,128)(2,1)S(1)} collective-permute-done((bf16[8,32,128]{2,1,0:T(8,128)(2,1)S(1)}, bf16[8,32,128]{2,1,0:T(8,128)(2,1)S(1)}, u32[]{:S(2)}, u32[]{:S(2)}) %collective-permute-start.6) | collective-permute-done | bytes 65568 | tf_op jit(solution)/shard_map/ppermute | solution.py:299
  40.3 0.0 copy-done.1
  40.3 1.4 %late_products.1 = (f32[64,1024]{1,0:T(8,128)S(1)}, f32[32,8,128]{2,1,0:T(8,128)S(1)}, f32[32,8,128]{2,1,0:T(8,128)S(1)}) custom-call(s32[8,8]{1,0:T(8,128)S(1)} %copy-done.1, f32[64,1024]{1,0:T(8,128)S(1)} %early_products.1.early, bf16[8,256,128]{2,1,0:T(8,128)(2,1)S(1)} %get-tuple-element.24.refs_0_, ...), custom_call_target="tpu_custom_call" | custom-call | tf_op jit(solution)/shard_map/late_products/pallas_call | solution.py:201
  41.7 0.1 collective-permute-start.7
  41.8 1.3 %collective-permute-done.7 = f32[32,8,128]{2,1,0:T(8,128)S(1)} collective-permute-done((f32[32,8,128]{2,1,0:T(8,128)S(1)}, f32[32,8,128]{2,1,0:T(8,128)S(1)}, u32[]{:S(2)}, u32[]{:S(2)}) %collective-permute-start.7) | collective-permute-done | bytes 131104 | tf_op jit(solution)/shard_map/ppermute | solution.py:299
  43.2 1.6 %collective-permute-start.8 = (f32[32,8,128]{2,1,0:T(8,128)S(1)}, f32[32,8,128]{2,1,0:T(8,128)S(1)}, u32[]{:S(2)}, u32[]{:S(2)}) collective-permute-start(f32[32,8,128]{2,1,0:T(8,128)S(1)} %add.3.first), channel_id=1, source_target_pairs={{0,2},{1,3},{2,0},{3,1},{4,6},{5,7},{6,4},{7,5},{8,10},{9,11},{10,... | collective-permute-start | bytes 393224 | tf_op jit(solution)/shard_map/ppermute | solution.py:299
  44.7 0.0 collective-permute-start.9
  44.7 4.0 %collective-permute-done.8.second = f32[32,8,128]{2,1,0:T(8,128)S(1)} collective-permute-done((f32[32,8,128]{2,1,0:T(8,128)S(1)}, f32[32,8,128]{2,1,0:T(8,128)S(1)}, u32[]{:S(2)}, u32[]{:S(2)}) %collective-permute-start.8) | collective-permute-done | bytes 131104 | tf_op jit(solution)/shard_map/ppermute | solution.py:299
  48.8 0.0 collective-permute-start.10
  48.8 1.0 %distances.2 = (f32[64,1024]{1,0:T(8,128)}, f32[32,64]{1,0:T(8,128)S(1)}) custom-call(f32[64,1024]{1,0:T(8,128)S(1)} %get-tuple-element.29.sketch, f32[32,8,128]{2,1,0:T(8,128)S(1)} %add.3.first, f32[32,8,128]{2,1,0:T(8,128)S(1)} %collective-permute-done.8.second), custom_call_target="tpu_custom_call" | custom-call | tf_op jit(solution)/shard_map/distances/pallas_call | solution.py:249
  49.8 0.0 collective-permute-done.9.first
  49.8 0.3 collective-permute-done.10.second
  50.1 1.1 %distances.3 = bf16[32,128]{1,0:T(8,128)(2,1)S(1)} custom-call(f32[64,1024]{1,0:T(8,128)S(1)} %get-tuple-element.29.sketch, f32[32,8,128]{2,1,0:T(8,128)S(1)} %collective-permute-done.9.first, f32[32,8,128]{2,1,0:T(8,128)S(1)} %collective-permute-done.10.second, f32[32,64]{1,0:T(8,128)S(1)} %get-tuple-element.33.refs_0_), custom_call_target="tpu_custom_call" | custom-call | tf_op jit(solution)/shard_map/distances/pallas_call | solution.py:258
  51.2 10.2 %all_to_all.10.parts = bf16[8,32,128]{2,1,0:T(8,128)(2,1)S(1)} all-to-all(bf16[8,32,128]{2,1,0:T(8,128)(2,1)S(1)} %broadcast_in_dim.2), channel_id=1, replica_groups=mesh['feat'=8,'ex'=4] {'feat'}, dimensions={0} | all-to-all | bytes 131072 | tf_op jit(solution)/shard_map/all_to_all | solution.py:335
  61.5 0.7 %nearest.1 = f32[8,64]{1,0:T(8,128)} custom-call(bf16[8,32,128]{2,1,0:T(8,128)(2,1)S(1)} %all_to_all.10.parts), custom_call_target="tpu_custom_call" | custom-call | tf_op jit(solution)/shard_map/nearest/pallas_call | solution.py:288
  (2 shorter events, 0.0 us)
Async XLA Ops:
  8.0 26.1 %all-to-all-start = ((bf16[64,32,128]{2,1,0:T(8,128)(2,1)}), bf16[64,32,128]{2,1,0:T(8,128)(2,1)S(1)}, u32[]{:S(2)}, u32[]{:S(2)}) async-start(bf16[64,32,128]{2,1,0:T(8,128)(2,1)} %first_products.2), calls=%async_computation | async-start | bytes 1048576 | tf_op jit(solution)/shard_map/all_to_all | solution.py:313
  15.3 18.2 %copy-start = (bf16[8,1024,128]{2,1,0:T(8,128)(2,1)S(1)}, bf16[8,1024,128]{2,1,0:T(8,128)(2,1)}, u32[]{:S(2)}) copy-start(bf16[8,1024,128]{2,1,0:T(8,128)(2,1)} %second.1) | copy-start | bytes 6291460
  15.3 25.0 %copy-start.1 = (s32[8,8]{1,0:T(8,128)S(1)}, s32[8,8]{1,0:T(8,128)}, u32[]{:S(2)}) copy-start(s32[8,8]{1,0:T(8,128)} %picks.1) | copy-start | bytes 772
  22.1 7.9 %collective-permute-start = (bf16[8,32,128]{2,1,0:T(8,128)(2,1)S(1)}, bf16[8,32,128]{2,1,0:T(8,128)(2,1)S(1)}, u32[]{:S(2)}, u32[]{:S(2)}) collective-permute-start(bf16[8,32,128]{2,1,0:T(8,128)(2,1)S(1)} %get-tuple-element.21), channel_id=1, source_target_pairs={{0,4},{4,0},{8,12},{12,8},{16,20},{20,16},{24,28},{28,24},{1,5},{5... | collective-permute-start | bytes 196616 | tf_op jit(solution)/shard_map/ppermute | solution.py:299
  24.2 9.1 %collective-permute-start.1 = (bf16[8,32,128]{2,1,0:T(8,128)(2,1)S(1)}, bf16[8,32,128]{2,1,0:T(8,128)(2,1)S(1)}, u32[]{:S(2)}, u32[]{:S(2)}) collective-permute-start(bf16[8,32,128]{2,1,0:T(8,128)(2,1)S(1)} %get-tuple-element.22), channel_id=1, source_target_pairs={{0,8},{4,12},{8,0},{12,4},{16,24},{20,28},{24,16},{28,20},{1,9},{5... | collective-permute-start | bytes 196616 | tf_op jit(solution)/shard_map/ppermute | solution.py:299
  25.6 8.5 %collective-permute-start.2 = (bf16[8,32,128]{2,1,0:T(8,128)(2,1)S(1)}, bf16[8,32,128]{2,1,0:T(8,128)(2,1)S(1)}, u32[]{:S(2)}, u32[]{:S(2)}) collective-permute-start(bf16[8,32,128]{2,1,0:T(8,128)(2,1)S(1)} %get-tuple-element.23), channel_id=1, source_target_pairs={{0,12},{4,8},{8,4},{12,0},{16,28},{20,24},{24,20},{28,16},{1,13},{... | collective-permute-start | bytes 196616 | tf_op jit(solution)/shard_map/ppermute | solution.py:299
  25.7 9.2 %collective-permute-start.3 = (bf16[8,32,128]{2,1,0:T(8,128)(2,1)S(1)}, bf16[8,32,128]{2,1,0:T(8,128)(2,1)S(1)}, u32[]{:S(2)}, u32[]{:S(2)}) collective-permute-start(bf16[8,32,128]{2,1,0:T(8,128)(2,1)S(1)} %get-tuple-element.25), channel_id=1, source_target_pairs={{0,16},{4,20},{8,24},{12,28},{16,0},{20,4},{24,8},{28,12},{1,17},{... | collective-permute-start | bytes 196616 | tf_op jit(solution)/shard_map/ppermute | solution.py:299
  28.5 10.8 %collective-permute-start.4 = (bf16[8,32,128]{2,1,0:T(8,128)(2,1)S(1)}, bf16[8,32,128]{2,1,0:T(8,128)(2,1)S(1)}, u32[]{:S(2)}, u32[]{:S(2)}) collective-permute-start(bf16[8,32,128]{2,1,0:T(8,128)(2,1)S(1)} %get-tuple-element.26), channel_id=1, source_target_pairs={{0,20},{4,16},{8,28},{12,24},{16,4},{20,0},{24,12},{28,8},{1,21},{... | collective-permute-start | bytes 196616 | tf_op jit(solution)/shard_map/ppermute | solution.py:299
  30.0 9.4 %collective-permute-start.5 = (bf16[8,32,128]{2,1,0:T(8,128)(2,1)S(1)}, bf16[8,32,128]{2,1,0:T(8,128)(2,1)S(1)}, u32[]{:S(2)}, u32[]{:S(2)}) collective-permute-start(bf16[8,32,128]{2,1,0:T(8,128)(2,1)S(1)} %get-tuple-element.27), channel_id=1, source_target_pairs={{0,24},{4,28},{8,16},{12,20},{16,8},{20,12},{24,0},{28,4},{1,25},{... | collective-permute-start | bytes 196616 | tf_op jit(solution)/shard_map/ppermute | solution.py:299
  33.3 7.1 %collective-permute-start.6 = (bf16[8,32,128]{2,1,0:T(8,128)(2,1)S(1)}, bf16[8,32,128]{2,1,0:T(8,128)(2,1)S(1)}, u32[]{:S(2)}, u32[]{:S(2)}) collective-permute-start(bf16[8,32,128]{2,1,0:T(8,128)(2,1)S(1)} %get-tuple-element.28), channel_id=1, source_target_pairs={{0,28},{4,24},{8,20},{12,16},{16,12},{20,8},{24,4},{28,0},{1,29},{... | collective-permute-start | bytes 196616 | tf_op jit(solution)/shard_map/ppermute | solution.py:299
  41.7 1.4 %collective-permute-start.7 = (f32[32,8,128]{2,1,0:T(8,128)S(1)}, f32[32,8,128]{2,1,0:T(8,128)S(1)}, u32[]{:S(2)}, u32[]{:S(2)}) collective-permute-start(f32[32,8,128]{2,1,0:T(8,128)S(1)} %get-tuple-element.31), channel_id=1, source_target_pairs={{0,1},{1,0},{2,3},{3,2},{4,5},{5,4},{6,7},{7,6},{8,9},{9,8},{10,11... | collective-permute-start | bytes 393224 | tf_op jit(solution)/shard_map/ppermute | solution.py:299
  43.2 5.6 %collective-permute-start.8 = (f32[32,8,128]{2,1,0:T(8,128)S(1)}, f32[32,8,128]{2,1,0:T(8,128)S(1)}, u32[]{:S(2)}, u32[]{:S(2)}) collective-permute-start(f32[32,8,128]{2,1,0:T(8,128)S(1)} %add.3.first), channel_id=1, source_target_pairs={{0,2},{1,3},{2,0},{3,1},{4,6},{5,7},{6,4},{7,5},{8,10},{9,11},{10,... | collective-permute-start | bytes 393224 | tf_op jit(solution)/shard_map/ppermute | solution.py:299
  44.7 5.1 %collective-permute-start.9 = (f32[32,8,128]{2,1,0:T(8,128)S(1)}, f32[32,8,128]{2,1,0:T(8,128)S(1)}, u32[]{:S(2)}, u32[]{:S(2)}) collective-permute-start(f32[32,8,128]{2,1,0:T(8,128)S(1)} %add.3.first), channel_id=1, source_target_pairs={{0,1},{1,0},{2,3},{3,2},{4,5},{5,4},{6,7},{7,6},{8,9},{9,8},{10,11... | collective-permute-start | bytes 393224 | tf_op jit(solution)/shard_map/ppermute | solution.py:299
  48.8 1.3 %collective-permute-start.10 = (f32[32,8,128]{2,1,0:T(8,128)S(1)}, f32[32,8,128]{2,1,0:T(8,128)S(1)}, u32[]{:S(2)}, u32[]{:S(2)}) collective-permute-start(f32[32,8,128]{2,1,0:T(8,128)S(1)} %collective-permute-done.8.second), channel_id=1, source_target_pairs={{0,1},{1,0},{2,3},{3,2},{4,5},{5,4},{6,7},{7,6},{8,9},{9,8},{10,11... | collective-permute-start | bytes 393224 | tf_op jit(solution)/shard_map/ppermute | solution.py:299

commit v6 on v5

--- a/solution.py
+++ b/solution.py
@@ -106,7 +106,8 @@
                     else:
                         at = source * local + start + h * half
                     rows.append(second[k, pl.ds(at, half), :])
-                out[k, h * width : (h + 1) * width, :] = jnp.concatenate(rows, axis=0).T
+                depth = out.shape[2] // 2
+                out[k, :, h * depth : (h + 1) * depth] = jnp.concatenate(rows, axis=0).T
 
 
 def turned(second, local, plan):
@@ -117,7 +118,7 @@
         in_specs=[vmem],
         out_specs=[vmem] * len(plan),
         out_shape=[
-            jax.ShapeDtypeStruct((groups, 2 * width, sum(span[-1] for span in spans)), BF16) for spans in plan
+            jax.ShapeDtypeStruct((groups, width, 2 * sum(span[-1] for span in spans)), BF16) for spans in plan
         ],
         compiler_params=params(),
         name="turned_factor",
@@ -129,10 +130,10 @@
     for a, own in zip(factors, pieces):
         groups = a.shape[0]
         right = jnp.concatenate([x[at + k] for x in own for at in range(0, x.shape[0], groups)], axis=0)
+        right = jnp.concatenate([right[:, :rows], right[:, rows:]], axis=0)
         part = lax.dot_general(a[k], right, NN, preferred_element_type=F32)
         total = part if total is None else total + part
-    width = total.shape[0] // 2
-    return (total[:width, :rows] + total[width:, rows:]).T
+    return total.T
 
 
 def split_refs(counts, refs):
@@ -144,21 +145,20 @@
 
 def early_kernel(counts, *refs):
     factors, pieces, (out,) = split_refs(counts, refs)
-    groups, both, _ = factors[0].shape
-    width = both // 2
+    groups, width, _ = factors[0].shape
     for k in range(groups):
         out[:, k * width : (k + 1) * width] = products(k, factors, pieces, out.shape[0])
 
 
 def early_products(factors, pieces, rows):
-    groups, both, _ = factors[0].shape
+    groups, width, _ = factors[0].shape
     vmem = pl.BlockSpec(memory_space=pltpu.VMEM)
     counts = [len(own) for own in pieces]
     return pl.pallas_call(
         functools.partial(early_kernel, counts),
         in_specs=[vmem] * (len(counts) + sum(counts)),
         out_specs=vmem,
-        out_shape=jax.ShapeDtypeStruct((rows, groups * both // 2), F32),
+        out_shape=jax.ShapeDtypeStruct((rows, groups * width), F32),
         compiler_params=params(),
         name="early_products",
     )(*factors, *[x for own in pieces for x in own])
@@ -166,8 +166,8 @@
 
 def late_kernel(counts, picks, early, *refs):
     factors, pieces, (sketch, mine, other, held) = split_refs(counts, refs)
-    groups, both, _ = factors[0].shape
-    width, rows = both // 2, sketch.shape[0]
+    groups, width, _ = factors[0].shape
+    rows = sketch.shape[0]
     slots = mine.shape[1]
     if groups < slots:
         held[...] = jnp.zeros_like(held)
@@ -191,8 +191,7 @@
 
 def late_products(picks, early, factors, pieces):
     rows = early.shape[0]
-    groups, both, _ = factors[0].shape
-    width = both // 2
+    groups, width, _ = factors[0].shape
     slots = -(-groups // 8) * 8
     smem = pl.BlockSpec(memory_space=pltpu.SMEM)
     vmem = pl.BlockSpec(memory_space=pltpu.VMEM)

time: 62.4 us -> 62.3 us (level)
  no operation moved by 1% of the time
where the time goes in v6:
time: 62.3 us; the launch traced here: 62 us
  starting transfers between devices  20.4 us (33%)
  Pallas kernels  19.5 us (31%)
  waiting for transfers between devices  11.2 us (18%)
  blocking collectives  10.2 us (16%)
  between operations  0.73 us (1%)
    pallas_call x2, Pallas kernels, first_products(): pl.pallas_call(functools.partial(first_kernel, feat, start, half, step, f...  14.2 us
    ppermute x11, starting transfers between devices, swap(): return lax.ppermute(x, axis, [(i, i ^ step) for i in range(size)])  13.1 us
    ppermute x11, waiting for transfers between devices, swap(): return lax.ppermute(x, axis, [(i, i ^ step) for i in range(size)])  11.2 us
    all_to_all x1, blocking collectives, per_device(): lax.all_to_all(spread, 'feat', split_axis=0, concat_axis=0, tiled=True)  10.2 us
    all_to_all x1, starting transfers between devices, per_device(): lax.all_to_all(inner, 'feat', split_axis=0, concat_axis=0, tiled=True)  7.27 us
  transfers between devices with their start and end apart: 12, of which 5 were waited for; matrix products, arithmetic and copies ran while one was open for 0% of the time, Pallas kernels for 15%

profile of v6, /device:TPU:0, one launch (start us, length us, event | category | flops | bytes accessed | tf_op | source)
XLA Modules:
  0.0 62.0 jit_solution(11658578522604248488)
XLA Ops:
  0.6 7.4 %first_products.2 = bf16[64,32,128]{2,1,0:T(8,128)(2,1)} custom-call(bf16[64,131072]{1,0:T(8,128)(2,1)} %refs_0_.3, bf16[128,64,1024]{2,1,0:T(8,128)(2,1)} %bitcast.1), custom_call_target="tpu_custom_call" | custom-call | flops 536870912 | bytes 16777216 | tf_op jit(solution)/shard_map/first_products/pallas_call | solution.py:75
  8.0 7.3 %all-to-all-start = ((bf16[64,32,128]{2,1,0:T(8,128)(2,1)}), bf16[64,32,128]{2,1,0:T(8,128)(2,1)S(1)}, u32[]{:S(2)}, u32[]{:S(2)}) async-start(bf16[64,32,128]{2,1,0:T(8,128)(2,1)} %first_products.2), calls=%async_computation | async-start | bytes 1048576 | tf_op jit(solution)/shard_map/all_to_all | solution.py:312
  15.3 0.0 copy-start
  15.3 0.0 copy-start.1
  15.3 6.7 %first_products.3 = (bf16[8,32,128]{2,1,0:T(8,128)(2,1)S(1)}, bf16[8,32,128]{2,1,0:T(8,128)(2,1)S(1)}, bf16[8,32,128]{2,1,0:T(8,128)(2,1)S(1)}, bf16[8,32,128]{2...) custom-call(bf16[64,131072]{1,0:T(8,128)(2,1)} %refs_0_.3, ...), custom_call_target="tpu_custom_call" | custom-call | flops 536870912 | bytes 16777216 | tf_op jit(solution)/shard_map/first_products/pallas_call | solution.py:75
  22.1 2.1 %collective-permute-start = (bf16[8,32,128]{2,1,0:T(8,128)(2,1)S(1)}, bf16[8,32,128]{2,1,0:T(8,128)(2,1)S(1)}, u32[]{:S(2)}, u32[]{:S(2)}) collective-permute-start(bf16[8,32,128]{2,1,0:T(8,128)(2,1)S(1)} %get-tuple-element.21), channel_id=1, source_target_pairs={{0,4},{4,0},{8,12},{12,8},{16,20},{20,16},{24,28},{28,24},{1,5},{5... | collective-permute-start | bytes 196616 | tf_op jit(solution)/shard_map/ppermute | solution.py:298
  24.2 1.5 %collective-permute-start.1 = (bf16[8,32,128]{2,1,0:T(8,128)(2,1)S(1)}, bf16[8,32,128]{2,1,0:T(8,128)(2,1)S(1)}, u32[]{:S(2)}, u32[]{:S(2)}) collective-permute-start(bf16[8,32,128]{2,1,0:T(8,128)(2,1)S(1)} %get-tuple-element.22), channel_id=1, source_target_pairs={{0,8},{4,12},{8,0},{12,4},{16,24},{20,28},{24,16},{28,20},{1,9},{5... | collective-permute-start | bytes 196616 | tf_op jit(solution)/shard_map/ppermute | solution.py:298
  25.6 0.1 collective-permute-start.2
  25.7 2.8 %collective-permute-start.3 = (bf16[8,32,128]{2,1,0:T(8,128)(2,1)S(1)}, bf16[8,32,128]{2,1,0:T(8,128)(2,1)S(1)}, u32[]{:S(2)}, u32[]{:S(2)}) collective-permute-start(bf16[8,32,128]{2,1,0:T(8,128)(2,1)S(1)} %get-tuple-element.25), channel_id=1, source_target_pairs={{0,16},{4,20},{8,24},{12,28},{16,0},{20,4},{24,8},{28,12},{1,17},{... | collective-permute-start | bytes 196616 | tf_op jit(solution)/shard_map/ppermute | solution.py:298
  28.5 1.5 %collective-permute-start.4 = (bf16[8,32,128]{2,1,0:T(8,128)(2,1)S(1)}, bf16[8,32,128]{2,1,0:T(8,128)(2,1)S(1)}, u32[]{:S(2)}, u32[]{:S(2)}) collective-permute-start(bf16[8,32,128]{2,1,0:T(8,128)(2,1)S(1)} %get-tuple-element.26), channel_id=1, source_target_pairs={{0,20},{4,16},{8,28},{12,24},{16,4},{20,0},{24,12},{28,8},{1,21},{... | collective-permute-start | bytes 196616 | tf_op jit(solution)/shard_map/ppermute | solution.py:298
  30.0 0.0 collective-permute-done.refs_4_
  30.0 3.3 %collective-permute-start.5 = (bf16[8,32,128]{2,1,0:T(8,128)(2,1)S(1)}, bf16[8,32,128]{2,1,0:T(8,128)(2,1)S(1)}, u32[]{:S(2)}, u32[]{:S(2)}) collective-permute-start(bf16[8,32,128]{2,1,0:T(8,128)(2,1)S(1)} %get-tuple-element.27), channel_id=1, source_target_pairs={{0,24},{4,28},{8,16},{12,20},{16,8},{20,12},{24,0},{28,4},{1,25},{... | collective-permute-start | bytes 196616 | tf_op jit(solution)/shard_map/ppermute | solution.py:298
  33.3 0.0 collective-permute-done.1.refs_5_
  33.3 0.3 collective-permute-start.6
  33.5 0.0 copy-done
  33.5 0.6 turned_factor.1
  34.1 0.0 collective-permute-done.2.refs_6_
  34.2 0.0 all-to-all-done.refs_2_
  34.2 0.7 %early_products.1.early = f32[64,1024]{1,0:T(8,128)S(1)} custom-call(bf16[8,128,512]{2,1,0:T(8,128)(2,1)S(1)} %get-tuple-element.18.refs_0_, bf16[8,128,256]{2,1,0:T(8,128)(2,1)S(1)} %get-tuple-element.19.refs_1_, bf16[64,32,128]{2,1,0:T(8,128)(2,1)S(1)} %all-to-all-done.refs_2_, bf16[8,32,128]{2,1,0:T(8,128)(2,1)S(1)} %get-tuple-element.20.refs_3_, ...), custom_call_target="tpu_custom_call" | custom-call | tf_op jit(solution)/shard_map/early_products/pallas_call | solution.py:157
  34.8 0.0 collective-permute-done.3.refs_1_
  34.8 4.5 %collective-permute-done.4.refs_2_ = bf16[8,32,128]{2,1,0:T(8,128)(2,1)S(1)} collective-permute-done((bf16[8,32,128]{2,1,0:T(8,128)(2,1)S(1)}, bf16[8,32,128]{2,1,0:T(8,128)(2,1)S(1)}, u32[]{:S(2)}, u32[]{:S(2)}) %collective-permute-start.4) | collective-permute-done | bytes 65568 | tf_op jit(solution)/shard_map/ppermute | solution.py:298
  39.4 0.0 collective-permute-done.5.refs_3_
  39.4 1.0 %collective-permute-done.6.refs_4_ = bf16[8,32,128]{2,1,0:T(8,128)(2,1)S(1)} collective-permute-done((bf16[8,32,128]{2,1,0:T(8,128)(2,1)S(1)}, bf16[8,32,128]{2,1,0:T(8,128)(2,1)S(1)}, u32[]{:S(2)}, u32[]{:S(2)}) %collective-permute-start.6) | collective-permute-done | bytes 65568 | tf_op jit(solution)/shard_map/ppermute | solution.py:298
  40.3 0.0 copy-done.1
  40.3 1.2 %late_products.1 = (f32[64,1024]{1,0:T(8,128)S(1)}, f32[32,8,128]{2,1,0:T(8,128)S(1)}, f32[32,8,128]{2,1,0:T(8,128)S(1)}) custom-call(s32[8,8]{1,0:T(8,128)S(1)} %copy-done.1, f32[64,1024]{1,0:T(8,128)S(1)} %early_products.1.early, bf16[8,128,256]{2,1,0:T(8,128)(2,1)S(1)} %get-tuple-element.24.refs_0_, ...), custom_call_target="tpu_custom_call" | custom-call | tf_op jit(solution)/shard_map/late_products/pallas_call | solution.py:200
  41.6 0.1 collective-permute-start.7
  41.7 1.3 %collective-permute-done.7 = f32[32,8,128]{2,1,0:T(8,128)S(1)} collective-permute-done((f32[32,8,128]{2,1,0:T(8,128)S(1)}, f32[32,8,128]{2,1,0:T(8,128)S(1)}, u32[]{:S(2)}, u32[]{:S(2)}) %collective-permute-start.7) | collective-permute-done | bytes 131104 | tf_op jit(solution)/shard_map/ppermute | solution.py:298
  43.0 1.6 %collective-permute-start.8 = (f32[32,8,128]{2,1,0:T(8,128)S(1)}, f32[32,8,128]{2,1,0:T(8,128)S(1)}, u32[]{:S(2)}, u32[]{:S(2)}) collective-permute-start(f32[32,8,128]{2,1,0:T(8,128)S(1)} %add.3.first), channel_id=1, source_target_pairs={{0,2},{1,3},{2,0},{3,1},{4,6},{5,7},{6,4},{7,5},{8,10},{9,11},{10,... | collective-permute-start | bytes 393224 | tf_op jit(solution)/shard_map/ppermute | solution.py:298
  44.6 0.0 collective-permute-start.9
  44.6 4.0 %collective-permute-done.8.second = f32[32,8,128]{2,1,0:T(8,128)S(1)} collective-permute-done((f32[32,8,128]{2,1,0:T(8,128)S(1)}, f32[32,8,128]{2,1,0:T(8,128)S(1)}, u32[]{:S(2)}, u32[]{:S(2)}) %collective-permute-start.8) | collective-permute-done | bytes 131104 | tf_op jit(solution)/shard_map/ppermute | solution.py:298
  48.6 0.0 collective-permute-start.10
  48.6 1.0 %distances.2 = (f32[64,1024]{1,0:T(8,128)}, f32[32,64]{1,0:T(8,128)S(1)}) custom-call(f32[64,1024]{1,0:T(8,128)S(1)} %get-tuple-element.29.sketch, f32[32,8,128]{2,1,0:T(8,128)S(1)} %add.3.first, f32[32,8,128]{2,1,0:T(8,128)S(1)} %collective-permute-done.8.second), custom_call_target="tpu_custom_call" | custom-call | tf_op jit(solution)/shard_map/distances/pallas_call | solution.py:248
  49.7 0.0 collective-permute-done.9.first
  49.7 0.3 collective-permute-done.10.second
  50.0 1.1 %distances.3 = bf16[32,128]{1,0:T(8,128)(2,1)S(1)} custom-call(f32[64,1024]{1,0:T(8,128)S(1)} %get-tuple-element.29.sketch, f32[32,8,128]{2,1,0:T(8,128)S(1)} %collective-permute-done.9.first, f32[32,8,128]{2,1,0:T(8,128)S(1)} %collective-permute-done.10.second, f32[32,64]{1,0:T(8,128)S(1)} %get-tuple-element.33.refs_0_), custom_call_target="tpu_custom_call" | custom-call | tf_op jit(solution)/shard_map/distances/pallas_call | solution.py:257
  51.1 10.2 %all_to_all.10.parts = bf16[8,32,128]{2,1,0:T(8,128)(2,1)S(1)} all-to-all(bf16[8,32,128]{2,1,0:T(8,128)(2,1)S(1)} %broadcast_in_dim.2), channel_id=1, replica_groups=mesh['feat'=8,'ex'=4] {'feat'}, dimensions={0} | all-to-all | bytes 131072 | tf_op jit(solution)/shard_map/all_to_all | solution.py:334
  61.3 0.7 %nearest.1 = f32[8,64]{1,0:T(8,128)} custom-call(bf16[8,32,128]{2,1,0:T(8,128)(2,1)S(1)} %all_to_all.10.parts), custom_call_target="tpu_custom_call" | custom-call | tf_op jit(solution)/shard_map/nearest/pallas_call | solution.py:287
  (2 shorter events, 0.0 us)
Async XLA Ops:
  8.0 26.1 %all-to-all-start = ((bf16[64,32,128]{2,1,0:T(8,128)(2,1)}), bf16[64,32,128]{2,1,0:T(8,128)(2,1)S(1)}, u32[]{:S(2)}, u32[]{:S(2)}) async-start(bf16[64,32,128]{2,1,0:T(8,128)(2,1)} %first_products.2), calls=%async_computation | async-start | bytes 1048576 | tf_op jit(solution)/shard_map/all_to_all | solution.py:312
  15.3 18.2 %copy-start = (bf16[8,1024,128]{2,1,0:T(8,128)(2,1)S(1)}, bf16[8,1024,128]{2,1,0:T(8,128)(2,1)}, u32[]{:S(2)}) copy-start(bf16[8,1024,128]{2,1,0:T(8,128)(2,1)} %second.1) | copy-start | bytes 6291460
  15.3 25.0 %copy-start.1 = (s32[8,8]{1,0:T(8,128)S(1)}, s32[8,8]{1,0:T(8,128)}, u32[]{:S(2)}) copy-start(s32[8,8]{1,0:T(8,128)} %picks.1) | copy-start | bytes 772
  22.1 7.9 %collective-permute-start = (bf16[8,32,128]{2,1,0:T(8,128)(2,1)S(1)}, bf16[8,32,128]{2,1,0:T(8,128)(2,1)S(1)}, u32[]{:S(2)}, u32[]{:S(2)}) collective-permute-start(bf16[8,32,128]{2,1,0:T(8,128)(2,1)S(1)} %get-tuple-element.21), channel_id=1, source_target_pairs={{0,4},{4,0},{8,12},{12,8},{16,20},{20,16},{24,28},{28,24},{1,5},{5... | collective-permute-start | bytes 196616 | tf_op jit(solution)/shard_map/ppermute | solution.py:298
  24.2 9.1 %collective-permute-start.1 = (bf16[8,32,128]{2,1,0:T(8,128)(2,1)S(1)}, bf16[8,32,128]{2,1,0:T(8,128)(2,1)S(1)}, u32[]{:S(2)}, u32[]{:S(2)}) collective-permute-start(bf16[8,32,128]{2,1,0:T(8,128)(2,1)S(1)} %get-tuple-element.22), channel_id=1, source_target_pairs={{0,8},{4,12},{8,0},{12,4},{16,24},{20,28},{24,16},{28,20},{1,9},{5... | collective-permute-start | bytes 196616 | tf_op jit(solution)/shard_map/ppermute | solution.py:298
  25.6 8.5 %collective-permute-start.2 = (bf16[8,32,128]{2,1,0:T(8,128)(2,1)S(1)}, bf16[8,32,128]{2,1,0:T(8,128)(2,1)S(1)}, u32[]{:S(2)}, u32[]{:S(2)}) collective-permute-start(bf16[8,32,128]{2,1,0:T(8,128)(2,1)S(1)} %get-tuple-element.23), channel_id=1, source_target_pairs={{0,12},{4,8},{8,4},{12,0},{16,28},{20,24},{24,20},{28,16},{1,13},{... | collective-permute-start | bytes 196616 | tf_op jit(solution)/shard_map/ppermute | solution.py:298
  25.7 9.1 %collective-permute-start.3 = (bf16[8,32,128]{2,1,0:T(8,128)(2,1)S(1)}, bf16[8,32,128]{2,1,0:T(8,128)(2,1)S(1)}, u32[]{:S(2)}, u32[]{:S(2)}) collective-permute-start(bf16[8,32,128]{2,1,0:T(8,128)(2,1)S(1)} %get-tuple-element.25), channel_id=1, source_target_pairs={{0,16},{4,20},{8,24},{12,28},{16,0},{20,4},{24,8},{28,12},{1,17},{... | collective-permute-start | bytes 196616 | tf_op jit(solution)/shard_map/ppermute | solution.py:298
  28.5 10.8 %collective-permute-start.4 = (bf16[8,32,128]{2,1,0:T(8,128)(2,1)S(1)}, bf16[8,32,128]{2,1,0:T(8,128)(2,1)S(1)}, u32[]{:S(2)}, u32[]{:S(2)}) collective-permute-start(bf16[8,32,128]{2,1,0:T(8,128)(2,1)S(1)} %get-tuple-element.26), channel_id=1, source_target_pairs={{0,20},{4,16},{8,28},{12,24},{16,4},{20,0},{24,12},{28,8},{1,21},{... | collective-permute-start | bytes 196616 | tf_op jit(solution)/shard_map/ppermute | solution.py:298
  30.0 9.4 %collective-permute-start.5 = (bf16[8,32,128]{2,1,0:T(8,128)(2,1)S(1)}, bf16[8,32,128]{2,1,0:T(8,128)(2,1)S(1)}, u32[]{:S(2)}, u32[]{:S(2)}) collective-permute-start(bf16[8,32,128]{2,1,0:T(8,128)(2,1)S(1)} %get-tuple-element.27), channel_id=1, source_target_pairs={{0,24},{4,28},{8,16},{12,20},{16,8},{20,12},{24,0},{28,4},{1,25},{... | collective-permute-start | bytes 196616 | tf_op jit(solution)/shard_map/ppermute | solution.py:298
  33.3 7.1 %collective-permute-start.6 = (bf16[8,32,128]{2,1,0:T(8,128)(2,1)S(1)}, bf16[8,32,128]{2,1,0:T(8,128)(2,1)S(1)}, u32[]{:S(2)}, u32[]{:S(2)}) collective-permute-start(bf16[8,32,128]{2,1,0:T(8,128)(2,1)S(1)} %get-tuple-element.28), channel_id=1, source_target_pairs={{0,28},{4,24},{8,20},{12,16},{16,12},{20,8},{24,4},{28,0},{1,29},{... | collective-permute-start | bytes 196616 | tf_op jit(solution)/shard_map/ppermute | solution.py:298
  41.6 1.4 %collective-permute-start.7 = (f32[32,8,128]{2,1,0:T(8,128)S(1)}, f32[32,8,128]{2,1,0:T(8,128)S(1)}, u32[]{:S(2)}, u32[]{:S(2)}) collective-permute-start(f32[32,8,128]{2,1,0:T(8,128)S(1)} %get-tuple-element.31), channel_id=1, source_target_pairs={{0,1},{1,0},{2,3},{3,2},{4,5},{5,4},{6,7},{7,6},{8,9},{9,8},{10,11... | collective-permute-start | bytes 393224 | tf_op jit(solution)/shard_map/ppermute | solution.py:298
  43.0 5.6 %collective-permute-start.8 = (f32[32,8,128]{2,1,0:T(8,128)S(1)}, f32[32,8,128]{2,1,0:T(8,128)S(1)}, u32[]{:S(2)}, u32[]{:S(2)}) collective-permute-start(f32[32,8,128]{2,1,0:T(8,128)S(1)} %add.3.first), channel_id=1, source_target_pairs={{0,2},{1,3},{2,0},{3,1},{4,6},{5,7},{6,4},{7,5},{8,10},{9,11},{10,... | collective-permute-start | bytes 393224 | tf_op jit(solution)/shard_map/ppermute | solution.py:298
  44.6 5.1 %collective-permute-start.9 = (f32[32,8,128]{2,1,0:T(8,128)S(1)}, f32[32,8,128]{2,1,0:T(8,128)S(1)}, u32[]{:S(2)}, u32[]{:S(2)}) collective-permute-start(f32[32,8,128]{2,1,0:T(8,128)S(1)} %add.3.first), channel_id=1, source_target_pairs={{0,1},{1,0},{2,3},{3,2},{4,5},{5,4},{6,7},{7,6},{8,9},{9,8},{10,11... | collective-permute-start | bytes 393224 | tf_op jit(solution)/shard_map/ppermute | solution.py:298
  48.6 1.3 %collective-permute-start.10 = (f32[32,8,128]{2,1,0:T(8,128)S(1)}, f32[32,8,128]{2,1,0:T(8,128)S(1)}, u32[]{:S(2)}, u32[]{:S(2)}) collective-permute-start(f32[32,8,128]{2,1,0:T(8,128)S(1)} %collective-permute-done.8.second), channel_id=1, source_target_pairs={{0,1},{1,0},{2,3},{3,2},{4,5},{5,4},{6,7},{7,6},{8,9},{9,8},{10,11... | collective-permute-start | bytes 393224 | tf_op jit(solution)/shard_map/ppermute | solution.py:298

commit v7 on v6

--- a/solution.py
+++ b/solution.py
@@ -18,7 +18,7 @@
     return pltpu.CompilerParams(vmem_limit_bytes=mib * MIB)
 
 
-def first_kernel(feat, start, half, step, flush, *refs):
+def first_kernel(feat, pair, start, half, step, flush, *refs):
     grads, factor, *outs, g_buf, w_buf, acc, sems = refs
     _, groups, size = factor.shape
     kept = groups // feat
@@ -52,13 +52,15 @@
                 for q in range(kept):
                     at = pl.multiple_of(first + q * half + done, 8)
                     rows = acc[pl.ds(at, flush), :].astype(BF16)
-                    if split:
-                        outs[d][q, done : done + flush, :] = rows
+                    if split and pair and d in (2, 3):
+                        outs[2][(d - 2) * kept + q, done : done + flush, :] = rows
+                    elif split:
+                        outs[d - 1 if pair and d > 3 else d][q, done : done + flush, :] = rows
                     else:
                         outs[0][d * kept + q, done : done + flush, :] = rows
 
 
-def first_products(grads, factor, feat, split, start, count):
+def first_products(grads, factor, feat, pair, split, start, count):
     rows = grads.shape[0]
     _, groups, size = factor.shape
     kept = groups // feat
@@ -68,12 +70,14 @@
     lanes = 2 * rows
     if split:
         out_shape = [jax.ShapeDtypeStruct((kept, half, lanes), BF16)] * feat
+        if pair:
+            out_shape[2:4] = [jax.ShapeDtypeStruct((2 * kept, half, lanes), BF16)]
     else:
         out_shape = [jax.ShapeDtypeStruct((groups, half, lanes), BF16)]
     vmem = pl.BlockSpec(memory_space=pltpu.VMEM)
     hbm = pl.BlockSpec(memory_space=pl.ANY)
     return pl.pallas_call(
-        functools.partial(first_kernel, feat, start, half, step, flush),
+        functools.partial(first_kernel, feat, pair, start, half, step, flush),
         in_specs=[hbm, hbm],
         out_specs=[vmem] * len(out_shape),
         out_shape=out_shape,
@@ -93,36 +97,39 @@
     )(grads, factor)
 
 
-def turn_kernel(plan, local, second, *outs):
+def pack_kernel(own, beside, across, near, message):
+    kept = own.shape[0]
+    near[:kept] = own[...]
+    near[kept:] = across[:kept]
+    message[:kept] = beside[...]
+    message[kept:] = across[kept:]
+
+
+def packed(own, beside, across):
+    vmem = pl.BlockSpec(memory_space=pltpu.VMEM)
+    return pl.pallas_call(
+        pack_kernel,
+        in_specs=[vmem] * 3,
+        out_specs=[vmem] * 2,
+        out_shape=[jax.ShapeDtypeStruct(across.shape, BF16)] * 2,
+        compiler_params=params(),
+        name="packed",
+    )(own, beside, across)
+
+
+def turn(second, k, spans, local, out):
     me = lax.axis_index("feat")
     width = second.shape[2]
-    for spans, out in zip(plan, outs):
-        for k in range(second.shape[0]):
-            for h in range(2):
-                rows = []
-                for relative, source, start, half in spans:
-                    if relative:
-                        at = pl.multiple_of((me ^ source) * local + start + h * half, 8)
-                    else:
-                        at = source * local + start + h * half
-                    rows.append(second[k, pl.ds(at, half), :])
-                depth = out.shape[2] // 2
-                out[k, :, h * depth : (h + 1) * depth] = jnp.concatenate(rows, axis=0).T
-
-
-def turned(second, local, plan):
-    groups, _, width = second.shape
-    vmem = pl.BlockSpec(memory_space=pltpu.VMEM)
-    return pl.pallas_call(
-        functools.partial(turn_kernel, plan, local),
-        in_specs=[vmem],
-        out_specs=[vmem] * len(plan),
-        out_shape=[
-            jax.ShapeDtypeStruct((groups, width, 2 * sum(span[-1] for span in spans)), BF16) for spans in plan
-        ],
-        compiler_params=params(),
-        name="turned_factor",
-    )(second)
+    for h in range(2):
+        rows = []
+        for relative, source, start, half in spans:
+            if relative:
+                at = pl.multiple_of((me ^ source) * local + start + h * half, 8)
+            else:
+                at = source * local + start + h * half
+            rows.append(second[k, pl.ds(at, half), :])
+        depth = out.shape[2] // 2
+        out[k, :, h * depth : (h + 1) * depth] = jnp.concatenate(rows, axis=0).T
 
 
 def products(k, factors, pieces, rows):
@@ -136,44 +143,48 @@
     return total.T
 
 
-def split_refs(counts, refs):
+def early_kernel(plan, local, counts, second, *refs):
     refs = list(refs)
-    factors = [refs.pop(0) for _ in counts]
     pieces = [[refs.pop(0) for _ in range(n)] for n in counts]
-    return factors, pieces, refs
-
-
-def early_kernel(counts, *refs):
-    factors, pieces, (out,) = split_refs(counts, refs)
-    groups, width, _ = factors[0].shape
+    out, late, held, sem, *factors = refs
+    copy = pltpu.make_async_copy(second, held, sem)
+    copy.start()
+    copy.wait()
+    groups, _, width = held.shape
     for k in range(groups):
+        for spans, factor in zip(plan, factors + [late]):
+            turn(held, k, spans, local, factor)
         out[:, k * width : (k + 1) * width] = products(k, factors, pieces, out.shape[0])
 
 
-def early_products(factors, pieces, rows):
-    groups, width, _ = factors[0].shape
+def early_products(second, plan, local, pieces, rows):
+    groups, _, width = second.shape
     vmem = pl.BlockSpec(memory_space=pltpu.VMEM)
     counts = [len(own) for own in pieces]
-    return pl.pallas_call(
-        functools.partial(early_kernel, counts),
-        in_specs=[vmem] * (len(counts) + sum(counts)),
-        out_specs=vmem,
-        out_shape=jax.ShapeDtypeStruct((rows, groups * width), F32),
-        compiler_params=params(),
+    shapes = [(groups, width, 2 * sum(span[-1] for span in spans)) for spans in plan]
+    return pl.pallas_call(
+        functools.partial(early_kernel, plan, local, counts),
+        in_specs=[pl.BlockSpec(memory_space=pl.ANY)] + [vmem] * sum(counts),
+        out_specs=[vmem] * 2,
+        out_shape=[jax.ShapeDtypeStruct((rows, groups * width), F32), jax.ShapeDtypeStruct(shapes[-1], BF16)],
+        scratch_shapes=[pltpu.VMEM(second.shape, BF16), pltpu.SemaphoreType.DMA]
+        + [pltpu.VMEM(shape, BF16) for shape in shapes[:-1]],
+        compiler_params=params(),
+        cost_estimate=pl.CostEstimate(flops=2000000000, bytes_accessed=2000000, transcendentals=0),
         name="early_products",
-    )(*factors, *[x for own in pieces for x in own])
-
-
-def late_kernel(counts, picks, early, *refs):
-    factors, pieces, (sketch, mine, other, held) = split_refs(counts, refs)
-    groups, width, _ = factors[0].shape
+    )(second, *[x for own in pieces for x in own])
+
+
+def late_kernel(picks, early, factor, *refs):
+    *pieces, sketch, mine, other, held = refs
+    groups, width, _ = factor.shape
     rows = sketch.shape[0]
     slots = mine.shape[1]
     if groups < slots:
         held[...] = jnp.zeros_like(held)
     for k in range(groups):
         cols = slice(k * width, (k + 1) * width)
-        mapped = early[:, cols] + products(k, factors, pieces, rows)
+        mapped = early[:, cols] + products(k, [factor], [pieces], rows)
         sketch[:, cols] = mapped
         held[pl.ds(k, rows, stride=slots), :] = mapped
     rounds, each = picks.shape
@@ -189,23 +200,22 @@
                 out[r * each + p] = jnp.where(held_here, held[pl.ds(start, slots), :], 0.0)
 
 
-def late_products(picks, early, factors, pieces):
+def late_products(picks, early, factor, pieces):
     rows = early.shape[0]
-    groups, width, _ = factors[0].shape
+    groups, width, _ = factor.shape
     slots = -(-groups // 8) * 8
     smem = pl.BlockSpec(memory_space=pltpu.SMEM)
     vmem = pl.BlockSpec(memory_space=pltpu.VMEM)
-    counts = [len(own) for own in pieces]
     fetched = jax.ShapeDtypeStruct((picks.size // 2, slots, width), F32)
     return pl.pallas_call(
-        functools.partial(late_kernel, counts),
-        in_specs=[smem] + [vmem] * (1 + len(counts) + sum(counts)),
+        late_kernel,
+        in_specs=[smem] + [vmem] * (2 + len(pieces)),
         out_specs=[vmem] * 3,
         out_shape=[jax.ShapeDtypeStruct(early.shape, F32), fetched, fetched],
         scratch_shapes=[pltpu.VMEM((rows * slots, width), F32)],
         compiler_params=params(),
         name="late_products",
-    )(picks, early, *factors, *[x for own in pieces for x in own])
+    )(picks, early, factor, *pieces)
 
 
 def distance_kernel(unroll, sketch, first, second, *refs):
@@ -308,18 +318,26 @@
     start, half = local - count, count // 2
     pieces, plan = [], []
     if start:
-        (inner,) = first_products(grads, factor, feat, False, 0, start)
+        (inner,) = first_products(grads, factor, feat, False, False, 0, start)
         pieces.append([lax.all_to_all(inner, "feat", split_axis=0, concat_axis=0, tiled=True)])
         plan.append([(False, d, 0, start // 2) for d in range(feat)])
-    split = first_products(grads, factor, feat, True, start, count)
-    far = [swap(x, "feat", feat, near + i) for i, x in enumerate(split[near:])]
-    close = [x if d == 0 else swap(x, "feat", feat, d) for d, x in enumerate(split[:near])]
+    pair = near == 4
+    split = first_products(grads, factor, feat, pair, True, start, count)
+    far = [swap(x, "feat", feat, near + i) for i, x in enumerate(split[len(split) - near :])]
+    far_places = list(range(near, feat))
+    if pair:
+        across = swap(split[2], "feat", feat, 2)
+        close, message = packed(split[0], split[1], across)
+        close, near_places = [close], [0, 2]
+        far, far_places = far + [swap(message, "feat", feat, 1)], far_places + [1, 3]
+    else:
+        close = [x if d == 0 else swap(x, "feat", feat, d) for d, x in enumerate(split[:near])]
+        near_places = list(range(near))
     pieces += [close, far]
-    plan += [[(True, d, start, half) for d in places] for places in (range(near), range(near, feat))]
-
-    factors = turned(second_factor, local, plan)
-    early = early_products(factors[:-1], pieces[:-1], rows)
-    sketch, mine, other = late_products(picks, early, factors[-1:], pieces[-1:])
+    plan += [[(True, d, start, half) for d in places] for places in (near_places, far_places)]
+
+    early, turned = early_products(second_factor, plan, local, pieces[:-1], rows)
+    sketch, mine, other = late_products(picks, early, turned, pieces[-1])
 
     chip = mine + swap(other, "ex", ex, 1)
     across = [chip]

time: 62.3 us -> 62.2 us (level)
  Pallas kernels: 19.5 us -> 21.2 us
  waiting for transfers between devices: 11.2 us -> 9.55 us
    ppermute x11 -> x10, waiting for transfers between devices: 11.2 us -> 6.02 us  [swap(): return lax.ppermute(x, axis, [(i, i ^ step) for i in range(size)])]
    all_to_all x1, waiting for transfers between devices: 0.01 us -> 3.53 us  [per_device(): lax.all_to_all(inner, 'feat', split_axis=0, concat_axis=0, tiled=True)]
    pallas_call x5, Pallas kernels: 16.7 us -> 18.4 us  [the longest x2 14.2 us: first_products(): pl.pallas_call(functools.partial(first_kernel, feat, pair, start, half, s...]
    ppermute x11 -> x10, starting transfers between devices: 13.1 us -> 12.9 us  [swap(): return lax.ppermute(x, axis, [(i, i ^ step) for i in range(size)])]
  transfers between devices with their start and end apart: 12 -> 11, of which waited for: 5 -> 5; matrix products, arithmetic and copies ran while one was open for 0% -> 0% of each run, Pallas kernels for 15% -> 17%
where the time goes in v7:
time: 62.2 us; the launch traced here: 62 us
  Pallas kernels  21.2 us (34%)
  starting transfers between devices  20.2 us (32%)
  blocking collectives  10.3 us (17%)
  waiting for transfers between devices  9.55 us (15%)
  between operations  0.73 us (1%)
    pallas_call x2, Pallas kernels, first_products(): pl.pallas_call(functools.partial(first_kernel, feat, pair, start, half, s...  14.2 us
    ppermute x10, starting transfers between devices, swap(): return lax.ppermute(x, axis, [(i, i ^ step) for i in range(size)])  12.9 us
    all_to_all x1, blocking collectives, per_device(): lax.all_to_all(spread, 'feat', split_axis=0, concat_axis=0, tiled=True)  10.3 us
    all_to_all x1, starting transfers between devices, per_device(): lax.all_to_all(inner, 'feat', split_axis=0, concat_axis=0, tiled=True)  7.27 us
    ppermute x10, waiting for transfers between devices, swap(): return lax.ppermute(x, axis, [(i, i ^ step) for i in range(size)])  6.02 us
    all_to_all x1, waiting for transfers between devices, per_device(): lax.all_to_all(inner, 'feat', split_axis=0, concat_axis=0, tiled=True)  3.53 us
    pallas_call x1, Pallas kernels, early_products(): pl.pallas_call(functools.partial(early_kernel, plan, local, counts), in_s...  2.93 us
    pallas_call x1, Pallas kernels, late_products(): pl.pallas_call(late_kernel, in_specs=[smem] + [vmem] * (2 + len(pieces)),...  1.33 us
  transfers between devices with their start and end apart: 11, of which 5 were waited for; matrix products, arithmetic and copies ran while one was open for 0% of the time, Pallas kernels for 17%

profile of v7, /device:TPU:0, one launch (start us, length us, event | category | flops | bytes accessed | tf_op | source)
XLA Modules:
  0.0 62.0 jit_solution(253507808954312989)
XLA Ops:
  0.6 7.4 %first_products.2 = bf16[64,32,128]{2,1,0:T(8,128)(2,1)} custom-call(bf16[64,131072]{1,0:T(8,128)(2,1)} %refs_0_.3, bf16[128,64,1024]{2,1,0:T(8,128)(2,1)} %bitcast.1), custom_call_target="tpu_custom_call" | custom-call | flops 536870912 | bytes 16777216 | tf_op jit(solution)/shard_map/first_products/pallas_call | solution.py:79
  8.0 7.3 %all-to-all-start = ((bf16[64,32,128]{2,1,0:T(8,128)(2,1)}), bf16[64,32,128]{2,1,0:T(8,128)(2,1)S(1)}, u32[]{:S(2)}, u32[]{:S(2)}) async-start(bf16[64,32,128]{2,1,0:T(8,128)(2,1)} %first_products.2), calls=%async_computation | async-start | bytes 1048576 | tf_op jit(solution)/shard_map/all_to_all | solution.py:322
  15.3 0.0 copy-start.1
  15.3 0.0 copy-start
  15.3 6.7 %first_products.3 = (bf16[8,32,128]{2,1,0:T(8,128)(2,1)S(1)}, bf16[8,32,128]{2,1,0:T(8,128)(2,1)S(1)}, bf16[16,32,128]{2,1,0:T(8,128)(2,1)S(1)}, bf16[8,32,128]{...) custom-call(bf16[64,131072]{1,0:T(8,128)(2,1)} %refs_0_.3, ...), custom_call_target="tpu_custom_call" | custom-call | flops 536870912 | bytes 16777216 | tf_op jit(solution)/shard_map/first_products/pallas_call | solution.py:79
  22.1 2.1 %collective-permute-start = (bf16[16,32,128]{2,1,0:T(8,128)(2,1)S(1)}, bf16[16,32,128]{2,1,0:T(8,128)(2,1)S(1)}, u32[]{:S(2)}, u32[]{:S(2)}) collective-permute-start(bf16[16,32,128]{2,1,0:T(8,128)(2,1)S(1)} %get-tuple-element.20), channel_id=1, source_target_pairs={{0,8},{4,12},{8,0},{12,4},{16,24},{20,28},{24,16},{28,20},{1,9},{5... | collective-permute-start | bytes 393224 | tf_op jit(solution)/shard_map/ppermute | solution.py:308
  24.2 2.4 %collective-permute-start.1 = (bf16[8,32,128]{2,1,0:T(8,128)(2,1)S(1)}, bf16[8,32,128]{2,1,0:T(8,128)(2,1)S(1)}, u32[]{:S(2)}, u32[]{:S(2)}) collective-permute-start(bf16[8,32,128]{2,1,0:T(8,128)(2,1)S(1)} %get-tuple-element.24), channel_id=1, source_target_pairs={{0,16},{4,20},{8,24},{12,28},{16,0},{20,4},{24,8},{28,12},{1,17},{... | collective-permute-start | bytes 196616 | tf_op jit(solution)/shard_map/ppermute | solution.py:308
  26.5 1.5 %collective-permute-start.2 = (bf16[8,32,128]{2,1,0:T(8,128)(2,1)S(1)}, bf16[8,32,128]{2,1,0:T(8,128)(2,1)S(1)}, u32[]{:S(2)}, u32[]{:S(2)}) collective-permute-start(bf16[8,32,128]{2,1,0:T(8,128)(2,1)S(1)} %get-tuple-element.25), channel_id=1, source_target_pairs={{0,20},{4,16},{8,28},{12,24},{16,4},{20,0},{24,12},{28,8},{1,21},{... | collective-permute-start | bytes 196616 | tf_op jit(solution)/shard_map/ppermute | solution.py:308
  28.0 2.4 %collective-permute-start.3 = (bf16[8,32,128]{2,1,0:T(8,128)(2,1)S(1)}, bf16[8,32,128]{2,1,0:T(8,128)(2,1)S(1)}, u32[]{:S(2)}, u32[]{:S(2)}) collective-permute-start(bf16[8,32,128]{2,1,0:T(8,128)(2,1)S(1)} %get-tuple-element.26), channel_id=1, source_target_pairs={{0,24},{4,28},{8,16},{12,20},{16,8},{20,12},{24,0},{28,4},{1,25},{... | collective-permute-start | bytes 196616 | tf_op jit(solution)/shard_map/ppermute | solution.py:308
  30.3 1.5 %collective-permute-start.4 = (bf16[8,32,128]{2,1,0:T(8,128)(2,1)S(1)}, bf16[8,32,128]{2,1,0:T(8,128)(2,1)S(1)}, u32[]{:S(2)}, u32[]{:S(2)}) collective-permute-start(bf16[8,32,128]{2,1,0:T(8,128)(2,1)S(1)} %get-tuple-element.27), channel_id=1, source_target_pairs={{0,28},{4,24},{8,20},{12,16},{16,12},{20,8},{24,4},{28,0},{1,29},{... | collective-permute-start | bytes 196616 | tf_op jit(solution)/shard_map/ppermute | solution.py:308
  31.8 0.0 collective-permute-done.across
  31.8 1.5 %collective-permute-start.5 = (bf16[16,32,128]{2,1,0:T(8,128)(2,1)S(1)}, bf16[16,32,128]{2,1,0:T(8,128)(2,1)S(1)}, u32[]{:S(2)}, u32[]{:S(2)}) collective-permute-start(bf16[16,32,128]{2,1,0:T(8,128)(2,1)S(1)} %get-tuple-element.28), channel_id=1, source_target_pairs={{0,4},{4,0},{8,12},{12,8},{16,20},{20,16},{24,28},{28,24},{1,5},{5... | collective-permute-start | bytes 393224 | tf_op jit(solution)/shard_map/ppermute | solution.py:308
  33.4 3.5 %all-to-all-done.refs_0_ = bf16[64,32,128]{2,1,0:T(8,128)(2,1)S(1)} async-done(((bf16[64,32,128]{2,1,0:T(8,128)(2,1)}), bf16[64,32,128]{2,1,0:T(8,128)(2,1)S(1)}, u32[]{:S(2)}, u32[]{:S(2)}) %all-to-all-start) | async-done | bytes 524320 | tf_op jit(solution)/shard_map/all_to_all | solution.py:322
  36.9 0.0 copy-done.1
  36.9 2.9 %early_products.1 = (f32[64,1024]{1,0:T(8,128)S(1)}, bf16[8,128,384]{2,1,0:T(8,128)(2,1)S(1)}) custom-call(bf16[8,1024,128]{2,1,0:T(8,128)(2,1)S(1)} %copy-done.1, bf16[64,32,128]{2,1,0:T(8,128)(2,1)S(1)} %all-to-all-done.refs_0_, bf16[16,32,128]{2,1,0:T(8,128)(2,1)S(1)} %get-tuple-element.21.refs_1_), custom_call_target="tpu_custom_call" | custom-call | flops 2000000000 | bytes 2000000 | tf_op jit(solution)/shard_map/early_products/pallas_call | solution.py:165
  39.8 0.0 collective-permute-done.1.refs_0_
  39.8 0.3 collective-permute-done.2.refs_1_
  40.2 0.0 collective-permute-done.3.refs_2_
  40.2 0.0 collective-permute-done.4.refs_3_
  40.2 0.0 collective-permute-done.5.refs_4_
  40.2 0.0 copy-done
  40.2 1.3 %late_products.1 = (f32[64,1024]{1,0:T(8,128)S(1)}, f32[32,8,128]{2,1,0:T(8,128)S(1)}, f32[32,8,128]{2,1,0:T(8,128)S(1)}) custom-call(s32[8,8]{1,0:T(8,128)S(1)} %copy-done, f32[64,1024]{1,0:T(8,128)S(1)} %get-tuple-element.22.early, bf16[8,128,384]{2,1,0:T(8,128)(2,1)S(1)} %get-tuple-element.23.factor, ...), custom_call_target="tpu_custom_call" | custom-call | tf_op jit(solution)/shard_map/late_products/pallas_call | solution.py:210
  41.5 0.1 collective-permute-start.6
  41.6 1.3 %collective-permute-done.6 = f32[32,8,128]{2,1,0:T(8,128)S(1)} collective-permute-done((f32[32,8,128]{2,1,0:T(8,128)S(1)}, f32[32,8,128]{2,1,0:T(8,128)S(1)}, u32[]{:S(2)}, u32[]{:S(2)}) %collective-permute-start.6) | collective-permute-done | bytes 131104 | tf_op jit(solution)/shard_map/ppermute | solution.py:308
  43.0 1.6 %collective-permute-start.7 = (f32[32,8,128]{2,1,0:T(8,128)S(1)}, f32[32,8,128]{2,1,0:T(8,128)S(1)}, u32[]{:S(2)}, u32[]{:S(2)}) collective-permute-start(f32[32,8,128]{2,1,0:T(8,128)S(1)} %add.3.first), channel_id=1, source_target_pairs={{0,2},{1,3},{2,0},{3,1},{4,6},{5,7},{6,4},{7,5},{8,10},{9,11},{10,... | collective-permute-start | bytes 393224 | tf_op jit(solution)/shard_map/ppermute | solution.py:308
  44.6 0.0 collective-permute-start.8
  44.6 4.0 %collective-permute-done.7.second = f32[32,8,128]{2,1,0:T(8,128)S(1)} collective-permute-done((f32[32,8,128]{2,1,0:T(8,128)S(1)}, f32[32,8,128]{2,1,0:T(8,128)S(1)}, u32[]{:S(2)}, u32[]{:S(2)}) %collective-permute-start.7) | collective-permute-done | bytes 131104 | tf_op jit(solution)/shard_map/ppermute | solution.py:308
  48.6 0.0 collective-permute-start.9
  48.6 1.0 %distances.2 = (f32[64,1024]{1,0:T(8,128)}, f32[32,64]{1,0:T(8,128)S(1)}) custom-call(f32[64,1024]{1,0:T(8,128)S(1)} %get-tuple-element.29.sketch, f32[32,8,128]{2,1,0:T(8,128)S(1)} %add.3.first, f32[32,8,128]{2,1,0:T(8,128)S(1)} %collective-permute-done.7.second), custom_call_target="tpu_custom_call" | custom-call | tf_op jit(solution)/shard_map/distances/pallas_call | solution.py:258
  49.6 0.0 collective-permute-done.8.first
  49.6 0.3 collective-permute-done.9.second
  49.9 1.1 %distances.3 = bf16[32,128]{1,0:T(8,128)(2,1)S(1)} custom-call(f32[64,1024]{1,0:T(8,128)S(1)} %get-tuple-element.29.sketch, f32[32,8,128]{2,1,0:T(8,128)S(1)} %collective-permute-done.8.first, f32[32,8,128]{2,1,0:T(8,128)S(1)} %collective-permute-done.9.second, f32[32,64]{1,0:T(8,128)S(1)} %get-tuple-element.33.refs_0_), custom_call_target="tpu_custom_call" | custom-call | tf_op jit(solution)/shard_map/distances/pallas_call | solution.py:267
  51.0 10.3 %all_to_all.10.parts = bf16[8,32,128]{2,1,0:T(8,128)(2,1)S(1)} all-to-all(bf16[8,32,128]{2,1,0:T(8,128)(2,1)S(1)} %broadcast_in_dim.2), channel_id=1, replica_groups=mesh['feat'=8,'ex'=4] {'feat'}, dimensions={0} | all-to-all | bytes 131072 | tf_op jit(solution)/shard_map/all_to_all | solution.py:352
  61.3 0.7 %nearest.1 = f32[8,64]{1,0:T(8,128)} custom-call(bf16[8,32,128]{2,1,0:T(8,128)(2,1)S(1)} %all_to_all.10.parts), custom_call_target="tpu_custom_call" | custom-call | tf_op jit(solution)/shard_map/nearest/pallas_call | solution.py:297
  (3 shorter events, 0.1 us)
Async XLA Ops:
  8.0 28.8 %all-to-all-start = ((bf16[64,32,128]{2,1,0:T(8,128)(2,1)}), bf16[64,32,128]{2,1,0:T(8,128)(2,1)S(1)}, u32[]{:S(2)}, u32[]{:S(2)}) async-start(bf16[64,32,128]{2,1,0:T(8,128)(2,1)} %first_products.2), calls=%async_computation | async-start | bytes 1048576 | tf_op jit(solution)/shard_map/all_to_all | solution.py:322
  15.3 21.6 %copy-start.1 = (bf16[8,1024,128]{2,1,0:T(8,128)(2,1)S(1)}, bf16[8,1024,128]{2,1,0:T(8,128)(2,1)}, u32[]{:S(2)}) copy-start(bf16[8,1024,128]{2,1,0:T(8,128)(2,1)} %second.1) | copy-start | bytes 6291460
  15.3 24.9 %copy-start = (s32[8,8]{1,0:T(8,128)S(1)}, s32[8,8]{1,0:T(8,128)}, u32[]{:S(2)}) copy-start(s32[8,8]{1,0:T(8,128)} %picks.1) | copy-start | bytes 772
  22.1 9.7 %collective-permute-start = (bf16[16,32,128]{2,1,0:T(8,128)(2,1)S(1)}, bf16[16,32,128]{2,1,0:T(8,128)(2,1)S(1)}, u32[]{:S(2)}, u32[]{:S(2)}) collective-permute-start(bf16[16,32,128]{2,1,0:T(8,128)(2,1)S(1)} %get-tuple-element.20), channel_id=1, source_target_pairs={{0,8},{4,12},{8,0},{12,4},{16,24},{20,28},{24,16},{28,20},{1,9},{5... | collective-permute-start | bytes 393224 | tf_op jit(solution)/shard_map/ppermute | solution.py:308
  24.2 15.7 %collective-permute-start.1 = (bf16[8,32,128]{2,1,0:T(8,128)(2,1)S(1)}, bf16[8,32,128]{2,1,0:T(8,128)(2,1)S(1)}, u32[]{:S(2)}, u32[]{:S(2)}) collective-permute-start(bf16[8,32,128]{2,1,0:T(8,128)(2,1)S(1)} %get-tuple-element.24), channel_id=1, source_target_pairs={{0,16},{4,20},{8,24},{12,28},{16,0},{20,4},{24,8},{28,12},{1,17},{... | collective-permute-start | bytes 196616 | tf_op jit(solution)/shard_map/ppermute | solution.py:308
  26.5 13.7 %collective-permute-start.2 = (bf16[8,32,128]{2,1,0:T(8,128)(2,1)S(1)}, bf16[8,32,128]{2,1,0:T(8,128)(2,1)S(1)}, u32[]{:S(2)}, u32[]{:S(2)}) collective-permute-start(bf16[8,32,128]{2,1,0:T(8,128)(2,1)S(1)} %get-tuple-element.25), channel_id=1, source_target_pairs={{0,20},{4,16},{8,28},{12,24},{16,4},{20,0},{24,12},{28,8},{1,21},{... | collective-permute-start | bytes 196616 | tf_op jit(solution)/shard_map/ppermute | solution.py:308
  28.0 12.2 %collective-permute-start.3 = (bf16[8,32,128]{2,1,0:T(8,128)(2,1)S(1)}, bf16[8,32,128]{2,1,0:T(8,128)(2,1)S(1)}, u32[]{:S(2)}, u32[]{:S(2)}) collective-permute-start(bf16[8,32,128]{2,1,0:T(8,128)(2,1)S(1)} %get-tuple-element.26), channel_id=1, source_target_pairs={{0,24},{4,28},{8,16},{12,20},{16,8},{20,12},{24,0},{28,4},{1,25},{... | collective-permute-start | bytes 196616 | tf_op jit(solution)/shard_map/ppermute | solution.py:308
  30.3 9.8 %collective-permute-start.4 = (bf16[8,32,128]{2,1,0:T(8,128)(2,1)S(1)}, bf16[8,32,128]{2,1,0:T(8,128)(2,1)S(1)}, u32[]{:S(2)}, u32[]{:S(2)}) collective-permute-start(bf16[8,32,128]{2,1,0:T(8,128)(2,1)S(1)} %get-tuple-element.27), channel_id=1, source_target_pairs={{0,28},{4,24},{8,20},{12,16},{16,12},{20,8},{24,4},{28,0},{1,29},{... | collective-permute-start | bytes 196616 | tf_op jit(solution)/shard_map/ppermute | solution.py:308
  31.8 8.4 %collective-permute-start.5 = (bf16[16,32,128]{2,1,0:T(8,128)(2,1)S(1)}, bf16[16,32,128]{2,1,0:T(8,128)(2,1)S(1)}, u32[]{:S(2)}, u32[]{:S(2)}) collective-permute-start(bf16[16,32,128]{2,1,0:T(8,128)(2,1)S(1)} %get-tuple-element.28), channel_id=1, source_target_pairs={{0,4},{4,0},{8,12},{12,8},{16,20},{20,16},{24,28},{28,24},{1,5},{5... | collective-permute-start | bytes 393224 | tf_op jit(solution)/shard_map/ppermute | solution.py:308
  41.5 1.4 %collective-permute-start.6 = (f32[32,8,128]{2,1,0:T(8,128)S(1)}, f32[32,8,128]{2,1,0:T(8,128)S(1)}, u32[]{:S(2)}, u32[]{:S(2)}) collective-permute-start(f32[32,8,128]{2,1,0:T(8,128)S(1)} %get-tuple-element.31), channel_id=1, source_target_pairs={{0,1},{1,0},{2,3},{3,2},{4,5},{5,4},{6,7},{7,6},{8,9},{9,8},{10,11... | collective-permute-start | bytes 393224 | tf_op jit(solution)/shard_map/ppermute | solution.py:308
  43.0 5.6 %collective-permute-start.7 = (f32[32,8,128]{2,1,0:T(8,128)S(1)}, f32[32,8,128]{2,1,0:T(8,128)S(1)}, u32[]{:S(2)}, u32[]{:S(2)}) collective-permute-start(f32[32,8,128]{2,1,0:T(8,128)S(1)} %add.3.first), channel_id=1, source_target_pairs={{0,2},{1,3},{2,0},{3,1},{4,6},{5,7},{6,4},{7,5},{8,10},{9,11},{10,... | collective-permute-start | bytes 393224 | tf_op jit(solution)/shard_map/ppermute | solution.py:308
  44.6 5.1 %collective-permute-start.8 = (f32[32,8,128]{2,1,0:T(8,128)S(1)}, f32[32,8,128]{2,1,0:T(8,128)S(1)}, u32[]{:S(2)}, u32[]{:S(2)}) collective-permute-start(f32[32,8,128]{2,1,0:T(8,128)S(1)} %add.3.first), channel_id=1, source_target_pairs={{0,1},{1,0},{2,3},{3,2},{4,5},{5,4},{6,7},{7,6},{8,9},{9,8},{10,11... | collective-permute-start | bytes 393224 | tf_op jit(solution)/shard_map/ppermute | solution.py:308
  48.6 1.3 %collective-permute-start.9 = (f32[32,8,128]{2,1,0:T(8,128)S(1)}, f32[32,8,128]{2,1,0:T(8,128)S(1)}, u32[]{:S(2)}, u32[]{:S(2)}) collective-permute-start(f32[32,8,128]{2,1,0:T(8,128)S(1)} %collective-permute-done.7.second), channel_id=1, source_target_pairs={{0,1},{1,0},{2,3},{3,2},{4,5},{5,4},{6,7},{7,6},{8,9},{9,8},{10,11... | collective-permute-start | bytes 393224 | tf_op jit(solution)/shard_map/ppermute | solution.py:308
